TPU v7x, 32 devices: a whole 2x2x4 slice. The times are simulated.
32 devices in a mesh: flt: 8 (over y, x, core), scn: 4 (over z).
Axes of the slice: x: 2, y: 2, z: 4, core: 2. Of those that a mesh axis runs over, the one named last changes fastest.
Arguments:
- tiles: bfloat16 [384, 128, 128], P('flt'), as said below
- tile_row: int32 [384], P('flt'), may hold values from 0 to 7, as said below
- tile_col: int32 [384], P('flt'), may hold values from 0 to 7, as said below
- tile_count: int32 [8], P('flt'), may hold values from 16 to 48, as said below
- slot_offset: int32 [8192], P('flt'), may hold values from 0 to 19
- capacity: int32 [128, 1024], P('scn', 'flt'), may hold values from 0 to 999
- plan0: float32 [8192], P('flt'), may hold values from 0 to 1
- hold0: float32 [128, 8192], P('scn', 'flt'), may hold values from 0 to 2
- dual0: float32 [128, 1024], P('scn', 'flt'), may hold values from 0 to 1
Outputs:
- plan: float32 [8192], P('flt')
- hold: float32 [128, 8192], P('scn', 'flt')
- dual: float32 [128, 1024], P('scn', 'flt')
Inputs may be any that keep to these rules, and one draw needn't show every extreme that they name: `tile_col`: the live slots of every flt index name each of its 8 column blocks. `tile_row`: the live slots of all flt indices together name every row block. `tile_count`: some flt index has exactly 16 live slots and some other has all 48. `tiles`: entries are finite; slots from `tile_count` on may hold any finite values and are ignored.
All inputs are finite; a program needn't handle non-finite values.
Results may differ from a plain program's by a relative error of at most 0.00155.
The roundings to bfloat16 on the way count: a program that leaves them out, or rounds other values in their place, can miss the bound.
Values may be sent and summed in bfloat16 or wider, within the bound.
No kernel may reach another device: no remote copies, remote signals or barrier semaphores. Data moves between devices by JAX's collectives and lax.ppermute only.
A program may use at most 64 MiB of HBM per device.

v0:
```python
import jax
import jax.numpy as jnp
from jax import lax
from jax.sharding import PartitionSpec as P

SWEEPS = 4
ITERS = 2


EPS = 1e-06
COST_RATE = 1.0
HOLD_BASE = 1.0
HOLD_CAP = 2.0
CAP_UNIT = 4.0
TAU_PLAN = 0.2
TAU_HOLD = 0.02
SIGMA = 0.05


def pull_columns(matrix, tile_row, tile_col, col_blocks, dual_low):
    scen, rows = dual_low.shape
    block = matrix.shape[1]
    blocks = dual_low.reshape(scen, rows // block, block)
    picked = jnp.take(blocks, tile_row, axis=1)
    product = jnp.einsum("stk,tkj->tsj", picked, matrix, preferred_element_type=jnp.float32)
    total = jax.ops.segment_sum(product, tile_col, num_segments=col_blocks)
    return jnp.transpose(total, (1, 0, 2)).reshape(scen, -1)


def push_rows(matrix, tile_row, tile_col, row_blocks, mixed_low):
    scen, cols = mixed_low.shape
    block = matrix.shape[1]
    blocks = mixed_low.reshape(scen, cols // block, block)
    picked = jnp.take(blocks, tile_col, axis=1)
    product = jnp.einsum("tkj,stj->tsk", matrix, picked, preferred_element_type=jnp.float32)
    total = jax.ops.segment_sum(product, tile_row, num_segments=row_blocks)
    return jnp.transpose(total, (1, 0, 2)).reshape(scen, -1)


def body(tiles, tile_row, tile_col, tile_count, slot_offset, capacity, plan0, hold0, dual0):
    slots = tiles.shape[0]
    block = tiles.shape[1]
    col_blocks = plan0.shape[0] // block
    own_rows = dual0.shape[1]
    own_blocks = own_rows // block
    row_blocks = own_blocks * lax.axis_size("flt")
    scen_all = dual0.shape[0] * lax.axis_size("scn")
    live = (jnp.arange(slots) < tile_count[0]).astype(jnp.float32)
    scale_row = jnp.ones((row_blocks, block), jnp.float32)
    scale_col = jnp.ones((col_blocks, block), jnp.float32)
    for sweep in range(SWEEPS):
        row_factor = jnp.take(scale_row, tile_row, axis=0)
        col_factor = jnp.take(scale_col, tile_col, axis=0)
        scaled = (
            jnp.abs(tiles).astype(jnp.float32)
            * live[:, None, None]
            * row_factor[:, :, None]
            * col_factor[:, None, :]
        )
        tile_rpeak = jnp.max(scaled, axis=2)
        tile_cpeak = jnp.max(scaled, axis=1)
        local_rpeak = jnp.maximum(
            jax.ops.segment_max(tile_rpeak, tile_row, num_segments=row_blocks), 0.0
        )
        col_peak = jnp.maximum(
            jax.ops.segment_max(tile_cpeak, tile_col, num_segments=col_blocks), 0.0
        )
        row_peak = lax.pmax(local_rpeak, "flt")
        scale_row = scale_row / jnp.sqrt(row_peak + EPS)
        scale_col = scale_col / jnp.sqrt(col_peak + EPS)
    row_factor = jnp.take(scale_row, tile_row, axis=0)
    col_factor = jnp.take(scale_col, tile_col, axis=0)
    matrix = (
        tiles.astype(jnp.float32)
        * live[:, None, None]
        * row_factor[:, :, None]
        * col_factor[:, None, :]
    ).astype(jnp.bfloat16)
    position = lax.axis_index("flt")
    col_scale = scale_col.reshape(-1)
    own_scale = lax.dynamic_slice_in_dim(scale_row, position * own_blocks, own_blocks, 0).reshape(
        -1
    )
    offsets = slot_offset.astype(jnp.float32)
    cost = COST_RATE * offsets * col_scale
    hold_cost = (HOLD_BASE + COST_RATE * offsets) * col_scale
    demand = CAP_UNIT * capacity.astype(jnp.float32) * own_scale[None, :]
    plan = plan0 / col_scale
    hold = hold0 / col_scale[None, :]
    dual = dual0 / own_scale[None, :]
    plan_top = 1.0 / col_scale
    hold_top = HOLD_CAP / col_scale
    for step in range(ITERS):
        gathered = lax.all_gather(dual.astype(jnp.bfloat16), "flt", axis=1, tiled=True)
        grad = pull_columns(matrix, tile_row, tile_col, col_blocks, gathered)
        mean_grad = lax.psum(jnp.sum(grad, axis=0), "scn") / scen_all
        plan_next = jnp.clip(plan - TAU_PLAN * (cost + mean_grad), 0.0, plan_top)
        hold_next = jnp.clip(hold - TAU_HOLD * (hold_cost[None, :] + grad), 0.0, hold_top[None, :])
        mixed = ((2.0 * plan_next - plan)[None, :] + (2.0 * hold_next - hold)).astype(jnp.bfloat16)
        plan = plan_next
        hold = hold_next
        partial_value = push_rows(matrix, tile_row, tile_col, row_blocks, mixed)
        load = lax.psum_scatter(partial_value, "flt", scatter_dimension=1, tiled=True)
        dual = jnp.maximum(dual + SIGMA * (load - demand), 0.0)
    return (plan * col_scale, hold * col_scale[None, :], dual * own_scale[None, :])


def solution(mesh):
    return jax.shard_map(
        body,
        mesh=mesh,
        in_specs=(
            P("flt", None, None),
            P("flt"),
            P("flt"),
            P("flt"),
            P("flt"),
            P("scn", "flt"),
            P("flt"),
            P("scn", "flt"),
            P("scn", "flt"),
        ),
        out_specs=(P("flt"), P("scn", "flt"), P("scn", "flt")),
        check_vma=False,
    )
```

profile of v0, /device:TPU:0, one launch (start us, length us, event | category | flops | bytes accessed | tf_op | source)
XLA Modules:
  0.0 219.5 jit_solution(9521335467744540982)
XLA Ops:
  7.2 0.8 compare_select_fusion
  12.0 3.2 %fusion = (f32[48,128]{1,0:T(8,128)S(1)}, f32[48,128]{1,0:T(8,128)S(1)}) fusion(f32[48,128]{1,0:T(8,128)S(1)} %get-tuple-element.24, f32[48,128]{1,0:T(8,128)S(1)} %get-tuple-element.25, f32[48]{0:T(128)S(1)} %compare_convert_fusion, bf16[48,128,128]{2,1,0:T(8,128)(2,1)} %param.13), kind=kLoop, calls=%fused_computation.32 | loop fusion | flops 5492736 | bytes 1671360 | tf_op jit(solution)/shard_map/reduce_max | solution.py:60
  15.2 0.9 scatter_custom_fusion.1
  16.1 15.1 %pmax.28 = f32[8,128]{1,0:T(8,128)S(1)} all-reduce(f32[8,128]{1,0:T(8,128)S(1)} %broadcast_maximum_fusion.3), channel_id=1, replica_groups=mesh['flt'=8,'scn'=4] {'flt'}, use_global_device_ids=true, to_apply=%region_4.6 | all-reduce | flops 1024 | bytes 8192 | tf_op jit(solution)/shard_map/pmax | solution.py:68
  31.9 0.9 scatter_custom_fusion
  33.5 2.1 fusion.2
  35.6 0.9 scatter_custom_fusion.3
  36.5 11.8 %pmax.29 = f32[8,128]{1,0:T(8,128)S(1)} all-reduce(f32[8,128]{1,0:T(8,128)S(1)} %broadcast_maximum_fusion.2), channel_id=1, replica_groups=mesh['flt'=8,'scn'=4] {'flt'}, use_global_device_ids=true, to_apply=%region_9.11 | all-reduce | flops 1024 | bytes 8192 | tf_op jit(solution)/shard_map/pmax | solution.py:68
  49.0 0.9 scatter_custom_fusion.2
  50.6 2.1 fusion.4
  52.7 1.0 scatter_custom_fusion.5
  53.8 11.8 %pmax.30 = f32[8,128]{1,0:T(8,128)S(1)} all-reduce(f32[8,128]{1,0:T(8,128)S(1)} %broadcast_maximum_fusion.1), channel_id=1, replica_groups=mesh['flt'=8,'scn'=4] {'flt'}, use_global_device_ids=true, to_apply=%region_14.16 | all-reduce | flops 1024 | bytes 8192 | tf_op jit(solution)/shard_map/pmax | solution.py:68
  66.3 0.9 scatter_custom_fusion.4
  67.9 2.1 fusion.6
  69.9 0.9 scatter_custom_fusion.7
  70.9 11.8 %pmax.31 = f32[8,128]{1,0:T(8,128)S(1)} all-reduce(f32[8,128]{1,0:T(8,128)S(1)} %broadcast_maximum_fusion), channel_id=1, replica_groups=mesh['flt'=8,'scn'=4] {'flt'}, use_global_device_ids=true, to_apply=%region_19.21 | all-reduce | flops 1024 | bytes 8192 | tf_op jit(solution)/shard_map/pmax | solution.py:68
  84.0 0.9 scatter_custom_fusion.6
  87.3 7.9 %all_gather.6 = bf16[32,1024]{1,0:T(8,128)(2,1)S(1)} all-gather(bf16[32,128]{1,0:T(8,128)(2,1)S(1)} %fusion.39), channel_id=1, replica_groups=mesh['flt'=8,'scn'=4] {'flt'}, dimensions={1}, use_global_device_ids=true | all-gather | bytes 73728 | tf_op jit(solution)/shard_map/all_gather | solution.py:94
  95.9 1.9 multiply_convert_fusion
  98.4 2.5 %scatter_fusion = f32[8,32,128]{2,1,0:T(8,128)S(1)} fusion(f32[8,32,128]{2,1,0:T(8,128)S(1)} %broadcast.75.clone, s32[48]{0:T(128)S(1)} %copy-done.14, f32[48,32,128]{2,1,0:T(8,128)S(1)} %fusion.14), kind=kCustom, calls=%fused_computation.22 | custom fusion | flops 196608 | bytes 2359488 | tf_op jit(solution)/shard_map/scatter-add | solution.py:26
  100.9 12.0 %psum.14 = f32[1024]{0:T(1024)S(1)} all-reduce(f32[1024]{0:T(1024)S(1)} %bitcast.118), channel_id=1, replica_groups=mesh['flt'=8,'scn'=4] {'scn'}, use_global_device_ids=true, to_apply=%region_22.25 | all-reduce | flops 1024 | bytes 8192 | tf_op jit(solution)/shard_map/psum | solution.py:96
  113.0 0.7 gather_fusion.11
  113.8 1.0 fusion.12
  114.8 2.5 %scatter_fusion.1 = f32[8,32,128]{2,1,0:T(8,128)S(1)} fusion(f32[8,32,128]{2,1,0:T(8,128)S(1)} %broadcast.75.clone.2, s32[48]{0:T(128)S(1)} %copy-done.15, f32[48,32,128]{2,1,0:T(8,128)S(1)} %fusion.12), kind=kCustom, calls=%fused_computation.23 | custom fusion | flops 196608 | bytes 2359488 | tf_op jit(solution)/shard_map/scatter-add | solution.py:36
  118.1 30.7 %reduce-scatter.3.cloned.1.call-done = f32[32,128]{1,0:T(8,128)} async-done(((f32[32,1024]{1,0:T(8,128)}), f32[32,128]{1,0:T(8,128)}) %reduce-scatter.3.cloned.1.call-update) | async-done | bytes 16400 | tf_op jit(solution)/shard_map/reduce_scatter | solution.py:103
  149.5 9.1 %all_gather.7 = bf16[32,1024]{1,0:T(8,128)(2,1)S(1)} all-gather(bf16[32,128]{1,0:T(8,128)(2,1)S(1)} %fusion.60), channel_id=1, replica_groups=mesh['flt'=8,'scn'=4] {'flt'}, dimensions={1}, use_global_device_ids=true | all-gather | bytes 73728 | tf_op jit(solution)/shard_map/all_gather | solution.py:94
  160.0 2.5 %scatter_fusion.2 = f32[8,32,128]{2,1,0:T(8,128)S(1)} fusion(f32[8,32,128]{2,1,0:T(8,128)S(1)} %broadcast.75.clone.1, s32[48]{0:T(128)S(1)} %copy-done.14, f32[48,32,128]{2,1,0:T(8,128)S(1)} %fusion.10), kind=kCustom, calls=%fused_computation.24 | custom fusion | flops 196608 | bytes 2359488 | tf_op jit(solution)/shard_map/scatter-add | solution.py:26
  162.5 11.7 %psum.15 = f32[1024]{0:T(1024)S(1)} all-reduce(f32[1024]{0:T(1024)S(1)} %bitcast.119), channel_id=1, replica_groups=mesh['flt'=8,'scn'=4] {'scn'}, use_global_device_ids=true, to_apply=%region_27.30 | all-reduce | flops 1024 | bytes 8192 | tf_op jit(solution)/shard_map/psum | solution.py:96
  176.4 1.0 fusion.8
  177.3 2.5 %scatter_fusion.3 = f32[8,32,128]{2,1,0:T(8,128)S(1)} fusion(f32[8,32,128]{2,1,0:T(8,128)S(1)} %broadcast.75, s32[48]{0:T(128)S(1)} %copy-done.15, f32[48,32,128]{2,1,0:T(8,128)S(1)} %fusion.8), kind=kCustom, calls=%fused_computation.25 | custom fusion | flops 196608 | bytes 2359488 | tf_op jit(solution)/shard_map/scatter-add | solution.py:36
  180.6 30.7 %reduce-scatter.5.cloned.1.call-done = f32[32,128]{1,0:T(8,128)} async-done(((f32[32,1024]{1,0:T(8,128)}), f32[32,128]{1,0:T(8,128)}) %reduce-scatter.5.cloned.1.call-update) | async-done | bytes 16400 | tf_op jit(solution)/shard_map/reduce_scatter | solution.py:103
  211.3 1.3 maximum_multiply_fusion
  (97 shorter events, 18.0 us)
Async XLA Ops:
  7.2 26.4 %copy-start = (bf16[48,128,128]{2,1,0:T(8,128)(2,1)S(1)}, bf16[48,128,128]{2,1,0:T(8,128)(2,1)}, u32[]{:S(2)}) copy-start(bf16[48,128,128]{2,1,0:T(8,128)(2,1)} %param.13) | copy-start | bytes 4718596
  7.2 141.6 %reduce-scatter.3.cloned.1.call-start = ((), (), s32[]{:S(2)}) async-start(), calls=%async_computation.2 | async-start | bytes 147456 | tf_op jit(solution)/shard_map/reduce_scatter | solution.py:103
  10.0 85.2 %copy-start.8 = (s32[1024]{0:T(1024)}, s32[1024]{0:T(1024)S(1)}, u32[]{:S(2)}) copy-start(s32[1024]{0:T(1024)S(1)} %pad_clamp_fusion.1) | copy-start | bytes 12292
  10.0 74.9 %copy-start.7 = (s32[1024]{0:T(1024)}, s32[1024]{0:T(1024)S(1)}, u32[]{:S(2)}) copy-start(s32[1024]{0:T(1024)S(1)} %pad_clamp_fusion) | copy-start | bytes 12292
  11.9 83.4 %copy-start.9 = (f32[48]{0:T(128)}, f32[48]{0:T(128)S(1)}, u32[]{:S(2)}) copy-start(f32[48]{0:T(128)S(1)} %compare_convert_fusion) | copy-start | bytes 580
  52.7 34.6 %copy-start.2 = (f32[32,128]{1,0:T(8,128)S(1)}, f32[32,128]{1,0:T(8,128)}, u32[]{:S(2)}) copy-start(f32[32,128]{1,0:T(8,128)} %param.21) | copy-start | bytes 49156
  86.7 0.5 copy-start.10
  97.7 0.7 copy-start.14
  98.3 14.6 %copy-start.6 = (s32[1024]{0:T(1024)S(1)}, s32[1024]{0:T(1024)}, u32[]{:S(2)}) copy-start(s32[1024]{0:T(1024)} %param.17) | copy-start | bytes 12292
  98.3 14.6 %copy-start.13 = (f32[1024]{0:T(1024)S(1)}, f32[1024]{0:T(1024)}, u32[]{:S(2)}) copy-start(f32[1024]{0:T(1024)} %param.19) | copy-start | bytes 12292
  98.3 14.6 %copy-start.1 = (f32[32,1024]{1,0:T(8,128)S(1)}, f32[32,1024]{1,0:T(8,128)}, u32[]{:S(2)}) copy-start(f32[32,1024]{1,0:T(8,128)} %param.20) | copy-start | bytes 393220
  113.8 1.0 copy-start.15
  114.8 34.0 %copy-start.3 = (f32[32,128]{1,0:T(8,128)S(1)}, f32[32,128]{1,0:T(8,128)}, u32[]{:S(2)}) copy-start(f32[32,128]{1,0:T(8,128)} %param.21) | copy-start | bytes 49156
  114.8 34.0 %copy-start.4 = (s32[32,128]{1,0:T(8,128)S(1)}, s32[32,128]{1,0:T(8,128)}, u32[]{:S(2)}) copy-start(s32[32,128]{1,0:T(8,128)} %param.18) | copy-start | bytes 49156
  114.8 34.0 %copy-start.11 = (f32[128]{0:T(128)S(1)}, f32[128]{0:T(128)}, u32[]{:S(2)}) copy-start(f32[128]{0:T(128)} %copy-done.10) | copy-start | bytes 1540
  114.8 34.0 %copy-start.12 = (f32[128]{0:T(128)S(1)}, f32[128]{0:T(128)}, u32[]{:S(2)}) copy-start(f32[128]{0:T(128)} %get-tuple-element.13) | copy-start | bytes 1540
  118.0 93.3 %reduce-scatter.5.cloned.1.call-start = ((), (), s32[]{:S(2)}) async-start(), calls=%async_computation.3 | async-start | bytes 147456 | tf_op jit(solution)/shard_map/reduce_scatter | solution.py:103
  177.3 34.0 %copy-start.5 = (f32[32,128]{1,0:T(8,128)S(1)}, f32[32,128]{1,0:T(8,128)}, u32[]{:S(2)}) copy-start(f32[32,128]{1,0:T(8,128)} %reduce-scatter.3.cloned.1.call-done) | copy-start | bytes 49156
Sparse Core Ops, SparseCore 0:
  118.1 30.6 reduce-scatter.2
  180.7 30.5 reduce-scatter.4
where the time goes:
time: 220 us; the launch traced here: 219 us
  blocking collectives  91.2 us (41%)
  waiting for transfers between devices  61.5 us (28%)
  other arithmetic  37.7 us (17%)
  between operations  15.2 us (7%)
  local copies, waits for them, and re-layouts  10.8 us (5%)
  matrix products  3.11 us (1%)
    reduce_scatter x2, waiting for transfers between devices, body(): lax.psum_scatter(partial_value, 'flt', scatter_dimension=1, tiled=True)  61.5 us
    pmax x4, blocking collectives, body(): row_peak = lax.pmax(local_rpeak, 'flt')  50.5 us
    psum x2, blocking collectives, body(): mean_grad = lax.psum(jnp.sum(grad, axis=0), 'scn') / scen_all  23.7 us
    all_gather x2, blocking collectives, body(): lax.all_gather(dual.astype(jnp.bfloat16), 'flt', axis=1, tiled=True)  17 us
    reduce_max x4, other arithmetic, body(): tile_rpeak = jnp.max(scaled, axis=2)  9.43 us
    scatter-add x2, other arithmetic, pull_columns(): total = jax.ops.segment_sum(product, tile_col, num_segments=col_blocks)  5.05 us
    scatter-add x2, other arithmetic, push_rows(): total = jax.ops.segment_sum(product, tile_row, num_segments=row_blocks)  5.05 us
  transfers between devices with their start and end apart: 2, of which 2 were waited for; matrix products, arithmetic and copies ran while one was open for 0% of the time, Pallas kernels for 0%

commit v1 on v0

v1 whole, which is shorter than its diff:
```python
import functools

import jax
import jax.numpy as jnp
from jax import lax
from jax.experimental import pallas as pl
from jax.experimental.pallas import tpu as pltpu
from jax.sharding import PartitionSpec as P

EPS = 1e-06
COST_RATE = 1.0
HOLD_BASE = 1.0
HOLD_CAP = 2.0
CAP_UNIT = 4.0
TAU_PLAN = 0.2
TAU_HOLD = 0.02
SIGMA = 0.05

B = 128
UNROLL = 4
VMEM = pl.BlockSpec(memory_space=pltpu.VMEM)
SMEM = pl.BlockSpec(memory_space=pltpu.SMEM)
F32 = jnp.float32
BF16 = jnp.bfloat16


def call(body, out_shape, scratch, n_smem, n_vmem):
    return pl.pallas_call(
        body,
        out_shape=out_shape,
        in_specs=[SMEM] * n_smem + [VMEM] * n_vmem,
        out_specs=[VMEM] * len(out_shape),
        scratch_shapes=scratch,
        compiler_params=pltpu.CompilerParams(vmem_limit_bytes=24 * 1024 * 1024),
    )


def loop(count, step):
    def trip(i, carry):
        for u in range(UNROLL):
            step(i * UNROLL + u)
        return carry

    lax.fori_loop(0, count // UNROLL, trip, 0)
    for t in range(count // UNROLL * UNROLL, count):
        step(t)


def fold_rows(a):
    return jnp.max(a.reshape(B // 8, 8, B), axis=0)


def lane_peaks(acc, blocks, first, packed):
    lane = lax.broadcasted_iota(jnp.int32, (B, B), 1)
    for b in range(blocks):
        peak = jnp.max(acc[b], axis=1, keepdims=True)
        packed = jnp.where(lane == first + b, peak, packed)
    return packed


def spread_rows(rep, scales):
    n = scales.shape[0]
    turned = jnp.concatenate([scales, jnp.zeros((B - n, B), F32)], axis=0).T
    for b in range(n):
        rep[b] = jnp.broadcast_to(turned[:, b : b + 1], (B, B))


def col_peaks(acc, col_blocks):
    return jnp.concatenate(
        [jnp.max(acc[c], axis=0, keepdims=True) for c in range(col_blocks)], axis=0
    )


def first_peaks(rb, cb, slots, meta, tiles, peaks, scale_col, racc, cacc):
    racc[...] = jnp.zeros_like(racc)
    cacc[...] = jnp.zeros_like(cacc)

    def plain(t):
        a = jnp.abs(tiles[t].astype(F32))
        r, c = meta[t], meta[slots + t]
        racc[r] = jnp.maximum(racc[r], a)
        cacc[c] = jnp.maximum(cacc[c], fold_rows(a))

    loop(slots, plain)
    packed = lane_peaks(racc, rb, 0, jnp.zeros((B, B), F32))
    scale_col[0:cb] = 1.0 / jnp.sqrt(col_peaks(cacc, cb) + EPS)
    scale_col[cb : cb + 1] = jnp.zeros((1, B), F32)
    racc[...] = jnp.zeros_like(racc)

    def scaled(t):
        a = jnp.abs(tiles[t].astype(F32))
        r, c = meta[t], meta[slots + t]
        racc[r] = jnp.maximum(racc[r], a * scale_col[pl.ds(c, 1), :])

    loop(slots, scaled)
    packed = lane_peaks(racc, rb, rb, packed)
    peaks[...] = packed.T[0 : 2 * rb]


def second_peaks(rb, cb, slots, per, pays, meta, place, tiles, scale_col1, *refs):
    parts = refs[:pays]
    payload, scale_row2, scale_col3, dual = refs[pays : pays + 4]
    rep, cacc, dacc, scol2, scol3, racc, racc_b = refs[pays + 4 :]
    peak = parts[0][0 : 2 * rb]
    for p in parts[1:]:
        peak = jnp.maximum(peak, p[0 : 2 * rb])
    srow1 = 1.0 / jnp.sqrt(peak[0:rb] + EPS)
    srow2 = srow1 / jnp.sqrt(srow1 * peak[rb : 2 * rb] + EPS)
    scale_row2[...] = srow2
    spread_rows(rep, jnp.concatenate([srow1, srow2], axis=0))
    rep[2 * rb] = jnp.zeros((B, B), F32)
    for k, p in enumerate(parts):
        for i in range(per):
            dual[place[k] + i] = p[2 * rb + 32 * i : 2 * rb + 32 * (i + 1)]
    payload[2 * rb : 3 * rb] = jnp.concatenate(
        [jnp.sum(dual[b], axis=0, keepdims=True) for b in range(rb)], axis=0
    )
    cacc[...] = jnp.zeros_like(cacc)
    dacc[...] = jnp.zeros_like(dacc)

    def columns(t):
        a = jnp.abs(tiles[t].astype(F32))
        r, c = meta[t], meta[slots + t]
        s = jnp.minimum(r, rb - 1)
        cacc[c] = jnp.maximum(cacc[c], fold_rows(a * rep[s]))
        dacc[c] = jnp.maximum(dacc[c], fold_rows(a * rep[s + rb]))

    loop(slots, columns)
    c1 = scale_col1[0:cb]
    c2 = c1 / jnp.sqrt(c1 * col_peaks(cacc, cb) + EPS)
    c3 = c2 / jnp.sqrt(c2 * col_peaks(dacc, cb) + EPS)
    scol2[0:cb] = c2
    scol3[0:cb] = c3
    scol2[cb : cb + 1] = jnp.zeros((1, B), F32)
    scol3[cb : cb + 1] = jnp.zeros((1, B), F32)
    scale_col3[...] = c3
    racc[...] = jnp.zeros_like(racc)
    racc_b[...] = jnp.zeros_like(racc_b)

    def rows(t):
        a = jnp.abs(tiles[t].astype(F32))
        r, c = meta[t], meta[slots + t]
        racc[r] = jnp.maximum(racc[r], a * scol2[pl.ds(c, 1), :])
        racc_b[r] = jnp.maximum(racc_b[r], a * scol3[pl.ds(c, 1), :])

    loop(slots, rows)
    packed = lane_peaks(racc, rb, 0, jnp.zeros((B, B), F32))
    packed = lane_peaks(racc_b, rb, rb, packed)
    payload[0 : 2 * rb] = packed.T[0 : 2 * rb]


def stack_dual(low, mean):
    hi = mean.astype(BF16).astype(F32)
    mid = (mean - hi).astype(BF16).astype(F32)
    lo = mean - hi - mid
    at = lax.broadcasted_iota(jnp.int32, (16, B), 0)
    tail = jnp.where(at == 0, hi, jnp.where(at == 1, mid, jnp.where(at == 2, lo, 0.0)))
    return jnp.concatenate([low, tail.astype(BF16)], axis=0)


def iterate(
    rb, cb, slots, scen_all, meta, mat, lhs, gacc, lacc, mixed, offsets, scol, read_plan, read_hold, write
):
    gacc[...] = jnp.zeros_like(gacc)

    def pull(t):
        r, c = jnp.minimum(meta[t], rb - 1), jnp.minimum(meta[slots + t], cb - 1)
        gacc[c] += jnp.dot(lhs[r], mat[t], preferred_element_type=F32)

    loop(slots, pull)
    for c in range(cb):
        scale = scol[c : c + 1]
        off = offsets[c : c + 1].astype(F32)
        cost = COST_RATE * off * scale
        hold_cost = (HOLD_BASE + COST_RATE * off) * scale
        grad = gacc[c, 0:32]
        mean_grad = (gacc[c, 32:33] + gacc[c, 33:34] + gacc[c, 34:35]) / scen_all
        plan, hold = read_plan(c, scale), read_hold(c, scale)
        plan_next = jnp.clip(plan - TAU_PLAN * (cost + mean_grad), 0.0, 1.0 / scale)
        hold_next = jnp.clip(hold - TAU_HOLD * (hold_cost + grad), 0.0, HOLD_CAP / scale)
        mixed[c] = ((2.0 * plan_next - plan) + (2.0 * hold_next - hold)).astype(BF16)
        write(c, scale, plan_next, hold_next)
    lacc[...] = jnp.zeros_like(lacc)

    def push(t):
        r, c = jnp.minimum(meta[t], rb - 1), jnp.minimum(meta[slots + t], cb - 1)
        lacc[r] += lax.dot_general(
            mixed[c], mat[t], (((1,), (1,)), ((), ())), preferred_element_type=F32
        )

    loop(slots, push)


def first_step(rb, cb, slots, scen_all, pays, split, meta, *refs):
    tiles, scale_row2, scale_col3, dual, offsets, capacity, plan0, hold0 = refs[:8]
    parts = refs[8 : 8 + pays]
    refs = refs[8 + pays :]
    mat, scale_row4, scale_col4, plan1, hold1 = refs[:5]
    loads, refs = refs[5 : 7 if split else 6], refs[7 if split else 6 :]
    rep, cacc, lhs, gacc, lacc, mixed = refs
    me = meta[2 * slots]
    peak = parts[0][0 : 2 * rb]
    ysum = parts[0][2 * rb : 3 * rb]
    for p in parts[1:]:
        peak = jnp.maximum(peak, p[0 : 2 * rb])
        ysum = ysum + p[2 * rb : 3 * rb]
    srow2 = scale_row2[...]
    srow3 = srow2 / jnp.sqrt(srow2 * peak[0:rb] + EPS)
    srow4 = srow3 / jnp.sqrt(srow3 * peak[rb : 2 * rb] + EPS)
    scale_row4[...] = srow4
    spread_rows(rep, jnp.concatenate([srow3, srow4], axis=0))
    rep[2 * rb] = jnp.zeros((B, B), F32)
    cacc[...] = jnp.zeros_like(cacc)

    def columns(t):
        a = jnp.abs(tiles[t].astype(F32))
        r, c = meta[t], meta[slots + t]
        cacc[c] = jnp.maximum(cacc[c], fold_rows(a * rep[jnp.minimum(r, rb - 1)]))

    loop(slots, columns)
    c3 = scale_col3[...]
    scale_col4[...] = c3 / jnp.sqrt(c3 * col_peaks(cacc, cb) + EPS)

    def build(t):
        r, c = meta[t], jnp.minimum(meta[slots + t], cb - 1)
        mat[t] = (tiles[t].astype(F32) * rep[r + rb] * scale_col4[pl.ds(c, 1), :]).astype(BF16)

    loop(slots, build)
    ymean = ysum / srow4
    for b in range(rb):
        low = (dual[b] / srow4[b : b + 1]).astype(BF16)
        lhs[b] = stack_dual(low, ymean[b : b + 1])

    def write(c, scale, plan, hold):
        plan1[c : c + 1] = plan
        hold1[:, c * B : (c + 1) * B] = hold

    iterate(
        rb, cb, slots, scen_all, meta, mat, lhs, gacc, lacc, mixed, offsets, scale_col4,
        lambda c, scale: plan0[c : c + 1] / scale,
        lambda c, scale: hold0[:, c * B : (c + 1) * B] / scale,
        write,
    )
    own = scale_row4[pl.ds(me, 1), :]
    lacc[me] += dual[me] / own * (1.0 / SIGMA) - CAP_UNIT * capacity[...].astype(F32) * own
    if split:
        parity = lax.rem(me, 2)
        for j in range(rb // 2):
            loads[0][j] = lacc[2 * j + parity]
            loads[1][j] = lacc[2 * j + 1 - parity]
    else:
        loads[0][...] = lacc[...]


def last_step(rb, cb, slots, scen_all, groups, stride, means, meta, place, *refs):
    mat, own_row, scale_col4, offsets, capacity, plan1, hold1, own_dual = refs[:8]
    lows = refs[8 : 8 + groups]
    sums = refs[8 + groups : 8 + groups + means]
    plan2, hold2, load, lhs, gacc, mixed = refs[8 + groups + means :]
    me = meta[2 * slots]
    ymean = sums[0][...]
    for s in sums[1:]:
        ymean = ymean + s[...]
    per = rb // groups
    for k in range(groups):
        for i in range(per):
            at = k * per + i
            lhs[place[k] + stride * i] = stack_dual(lows[k][i], ymean[at : at + 1])

    def write(c, scale, plan, hold):
        plan2[c : c + 1] = plan * scale
        hold2[:, c * B : (c + 1) * B] = hold * scale

    iterate(
        rb, cb, slots, scen_all, meta, mat, lhs, gacc, load, mixed, offsets, scale_col4,
        lambda c, scale: plan1[c : c + 1],
        lambda c, scale: hold1[:, c * B : (c + 1) * B],
        write,
    )
    own = own_row[...]
    load[me] += own_dual[...] * (1.0 / SIGMA) - CAP_UNIT * capacity[...].astype(F32) * own


def flip(x, axis, mask):
    n = lax.axis_size(axis)
    return lax.ppermute(x, axis, [(i, i ^ mask) for i in range(n)])


def flip_both(x, flt_mask, scn_mask):
    nf, ns = lax.axis_size("flt"), lax.axis_size("scn")
    pairs = [
        (f * ns + s, (f ^ flt_mask) * ns + (s ^ scn_mask)) for f in range(nf) for s in range(ns)
    ]
    return lax.ppermute(x, ("flt", "scn"), pairs)


def body(tiles, tile_row, tile_col, tile_count, slot_offset, capacity, plan0, hold0, dual0):
    slots = tiles.shape[0]
    cb = plan0.shape[0] // B
    nf, ns = lax.axis_size("flt"), lax.axis_size("scn")
    scen = dual0.shape[0]
    rb = nf
    scen_all = scen * ns
    small = nf == 8 and ns == 4
    me = lax.axis_index("flt").astype(jnp.int32)
    chip, core = me // 2, me % 2
    live = jnp.arange(slots, dtype=jnp.int32) < tile_count[0]
    meta = jnp.concatenate(
        [jnp.where(live, tile_row, rb), jnp.where(live, tile_col, cb), me[None]]
    )
    offsets = slot_offset.reshape(cb, B)
    f32 = functools.partial(jax.ShapeDtypeStruct, dtype=F32)

    peaks, scol1 = call(
        functools.partial(first_peaks, rb, cb, slots),
        [f32((2 * rb, B)), f32((cb + 1, B))],
        [pltpu.VMEM((rb + 1, B, B), F32), pltpu.VMEM((cb + 1, 8, B), F32)],
        1,
        1,
    )(meta, tiles)
    if small:
        mine = jnp.concatenate([peaks, dual0], axis=0)
        other = flip(mine, "flt", 1)
        both = [jnp.where(core == 0, dual0, other[2 * rb :]), jnp.where(core == 0, other[2 * rb :], dual0)]
        mine = jnp.concatenate([jnp.maximum(peaks, other[: 2 * rb])] + both, axis=0)
        parts = [mine] + [flip(mine, "flt", 2 * m) for m in (1, 2, 3)]
        place = jnp.stack([2 * (chip ^ m) for m in range(4)])
        per = 2
    else:
        gathered = lax.all_gather(dual0, "flt", axis=0, tiled=True)
        parts = [jnp.concatenate([lax.pmax(peaks, "flt"), gathered], axis=0)]
        place = jnp.zeros((1,), jnp.int32)
        per = rb
    payload, srow2, scol3, dual = call(
        functools.partial(second_peaks, rb, cb, slots, per, len(parts)),
        [f32((3 * rb, B)), f32((rb, B)), f32((cb, B)), f32((rb, scen, B))],
        [
            pltpu.VMEM((2 * rb + 1, B, B), F32),
            pltpu.VMEM((cb + 1, 8, B), F32),
            pltpu.VMEM((cb + 1, 8, B), F32),
            pltpu.VMEM((cb + 1, B), F32),
            pltpu.VMEM((cb + 1, B), F32),
            pltpu.VMEM((rb + 1, B, B), F32),
            pltpu.VMEM((rb + 1, B, B), F32),
        ],
        2,
        2 + len(parts),
    )(meta, place, tiles, scol1, *parts)
    peaks, ysum = payload[: 2 * rb], payload[2 * rb :]
    if small:
        mine = jnp.concatenate([jnp.maximum(peaks, flip(peaks, "flt", 1)), ysum], axis=0)
        parts = [mine] + [flip_both(mine, 2 * m, m) for m in (1, 2, 3)]
    else:
        parts = [jnp.concatenate([lax.pmax(peaks, "flt"), lax.psum(ysum, "scn")], axis=0)]
    lhs = pltpu.VMEM((rb, 48, B), BF16)
    gacc = pltpu.VMEM((cb, 48, B), F32)
    mixed = pltpu.VMEM((cb, scen, B), BF16)
    halves = [f32((rb // 2, scen, B))] * 2 if small else [f32((rb, scen, B))]
    outs = call(
        functools.partial(first_step, rb, cb, slots, scen_all, len(parts), small),
        [
            jax.ShapeDtypeStruct((slots, B, B), BF16),
            f32((rb, B)),
            f32((cb, B)),
            f32((cb, B)),
            f32((scen, cb * B)),
        ]
        + halves,
        [
            pltpu.VMEM((2 * rb + 1, B, B), F32),
            pltpu.VMEM((cb + 1, 8, B), F32),
            lhs,
            gacc,
            pltpu.VMEM((rb, scen, B), F32),
            mixed,
        ],
        1,
        8 + len(parts),
    )(meta, tiles, srow2, scol3, dual, offsets, capacity, plan0.reshape(cb, B), hold0, *parts)
    mat, srow4, scol4, plan1, hold1 = outs[:5]
    if small:
        half = outs[5] + flip(outs[6], "flt", 1)
        far = [flip(half, "flt", 2 * m) for m in (1, 2, 3)]
        y = jnp.maximum(SIGMA * (half + far[0] + far[1] + far[2]), 0.0)
        low = y.astype(BF16)
        part = jnp.sum(low.astype(F32), axis=1)
        lows = [low, flip(low, "flt", 1)]
        sums = jnp.concatenate([part, flip(part, "flt", 1)], axis=0)
        sums = [sums] + [flip(sums, "scn", m) for m in (1, 2, 3)]
        place = jnp.stack([core, 1 - core])
        own_dual = lax.dynamic_index_in_dim(y, chip, 0, False)
        stride = 2
    else:
        y = jnp.maximum(SIGMA * lax.psum(outs[5], "flt"), 0.0)
        lows = [y.astype(BF16)]
        sums = [lax.psum(jnp.sum(lows[0].astype(F32), axis=1), "scn")]
        place = jnp.zeros((1,), jnp.int32)
        own_dual = lax.dynamic_index_in_dim(y, me, 0, False)
        stride = 1
    own_row = lax.dynamic_slice_in_dim(srow4, me, 1, 0)
    plan, hold, load = call(
        functools.partial(last_step, rb, cb, slots, scen_all, len(lows), stride, len(sums)),
        [f32((cb, B)), f32((scen, cb * B)), f32((rb, scen, B))],
        [lhs, gacc, mixed],
        2,
        8 + len(lows) + len(sums),
    )(meta, place, mat, own_row, scol4, offsets, capacity, plan1, hold1, own_dual, *lows, *sums)
    total = jnp.sum(lax.all_to_all(load, "flt", 0, 0), axis=0)
    dual = jnp.maximum(SIGMA * total, 0.0) * own_row
    return plan.reshape(-1), hold, dual


def solution(mesh):
    return jax.shard_map(
        body,
        mesh=mesh,
        in_specs=(
            P("flt", None, None),
            P("flt"),
            P("flt"),
            P("flt"),
            P("flt"),
            P("scn", "flt"),
            P("flt"),
            P("scn", "flt"),
            P("scn", "flt"),
        ),
        out_specs=(P("flt"), P("scn", "flt"), P("scn", "flt")),
        check_vma=False,
    )
```

time: 220 us -> 68.2 us (0.31)
  blocking collectives: 91.2 us -> 0 us
  waiting for transfers between devices: 61.5 us -> 22.4 us
  other arithmetic: 37.7 us -> 1.61 us
  starting transfers between devices: 0.08 us -> 23.1 us
  Pallas kernels: 0 us -> 17.8 us
  between operations: 15.2 us -> 1.42 us
  local copies, waits for them, and re-layouts: 10.8 us -> 1.46 us
  matrix products: 3.11 us -> 0 us
    reduce_scatter x2 -> x0, waiting for transfers between devices: 61.5 us -> none  [body(): lax.psum_scatter(partial_value, 'flt', scatter_dimension=1, tiled=True)]
    pmax x4 -> x0, blocking collectives: 50.5 us -> none  [body(): row_peak = lax.pmax(local_rpeak, 'flt')]
    psum x2 -> x0, blocking collectives: 23.7 us -> none  [body(): mean_grad = lax.psum(jnp.sum(grad, axis=0), 'scn') / scen_all]
    ppermute x0 -> x17, starting transfers between devices: none -> 19.7 us  [the longest x14 13.6 us: flip(): return lax.ppermute(x, axis, [(i, i ^ mask) for i in range(n)])]
    pallas_call x0 -> x4, Pallas kernels: none -> 17.8 us  [the longest x1 7.16 us: body(): call(functools.partial(first_step, rb, cb, slots, scen_all, len(parts), s...]
    ppermute x0 -> x17, waiting for transfers between devices: none -> 17 us  [the longest x14 13.2 us: flip(): return lax.ppermute(x, axis, [(i, i ^ mask) for i in range(n)])]
    all_gather x2 -> x0, blocking collectives: 17 us -> none  [body(): lax.all_gather(dual.astype(jnp.bfloat16), 'flt', axis=1, tiled=True)]
    scatter-add x4 -> x0, other arithmetic: 10.1 us -> none  [the longest x2 5.05 us: pull_columns(): total = jax.ops.segment_sum(product, tile_col, num_segments=col_blocks)]
  transfers between devices with their start and end apart: 2 -> 18, of which waited for: 2 -> 15; matrix products, arithmetic and copies ran while one was open for 0% -> 0% of each run, Pallas kernels for 0% -> 0%
where the time goes in v1:
time: 68.2 us; the launch traced here: 67.9 us
  starting transfers between devices  23.1 us (34%)
  waiting for transfers between devices  22.4 us (33%)
  Pallas kernels  17.8 us (26%)
  other arithmetic  1.61 us (2%)
  local copies, waits for them, and re-layouts  1.46 us (2%)
  between operations  1.42 us (2%)
    ppermute x14, starting transfers between devices, flip(): return lax.ppermute(x, axis, [(i, i ^ mask) for i in range(n)])  13.6 us
    ppermute x14, waiting for transfers between devices, flip(): return lax.ppermute(x, axis, [(i, i ^ mask) for i in range(n)])  13.2 us
    pallas_call x1, Pallas kernels, body(): call(functools.partial(first_step, rb, cb, slots, scen_all, len(parts), s...  7.16 us
    ppermute x3, starting transfers between devices, flip_both(): return lax.ppermute(x, ('flt', 'scn'), pairs)  6.19 us
    pallas_call x1, Pallas kernels, body(): call(functools.partial(last_step, rb, cb, slots, scen_all, len(lows), str...  5.68 us
    all_to_all x1, waiting for transfers between devices, body(): total = jnp.sum(lax.all_to_all(load, 'flt', 0, 0), axis=0)  5.44 us
    ppermute x3, waiting for transfers between devices, flip_both(): return lax.ppermute(x, ('flt', 'scn'), pairs)  3.84 us
    all_to_all x1, starting transfers between devices, body(): total = jnp.sum(lax.all_to_all(load, 'flt', 0, 0), axis=0)  3.37 us
  transfers between devices with their start and end apart: 18, of which 15 were waited for; matrix products, arithmetic and copies ran while one was open for 0% of the time, Pallas kernels for 0%

profile of v1, /device:TPU:0, one launch (start us, length us, event | category | flops | bytes accessed | tf_op | source)
XLA Modules:
  0.0 67.9 jit_solution(9028932891003709926)
XLA Ops:
  1.3 0.7 compare_select_fusion
  2.1 1.4 %copy-done = bf16[48,128,128]{2,1,0:T(8,128)(2,1)S(1)} copy-done((bf16[48,128,128]{2,1,0:T(8,128)(2,1)S(1)}, bf16[48,128,128]{2,1,0:T(8,128)(2,1)}, u32[]{:S(2)}) %copy-start) | copy-done | bytes 1572888
  3.5 2.1 %shard_map.112 = (f32[16,128]{1,0:T(8,128)S(1)}, f32[9,128]{1,0:T(8,128)S(1)}) custom-call(s32[97]{0:T(128)S(1)} %pad_add_fusion.meta, bf16[48,128,128]{2,1,0:T(8,128)(2,1)S(1)} %copy-done), custom_call_target="tpu_custom_call" | custom-call | tf_op jit(solution)/shard_map/pallas_call | solution.py:314
  5.5 0.5 collective-permute-start
  6.1 0.8 %collective-permute-done = f32[48,128]{1,0:T(8,128)S(1)} collective-permute-done((f32[48,128]{1,0:T(8,128)S(1)}, f32[48,128]{1,0:T(8,128)S(1)}, u32[]{:S(2)}, u32[]{:S(2)}) %collective-permute-start) | collective-permute-done | bytes 24608 | tf_op jit(solution)/shard_map/ppermute | solution.py:286
  6.9 3.9 %collective-permute-start.3 = (f32[80,128]{1,0:T(8,128)S(1)}, f32[80,128]{1,0:T(8,128)S(1)}, u32[]{:S(2)}, u32[]{:S(2)}) collective-permute-start(f32[80,128]{1,0:T(8,128)S(1)} %pad_maximum_fusion.refs_0_), channel_id=1, source_target_pairs={{0,24},{4,28},{8,16},{12,20},{16,8},{20,12},{24,0},{28,4},{1,25},{... | collective-permute-start | bytes 122888 | tf_op jit(solution)/shard_map/ppermute | solution.py:286
  10.8 0.5 collective-permute-start.2
  11.5 1.3 %collective-permute-done.3.refs_3_ = f32[80,128]{1,0:T(8,128)S(1)} collective-permute-done((f32[80,128]{1,0:T(8,128)S(1)}, f32[80,128]{1,0:T(8,128)S(1)}, u32[]{:S(2)}, u32[]{:S(2)}) %collective-permute-start.3) | collective-permute-done | bytes 40992 | tf_op jit(solution)/shard_map/ppermute | solution.py:286
  12.8 2.0 %collective-permute-done.2.refs_2_ = f32[80,128]{1,0:T(8,128)S(1)} collective-permute-done((f32[80,128]{1,0:T(8,128)S(1)}, f32[80,128]{1,0:T(8,128)S(1)}, u32[]{:S(2)}, u32[]{:S(2)}) %collective-permute-start.2) | collective-permute-done | bytes 40992 | tf_op jit(solution)/shard_map/ppermute | solution.py:286
  15.3 3.0 %shard_map.113 = (f32[24,128]{1,0:T(8,128)S(1)}, f32[8,128]{1,0:T(8,128)S(1)}, f32[8,128]{1,0:T(8,128)S(1)}, f32[8,32,128]{2,1,0:T(8,128)S(1)}) custom-call(s32[97]{0:T(128)S(1)} %pad_add_fusion.meta, s32[4]{0:T(128)S(1)} %pad_add_fusion.2.place, bf16[48,128,128]{2,1,0:T(8,128)(2,1)S(1)} %copy-done.1, f32[9,128]{1,0:T(8,128)S(1)} %get-tuple-element.19.scale_col1, ...), custom_call_target="tpu_custom_call" | custom-call | tf_op jit(solution)/shard_map/pallas_call | solution.py:334
  18.3 1.1 %collective-permute-done.4 = f32[16,128]{1,0:T(8,128)S(1)} collective-permute-done((f32[16,128]{1,0:T(8,128)S(1)}, f32[16,128]{1,0:T(8,128)S(1)}, u32[]{:S(2)}, u32[]{:S(2)}) %collective-permute-start.4) | collective-permute-done | bytes 8224 | tf_op jit(solution)/shard_map/ppermute | solution.py:286
  19.5 4.5 %collective-permute-start.7 = (f32[24,128]{1,0:T(8,128)S(1)}, f32[24,128]{1,0:T(8,128)S(1)}, u32[]{:S(2)}, u32[]{:S(2)}) collective-permute-start(f32[24,128]{1,0:T(8,128)S(1)} %pad_maximum_fusion.2.refs_8_), channel_id=1, source_target_pairs={{0,27},{1,26},{2,25},{3,24},{4,31},{5,30},{6,29},{7,28},{8,19},{9,... | collective-permute-start | bytes 36872 | tf_op jit(solution)/shard_map/ppermute | solution.py:294
  24.0 1.7 %collective-permute-start.5 = (f32[24,128]{1,0:T(8,128)S(1)}, f32[24,128]{1,0:T(8,128)S(1)}, u32[]{:S(2)}, u32[]{:S(2)}) collective-permute-start(f32[24,128]{1,0:T(8,128)S(1)} %pad_maximum_fusion.2.refs_8_), channel_id=1, source_target_pairs={{0,9},{1,8},{2,11},{3,10},{4,13},{5,12},{6,15},{7,14},{8,1},{9,0},... | collective-permute-start | bytes 36872 | tf_op jit(solution)/shard_map/ppermute | solution.py:294
  25.7 1.1 %collective-permute-done.7.refs_11_ = f32[24,128]{1,0:T(8,128)S(1)} collective-permute-done((f32[24,128]{1,0:T(8,128)S(1)}, f32[24,128]{1,0:T(8,128)S(1)}, u32[]{:S(2)}, u32[]{:S(2)}) %collective-permute-start.7) | collective-permute-done | bytes 12320 | tf_op jit(solution)/shard_map/ppermute | solution.py:294
  26.8 2.7 %collective-permute-done.6.refs_10_ = f32[24,128]{1,0:T(8,128)S(1)} collective-permute-done((f32[24,128]{1,0:T(8,128)S(1)}, f32[24,128]{1,0:T(8,128)S(1)}, u32[]{:S(2)}, u32[]{:S(2)}) %collective-permute-start.6) | collective-permute-done | bytes 12320 | tf_op jit(solution)/shard_map/ppermute | solution.py:294
  29.5 7.2 %shard_map.114 = (bf16[48,128,128]{2,1,0:T(8,128)(2,1)S(1)}, f32[8,128]{1,0:T(8,128)S(1)}, f32[8,128]{1,0:T(8,128)S(1)}, f32[8,128]{1,0:T(8,128)S(1)}, f32[32,10...) custom-call(s32[97]{0:T(128)S(1)} %pad_add_fusion.meta, bf16[48,128,128]{2,1,0:T(8,128)(2,1)S(1)} %copy-done.1, ...), custom_call_target="tpu_custom_call" | custom-call | tf_op jit(solution)/shard_map/pallas_call | solution.py:359
  36.7 1.5 %collective-permute-done.8 = f32[4,32,128]{2,1,0:T(8,128)S(1)} collective-permute-done((f32[4,32,128]{2,1,0:T(8,128)}, f32[4,32,128]{2,1,0:T(8,128)S(1)}, u32[]{:S(2)}, u32[]{:S(2)}) %collective-permute-start.8) | collective-permute-done | bytes 65568 | tf_op jit(solution)/shard_map/ppermute | solution.py:286
  38.2 1.5 %collective-permute-start.11 = (f32[4,32,128]{2,1,0:T(8,128)S(1)}, f32[4,32,128]{2,1,0:T(8,128)S(1)}, u32[]{:S(2)}, u32[]{:S(2)}) collective-permute-start(f32[4,32,128]{2,1,0:T(8,128)S(1)} %add.26), channel_id=1, source_target_pairs={{0,24},{4,28},{8,16},{12,20},{16,8},{20,12},{24,0},{28,4},{1,25},{... | collective-permute-start | bytes 196616 | tf_op jit(solution)/shard_map/ppermute | solution.py:286
  39.7 1.6 %collective-permute-start.10 = (f32[4,32,128]{2,1,0:T(8,128)S(1)}, f32[4,32,128]{2,1,0:T(8,128)S(1)}, u32[]{:S(2)}, u32[]{:S(2)}) collective-permute-start(f32[4,32,128]{2,1,0:T(8,128)S(1)} %add.26), channel_id=1, source_target_pairs={{0,16},{4,20},{8,24},{12,28},{16,0},{20,4},{24,8},{28,12},{1,17},{... | collective-permute-start | bytes 196616 | tf_op jit(solution)/shard_map/ppermute | solution.py:286
  41.8 1.7 %collective-permute-done.11 = f32[4,32,128]{2,1,0:T(8,128)S(1)} collective-permute-done((f32[4,32,128]{2,1,0:T(8,128)S(1)}, f32[4,32,128]{2,1,0:T(8,128)S(1)}, u32[]{:S(2)}, u32[]{:S(2)}) %collective-permute-start.11) | collective-permute-done | bytes 65568 | tf_op jit(solution)/shard_map/ppermute | solution.py:286
  43.6 1.1 %collective-permute-done.10 = f32[4,32,128]{2,1,0:T(8,128)S(1)} collective-permute-done((f32[4,32,128]{2,1,0:T(8,128)S(1)}, f32[4,32,128]{2,1,0:T(8,128)S(1)}, u32[]{:S(2)}, u32[]{:S(2)}) %collective-permute-start.10) | collective-permute-done | bytes 65568 | tf_op jit(solution)/shard_map/ppermute | solution.py:286
  44.7 0.8 %collective-permute-done.9 = f32[4,32,128]{2,1,0:T(8,128)S(1)} collective-permute-done((f32[4,32,128]{2,1,0:T(8,128)S(1)}, f32[4,32,128]{2,1,0:T(8,128)S(1)}, u32[]{:S(2)}, u32[]{:S(2)}) %collective-permute-start.9) | collective-permute-done | bytes 65568 | tf_op jit(solution)/shard_map/ppermute | solution.py:286
  46.1 0.6 collective-permute-done.13
  46.8 0.9 %collective-permute-start.16 = (f32[8,128]{1,0:T(8,128)S(1)}, f32[8,128]{1,0:T(8,128)S(1)}, u32[]{:S(2)}, u32[]{:S(2)}) collective-permute-start(f32[8,128]{1,0:T(8,128)S(1)} %pad_maximum_fusion.3.refs_10_), channel_id=1, source_target_pairs={{0,3},{1,2},{2,1},{3,0},{4,7},{5,6},{6,5},{7,4},{8,11},{9,10},{10,... | collective-permute-start | bytes 12296 | tf_op jit(solution)/shard_map/ppermute | solution.py:286
  47.7 1.1 %collective-permute-start.15 = (f32[8,128]{1,0:T(8,128)S(1)}, f32[8,128]{1,0:T(8,128)S(1)}, u32[]{:S(2)}, u32[]{:S(2)}) collective-permute-start(f32[8,128]{1,0:T(8,128)S(1)} %pad_maximum_fusion.3.refs_10_), channel_id=1, source_target_pairs={{0,2},{1,3},{2,0},{3,1},{4,6},{5,7},{6,4},{7,5},{8,10},{9,11},{10,... | collective-permute-start | bytes 12296 | tf_op jit(solution)/shard_map/ppermute | solution.py:286
  48.8 2.4 %collective-permute-start.14 = (f32[8,128]{1,0:T(8,128)S(1)}, f32[8,128]{1,0:T(8,128)S(1)}, u32[]{:S(2)}, u32[]{:S(2)}) collective-permute-start(f32[8,128]{1,0:T(8,128)S(1)} %pad_maximum_fusion.3.refs_10_), channel_id=1, source_target_pairs={{0,1},{1,0},{2,3},{3,2},{4,5},{5,4},{6,7},{7,6},{8,9},{9,8},{10,11... | collective-permute-start | bytes 12296 | tf_op jit(solution)/shard_map/ppermute | solution.py:286
  51.2 1.0 %collective-permute-done.16.refs_13_ = f32[8,128]{1,0:T(8,128)S(1)} collective-permute-done((f32[8,128]{1,0:T(8,128)S(1)}, f32[8,128]{1,0:T(8,128)S(1)}, u32[]{:S(2)}, u32[]{:S(2)}) %collective-permute-start.16) | collective-permute-done | bytes 4128 | tf_op jit(solution)/shard_map/ppermute | solution.py:286
  52.2 0.5 collective-permute-done.14.refs_11_
  52.7 5.7 %shard_map.115 = (f32[8,128]{1,0:T(8,128)}, f32[32,1024]{1,0:T(8,128)}, f32[8,32,128]{2,1,0:T(8,128)}) custom-call(s32[97]{0:T(128)S(1)} %pad_add_fusion.meta, s32[2]{0:T(128)S(1)} %pad_add_fusion.1.place, bf16[48,128,128]{2,1,0:T(8,128)(2,1)S(1)} %get-tuple-element.25.refs_0_, f32[1,128]{1,0:T(1,128)S(1)} %constant_dynamic-slice_fusion.refs_1_, ...), custom_call_target="tpu_custom_call" | custom-call | tf_op jit(solution)/shard_map/pallas_call | solution.py:401
  58.4 3.4 %all-to-all-start = ((f32[8,32,128]{2,1,0:T(8,128)}), f32[8,32,128]{2,1,0:T(8,128)S(1)}, u32[]{:S(2)}, u32[]{:S(2)}) async-start(f32[8,32,128]{2,1,0:T(8,128)} %get-tuple-element.34), calls=%async_computation | async-start | bytes 262144 | tf_op jit(solution)/shard_map/all_to_all | solution.py:408
  61.8 5.4 %all-to-all-done = f32[8,32,128]{2,1,0:T(8,128)S(1)} async-done(((f32[8,32,128]{2,1,0:T(8,128)}), f32[8,32,128]{2,1,0:T(8,128)S(1)}, u32[]{:S(2)}, u32[]{:S(2)}) %all-to-all-start) | async-done | bytes 131104 | tf_op jit(solution)/shard_map/all_to_all | solution.py:408
  67.3 0.6 maximum_multiply_fusion
  (42 shorter events, 2.2 us)
Async XLA Ops:
  0.6 4.9 %copy-start.6 = (f32[32,128]{1,0:T(8,128)S(1)}, f32[32,128]{1,0:T(8,128)}, u32[]{:S(2)}) copy-start(f32[32,128]{1,0:T(8,128)} %param.17) | copy-start | bytes 49156
  2.1 1.4 %copy-start = (bf16[48,128,128]{2,1,0:T(8,128)(2,1)S(1)}, bf16[48,128,128]{2,1,0:T(8,128)(2,1)}, u32[]{:S(2)}) copy-start(bf16[48,128,128]{2,1,0:T(8,128)(2,1)} %refs_0_.1) | copy-start | bytes 4718596
  3.5 11.8 %copy-start.1 = (bf16[48,128,128]{2,1,0:T(8,128)(2,1)S(1)}, bf16[48,128,128]{2,1,0:T(8,128)(2,1)}, u32[]{:S(2)}) copy-start(bf16[48,128,128]{2,1,0:T(8,128)(2,1)} %refs_0_.1) | copy-start | bytes 4718596
  3.5 26.0 %copy-start.2 = (f32[32,1024]{1,0:T(8,128)S(1)}, f32[32,1024]{1,0:T(8,128)}, u32[]{:S(2)}) copy-start(f32[32,1024]{1,0:T(8,128)} %refs_7_.1) | copy-start | bytes 393220
  3.5 26.0 %copy-start.3 = (s32[32,128]{1,0:T(8,128)S(1)}, s32[32,128]{1,0:T(8,128)}, u32[]{:S(2)}) copy-start(s32[32,128]{1,0:T(8,128)} %refs_4_.1) | copy-start | bytes 49156
  3.5 26.0 %copy-start.4 = (s32[1024]{0:T(1024)S(1)}, s32[1024]{0:T(1024)}, u32[]{:S(2)}) copy-start(s32[1024]{0:T(1024)} %param.13) | copy-start | bytes 12292
  3.5 26.1 %copy-start.5 = (f32[1024]{0:T(1024)S(1)}, f32[1024]{0:T(1024)}, u32[]{:S(2)}) copy-start(f32[1024]{0:T(1024)} %param.15) | copy-start | bytes 12292
  5.5 1.4 %collective-permute-start = (f32[48,128]{1,0:T(8,128)S(1)}, f32[48,128]{1,0:T(8,128)S(1)}, u32[]{:S(2)}, u32[]{:S(2)}) collective-permute-start(f32[48,128]{1,0:T(8,128)S(1)} %pad_maximum_fusion.1), channel_id=1, source_target_pairs={{0,4},{4,0},{8,12},{12,8},{16,20},{20,16},{24,28},{28,24},{1,5},{5... | collective-permute-start | bytes 73736 | tf_op jit(solution)/shard_map/ppermute | solution.py:286
  6.9 5.8 %collective-permute-start.3 = (f32[80,128]{1,0:T(8,128)S(1)}, f32[80,128]{1,0:T(8,128)S(1)}, u32[]{:S(2)}, u32[]{:S(2)}) collective-permute-start(f32[80,128]{1,0:T(8,128)S(1)} %pad_maximum_fusion.refs_0_), channel_id=1, source_target_pairs={{0,24},{4,28},{8,16},{12,20},{16,8},{20,12},{24,0},{28,4},{1,25},{... | collective-permute-start | bytes 122888 | tf_op jit(solution)/shard_map/ppermute | solution.py:286
  10.8 4.0 %collective-permute-start.2 = (f32[80,128]{1,0:T(8,128)S(1)}, f32[80,128]{1,0:T(8,128)S(1)}, u32[]{:S(2)}, u32[]{:S(2)}) collective-permute-start(f32[80,128]{1,0:T(8,128)S(1)} %pad_maximum_fusion.refs_0_), channel_id=1, source_target_pairs={{0,16},{4,20},{8,24},{12,28},{16,0},{20,4},{24,8},{28,12},{1,17},{... | collective-permute-start | bytes 122888 | tf_op jit(solution)/shard_map/ppermute | solution.py:286
  11.3 4.0 %collective-permute-start.1 = (f32[80,128]{1,0:T(8,128)S(1)}, f32[80,128]{1,0:T(8,128)S(1)}, u32[]{:S(2)}, u32[]{:S(2)}) collective-permute-start(f32[80,128]{1,0:T(8,128)S(1)} %pad_maximum_fusion.refs_0_), channel_id=1, source_target_pairs={{0,8},{4,12},{8,0},{12,4},{16,24},{20,28},{24,16},{28,20},{1,9},{5... | collective-permute-start | bytes 122888 | tf_op jit(solution)/shard_map/ppermute | solution.py:286
  18.3 1.2 %collective-permute-start.4 = (f32[16,128]{1,0:T(8,128)S(1)}, f32[16,128]{1,0:T(8,128)S(1)}, u32[]{:S(2)}, u32[]{:S(2)}) collective-permute-start(f32[16,128]{1,0:T(8,128)S(1)} %slice.15), channel_id=1, source_target_pairs={{0,4},{4,0},{8,12},{12,8},{16,20},{20,16},{24,28},{28,24},{1,5},{5... | collective-permute-start | bytes 24584 | tf_op jit(solution)/shard_map/ppermute | solution.py:286
  19.5 7.3 %collective-permute-start.7 = (f32[24,128]{1,0:T(8,128)S(1)}, f32[24,128]{1,0:T(8,128)S(1)}, u32[]{:S(2)}, u32[]{:S(2)}) collective-permute-start(f32[24,128]{1,0:T(8,128)S(1)} %pad_maximum_fusion.2.refs_8_), channel_id=1, source_target_pairs={{0,27},{1,26},{2,25},{3,24},{4,31},{5,30},{6,29},{7,28},{8,19},{9,... | collective-permute-start | bytes 36872 | tf_op jit(solution)/shard_map/ppermute | solution.py:294
  24.0 5.5 %collective-permute-start.6 = (f32[24,128]{1,0:T(8,128)S(1)}, f32[24,128]{1,0:T(8,128)S(1)}, u32[]{:S(2)}, u32[]{:S(2)}) collective-permute-start(f32[24,128]{1,0:T(8,128)S(1)} %pad_maximum_fusion.2.refs_8_), channel_id=1, source_target_pairs={{0,18},{1,19},{2,16},{3,17},{4,22},{5,23},{6,20},{7,21},{8,26},{9,... | collective-permute-start | bytes 36872 | tf_op jit(solution)/shard_map/ppermute | solution.py:294
  24.0 5.5 %collective-permute-start.5 = (f32[24,128]{1,0:T(8,128)S(1)}, f32[24,128]{1,0:T(8,128)S(1)}, u32[]{:S(2)}, u32[]{:S(2)}) collective-permute-start(f32[24,128]{1,0:T(8,128)S(1)} %pad_maximum_fusion.2.refs_8_), channel_id=1, source_target_pairs={{0,9},{1,8},{2,11},{3,10},{4,13},{5,12},{6,15},{7,14},{8,1},{9,0},... | collective-permute-start | bytes 36872 | tf_op jit(solution)/shard_map/ppermute | solution.py:294
  36.7 1.5 %collective-permute-start.8 = (f32[4,32,128]{2,1,0:T(8,128)}, f32[4,32,128]{2,1,0:T(8,128)S(1)}, u32[]{:S(2)}, u32[]{:S(2)}) collective-permute-start(f32[4,32,128]{2,1,0:T(8,128)} %get-tuple-element.31), channel_id=1, source_target_pairs={{0,4},{4,0},{8,12},{12,8},{16,20},{20,16},{24,28},{28,24},{1,5},{5... | collective-permute-start | bytes 196616 | tf_op jit(solution)/shard_map/ppermute | solution.py:286
  38.2 5.4 %collective-permute-start.11 = (f32[4,32,128]{2,1,0:T(8,128)S(1)}, f32[4,32,128]{2,1,0:T(8,128)S(1)}, u32[]{:S(2)}, u32[]{:S(2)}) collective-permute-start(f32[4,32,128]{2,1,0:T(8,128)S(1)} %add.26), channel_id=1, source_target_pairs={{0,24},{4,28},{8,16},{12,20},{16,8},{20,12},{24,0},{28,4},{1,25},{... | collective-permute-start | bytes 196616 | tf_op jit(solution)/shard_map/ppermute | solution.py:286
  39.7 5.0 %collective-permute-start.10 = (f32[4,32,128]{2,1,0:T(8,128)S(1)}, f32[4,32,128]{2,1,0:T(8,128)S(1)}, u32[]{:S(2)}, u32[]{:S(2)}) collective-permute-start(f32[4,32,128]{2,1,0:T(8,128)S(1)} %add.26), channel_id=1, source_target_pairs={{0,16},{4,20},{8,24},{12,28},{16,0},{20,4},{24,8},{28,12},{1,17},{... | collective-permute-start | bytes 196616 | tf_op jit(solution)/shard_map/ppermute | solution.py:286
  41.2 4.3 %collective-permute-start.9 = (f32[4,32,128]{2,1,0:T(8,128)S(1)}, f32[4,32,128]{2,1,0:T(8,128)S(1)}, u32[]{:S(2)}, u32[]{:S(2)}) collective-permute-start(f32[4,32,128]{2,1,0:T(8,128)S(1)} %add.26), channel_id=1, source_target_pairs={{0,8},{4,12},{8,0},{12,4},{16,24},{20,28},{24,16},{28,20},{1,9},{5... | collective-permute-start | bytes 196616 | tf_op jit(solution)/shard_map/ppermute | solution.py:286
  45.5 1.2 %collective-permute-start.13 = (f32[4,128]{1,0:T(4,128)S(1)}, f32[4,128]{1,0:T(4,128)S(1)}, u32[]{:S(2)}, u32[]{:S(2)}) collective-permute-start(f32[4,128]{1,0:T(4,128)S(1)} %get-tuple-element.35), channel_id=1, source_target_pairs={{0,4},{4,0},{8,12},{12,8},{16,20},{20,16},{24,28},{28,24},{1,5},{5... | collective-permute-start | bytes 6152 | tf_op jit(solution)/shard_map/ppermute | solution.py:286
  45.6 7.1 %collective-permute-start.12 = (bf16[4,32,128]{2,1,0:T(8,128)(2,1)S(1)}, bf16[4,32,128]{2,1,0:T(8,128)(2,1)S(1)}, u32[]{:S(2)}, u32[]{:S(2)}) collective-permute-start(bf16[4,32,128]{2,1,0:T(8,128)(2,1)S(1)} %get-tuple-element.36.refs_8_), channel_id=1, source_target_pairs={{0,4},{4,0},{8,12},{12,8},{16,20},{20,16},{24,28},{28,24},{1,5},{5... | collective-permute-start | bytes 98312 | tf_op jit(solution)/shard_map/ppermute | solution.py:286
  46.8 5.4 %collective-permute-start.16 = (f32[8,128]{1,0:T(8,128)S(1)}, f32[8,128]{1,0:T(8,128)S(1)}, u32[]{:S(2)}, u32[]{:S(2)}) collective-permute-start(f32[8,128]{1,0:T(8,128)S(1)} %pad_maximum_fusion.3.refs_10_), channel_id=1, source_target_pairs={{0,3},{1,2},{2,1},{3,0},{4,7},{5,6},{6,5},{7,4},{8,11},{9,10},{10,... | collective-permute-start | bytes 12296 | tf_op jit(solution)/shard_map/ppermute | solution.py:286
  47.7 4.5 %collective-permute-start.15 = (f32[8,128]{1,0:T(8,128)S(1)}, f32[8,128]{1,0:T(8,128)S(1)}, u32[]{:S(2)}, u32[]{:S(2)}) collective-permute-start(f32[8,128]{1,0:T(8,128)S(1)} %pad_maximum_fusion.3.refs_10_), channel_id=1, source_target_pairs={{0,2},{1,3},{2,0},{3,1},{4,6},{5,7},{6,4},{7,5},{8,10},{9,11},{10,... | collective-permute-start | bytes 12296 | tf_op jit(solution)/shard_map/ppermute | solution.py:286
  48.8 4.0 %collective-permute-start.14 = (f32[8,128]{1,0:T(8,128)S(1)}, f32[8,128]{1,0:T(8,128)S(1)}, u32[]{:S(2)}, u32[]{:S(2)}) collective-permute-start(f32[8,128]{1,0:T(8,128)S(1)} %pad_maximum_fusion.3.refs_10_), channel_id=1, source_target_pairs={{0,1},{1,0},{2,3},{3,2},{4,5},{5,4},{6,7},{7,6},{8,9},{9,8},{10,11... | collective-permute-start | bytes 12296 | tf_op jit(solution)/shard_map/ppermute | solution.py:286
  58.4 8.8 %all-to-all-start = ((f32[8,32,128]{2,1,0:T(8,128)}), f32[8,32,128]{2,1,0:T(8,128)S(1)}, u32[]{:S(2)}, u32[]{:S(2)}) async-start(f32[8,32,128]{2,1,0:T(8,128)} %get-tuple-element.34), calls=%async_computation | async-start | bytes 262144 | tf_op jit(solution)/shard_map/all_to_all | solution.py:408

commit v2 on v0

v2 whole, which is shorter than its diff:
```python
import functools

import jax
import jax.numpy as jnp
from jax import lax
from jax.experimental import pallas as pl
from jax.experimental.pallas import tpu as pltpu
from jax.sharding import PartitionSpec as P

EPS = 1e-06
COST_RATE = 1.0
HOLD_BASE = 1.0
HOLD_CAP = 2.0
CAP_UNIT = 4.0
TAU_PLAN = 0.2
TAU_HOLD = 0.02
SIGMA = 0.05

B = 128
UNROLL = 16
VMEM = pl.BlockSpec(memory_space=pltpu.VMEM)
HBM = pl.BlockSpec(memory_space=pltpu.HBM)
F32 = jnp.float32
BF16 = jnp.bfloat16


def call(body, out_shape, scratch, n_hbm, n_vmem, limit=24 * 1024 * 1024):
    return pl.pallas_call(
        body,
        out_shape=out_shape,
        in_specs=[HBM] * n_hbm + [VMEM] * n_vmem,
        out_specs=[VMEM] * len(out_shape),
        scratch_shapes=scratch,
        compiler_params=pltpu.CompilerParams(vmem_limit_bytes=limit),
    )


def loop(first, last, unroll, step):
    trips = (last - first) // unroll

    def trip(i, carry):
        for u in range(unroll):
            step(first + i * unroll + u)
        return carry

    if trips == 1:
        trip(0, 0)
    else:
        lax.fori_loop(0, trips, trip, 0)
    for t in range(first + trips * unroll, last):
        step(t)


def index_scratch(slots):
    return [
        pltpu.SMEM((slots,), jnp.int32),
        pltpu.SMEM((slots,), jnp.int32),
        pltpu.SMEM((1,), jnp.int32),
        pltpu.SemaphoreType.DMA((3,)),
    ]


def fetch_index(sources, held):
    sems = held[3]
    copies = [pltpu.make_async_copy(s, held[i], sems.at[i]) for i, s in enumerate(sources)]
    for c in copies:
        c.start()

    def wait():
        for c in copies:
            c.wait()

    return wait


def position(held, rb, cb, t):
    live = t < held[2][0]
    return jnp.where(live, held[0][t], rb), jnp.where(live, held[1][t], cb)


def fold_rows(a):
    return jnp.max(a.reshape(B // 8, 8, B), axis=0)


def lane_peaks(acc, blocks, first, packed):
    lane = lax.broadcasted_iota(jnp.int32, (B, B), 1)
    for b in range(blocks):
        peak = jnp.max(acc[b].astype(F32), axis=1, keepdims=True)
        packed = jnp.where(lane == first + b, peak, packed)
    return packed


def spread_rows(rep, scales):
    n = scales.shape[0]
    turned = jnp.concatenate([scales, jnp.zeros((B - n, B), F32)], axis=0).T
    for b in range(n):
        rep[b] = jnp.broadcast_to(turned[:, b : b + 1], (B, B))


def col_peaks(acc, col_blocks):
    return jnp.concatenate(
        [jnp.max(acc[c], axis=0, keepdims=True) for c in range(col_blocks)], axis=0
    )


def first_peaks(rb, cb, slots, chunk, *refs):
    index, tiles_hbm, dual_hbm, payload, scale_col = refs[:3], refs[3], refs[4], refs[5], refs[6]
    held, (tiles, racc16, cacc16, racc, sems, dual_sem) = refs[7:11], refs[11:]
    wait_index = fetch_index(index, held)
    copies = [
        pltpu.make_async_copy(
            tiles_hbm.at[pl.ds(i * chunk, chunk)], tiles.at[pl.ds(i * chunk, chunk)], sems.at[i]
        )
        for i in range(slots // chunk)
    ]
    for c in copies:
        c.start()
    dual_copy = pltpu.make_async_copy(dual_hbm, payload.at[pl.ds(2 * rb, dual_hbm.shape[0])], dual_sem)
    dual_copy.start()
    racc16[...] = jnp.zeros_like(racc16)
    cacc16[...] = jnp.zeros_like(cacc16)
    racc[...] = jnp.zeros_like(racc)
    wait_index()

    def plain(t):
        a = jnp.abs(tiles[t])
        r, c = position(held, rb, cb, t)
        racc16[r] = jnp.maximum(racc16[r], a)
        cacc16[c] = jnp.maximum(cacc16[c], jnp.max(a.reshape(B // 16, 16, B), axis=0))

    for i, c in enumerate(copies):
        c.wait()
        loop(i * chunk, (i + 1) * chunk, chunk, plain)
    col_peak = jnp.concatenate(
        [jnp.max(cacc16[c].astype(F32), axis=0, keepdims=True) for c in range(cb)], axis=0
    )
    scale_col[0:cb] = 1.0 / jnp.sqrt(col_peak + EPS)
    scale_col[cb : cb + 1] = jnp.zeros((1, B), F32)

    def scaled(t):
        a = jnp.abs(tiles[t].astype(F32))
        r, c = position(held, rb, cb, t)
        racc[r] = jnp.maximum(racc[r], a * scale_col[pl.ds(c, 1), :])

    loop(0, slots, UNROLL, scaled)
    packed = lane_peaks(racc16, rb, 0, jnp.zeros((B, B), F32))
    packed = lane_peaks(racc, rb, rb, packed)
    payload[0 : 2 * rb] = packed.T[0 : 2 * rb]
    dual_copy.wait()


def second_peaks(rb, cb, slots, pays, *refs):
    index, tiles, scale_col1, parts = refs[:3], refs[3], refs[4], refs[5 : 5 + pays]
    peaks, scale_row2, scale_col3, dual = refs[5 + pays : 9 + pays]
    held, refs = refs[9 + pays : 13 + pays], refs[13 + pays :]
    rep, cacc, dacc, scol2, scol3, racc, racc_b = refs
    wait_index = fetch_index(index, held)
    chip = lax.axis_index("flt") // 2
    peak = parts[0][0 : 2 * rb]
    for p in parts[1:]:
        peak = jnp.maximum(peak, p[0 : 2 * rb])
    srow1 = 1.0 / jnp.sqrt(peak[0:rb] + EPS)
    srow2 = srow1 / jnp.sqrt(srow1 * peak[rb : 2 * rb] + EPS)
    scale_row2[...] = srow2
    spread_rows(rep, jnp.concatenate([srow1, srow2], axis=0))
    scen = dual.shape[1]
    per = rb // pays
    for k, p in enumerate(parts):
        for i in range(per):
            at = i if pays == 1 else 2 * (chip ^ k) + i
            dual[at] = p[2 * rb + scen * i : 2 * rb + scen * (i + 1)]
    cacc[...] = jnp.zeros_like(cacc)
    dacc[...] = jnp.zeros_like(dacc)
    racc[...] = jnp.zeros_like(racc)
    racc_b[...] = jnp.zeros_like(racc_b)
    wait_index()

    def columns(t):
        a = jnp.abs(tiles[t].astype(F32))
        r, c = position(held, 0, cb, t)
        cacc[c] = jnp.maximum(cacc[c], fold_rows(a * rep[r]))
        dacc[c] = jnp.maximum(dacc[c], fold_rows(a * rep[r + rb]))

    loop(0, slots, UNROLL, columns)
    c1 = scale_col1[0:cb]
    c2 = c1 / jnp.sqrt(c1 * col_peaks(cacc, cb) + EPS)
    c3 = c2 / jnp.sqrt(c2 * col_peaks(dacc, cb) + EPS)
    scol2[0:cb] = c2
    scol3[0:cb] = c3
    scol2[cb : cb + 1] = jnp.zeros((1, B), F32)
    scol3[cb : cb + 1] = jnp.zeros((1, B), F32)
    scale_col3[...] = c3

    def rows(t):
        a = jnp.abs(tiles[t].astype(F32))
        r, c = position(held, rb, cb, t)
        racc[r] = jnp.maximum(racc[r], a * scol2[pl.ds(c, 1), :])
        racc_b[r] = jnp.maximum(racc_b[r], a * scol3[pl.ds(c, 1), :])

    loop(0, slots, UNROLL, rows)
    packed = lane_peaks(racc, rb, 0, jnp.zeros((B, B), F32))
    packed = lane_peaks(racc_b, rb, rb, packed)
    peaks[...] = packed.T[0 : 2 * rb]


def pull(slots, held, mat, lhs, gacc):
    gacc[...] = jnp.zeros_like(gacc)

    def step(t):
        gacc[held[1][t]] += jnp.dot(lhs[held[0][t]], mat[t], preferred_element_type=F32)

    loop(0, slots, slots, step)


def holds(cb, gacc, offsets, scol, read_hold, write):
    for c in range(cb):
        scale = scol[c : c + 1]
        hold_cost = (HOLD_BASE + COST_RATE * offsets[c : c + 1].astype(F32)) * scale
        hold = read_hold(c, scale)
        hold_next = jnp.clip(hold - TAU_HOLD * (hold_cost + gacc[c]), 0.0, HOLD_CAP / scale)
        write(c, scale, hold_next, 2.0 * hold_next - hold)


def build_step(rb, cb, slots, *refs):
    index, refs = refs[:3], refs[3:]
    tiles, srow3, srow4, scale_col3, low, offsets, hold0, mat, scale_col4, hold1, turn = refs[:11]
    held, (rep, cacc, scol, gacc) = refs[11:15], refs[15:]
    wait_index = fetch_index(index, held)
    spread_rows(rep, jnp.concatenate([srow3[...], srow4[...]], axis=0))
    cacc[...] = jnp.zeros_like(cacc)
    wait_index()

    def columns(t):
        a = jnp.abs(tiles[t].astype(F32))
        r, c = position(held, 0, cb, t)
        cacc[c] = jnp.maximum(cacc[c], fold_rows(a * rep[r]))

    loop(0, slots, UNROLL, columns)
    c3 = scale_col3[...]
    c4 = c3 / jnp.sqrt(c3 * col_peaks(cacc, cb) + EPS)
    scale_col4[...] = c4
    scol[0:cb] = c4

    def build(t):
        live = (t < held[2][0]).astype(F32)
        r, c = held[0][t], held[1][t]
        value = tiles[t].astype(F32) * live * rep[r + rb] * scol[pl.ds(c, 1), :]
        mat[t] = value.astype(BF16)

    loop(0, slots, UNROLL, build)
    pull(slots, held, mat, low, gacc)

    def write(c, scale, hold, double):
        hold1[:, c * B : (c + 1) * B] = hold
        turn[:, c * B : (c + 1) * B] = double

    holds(
        cb, gacc, offsets, scol, lambda c, scale: hold0[:, c * B : (c + 1) * B] / scale, write
    )


def hold_step(rb, cb, slots, groups, *refs):
    index, mat, scol, offsets, hold1, lows = refs[:3], refs[3], refs[4], refs[5], refs[6], refs[7 : 7 + groups]
    hold2, turn = refs[7 + groups : 9 + groups]
    held, (low, gacc) = refs[9 + groups : 13 + groups], refs[13 + groups :]
    wait_index = fetch_index(index, held)
    core = lax.rem(lax.axis_index("flt"), 2)
    for k in range(groups):
        for i in range(rb // groups):
            at = i if groups == 1 else 2 * i + (core if k == 0 else 1 - core)
            low[at] = lows[k][i]
    wait_index()
    pull(slots, held, mat, low, gacc)

    def write(c, scale, hold, double):
        hold2[:, c * B : (c + 1) * B] = hold * scale
        turn[:, c * B : (c + 1) * B] = double

    holds(cb, gacc, offsets, scol, lambda c, scale: hold1[:, c * B : (c + 1) * B], write)


def plan_step(rb, cb, slots, scen_all, means, order, split, last, *refs):
    index, refs = refs[:3], refs[3:]
    mat, srow4, scol, offsets, capacity, plan, turn, own_dual = refs[:8]
    sums, refs = refs[8 : 8 + means], refs[8 + means :]
    plan_next, loads, refs = refs[0], refs[1 : 1 + split], refs[1 + split :]
    held, (lhs, gacc, lacc, mixed) = refs[:4], refs[4:]
    wait_index = fetch_index(index, held)
    me = lax.axis_index("flt")
    core = lax.rem(me, 2)
    total = sums[0][...]
    for s in sums[1:]:
        total = total + s[...]
    half = rb // 2
    for b in range(rb):
        at = b if not order else (2 * b + core if b < half else 2 * (b - half) + 1 - core)
        lhs[at] = three_terms(total[b : b + 1])
    wait_index()
    pull(slots, held, mat, lhs, gacc)
    for c in range(cb):
        scale = scol[c : c + 1]
        cost = COST_RATE * offsets[c : c + 1].astype(F32) * scale
        mean_grad = (gacc[c, 0:1] + gacc[c, 1:2] + gacc[c, 2:3]) / scen_all
        x = plan[c : c + 1] if last else plan[c : c + 1] / scale
        x_next = jnp.clip(x - TAU_PLAN * (cost + mean_grad), 0.0, 1.0 / scale)
        mixed[c] = ((2.0 * x_next - x) + turn[:, c * B : (c + 1) * B]).astype(BF16)
        plan_next[c : c + 1] = x_next * scale if last else x_next
    lacc[...] = jnp.zeros_like(lacc)

    def push(t):
        lacc[held[0][t]] += lax.dot_general(
            mixed[held[1][t]], mat[t], (((1,), (1,)), ((), ())), preferred_element_type=F32
        )

    loop(0, slots, slots, push)
    own = srow4[pl.ds(me, 1), :]
    lacc[me] += own_dual[...] * (1.0 / SIGMA) - CAP_UNIT * capacity[...].astype(F32) * own
    if split == 2:
        for j in range(half):
            loads[0][j] = lacc[2 * j + core]
            loads[1][j] = lacc[2 * j + 1 - core]
    else:
        loads[0][...] = lacc[...]


def three_terms(value):
    hi = value.astype(BF16).astype(F32)
    mid = (value - hi).astype(BF16).astype(F32)
    lo = value - hi - mid
    at = lax.broadcasted_iota(jnp.int32, (16, B), 0)
    terms = jnp.where(at == 0, hi, jnp.where(at == 1, mid, jnp.where(at == 2, lo, 0.0)))
    return terms.astype(BF16)


def flip(x, axis, mask):
    n = lax.axis_size(axis)
    return lax.ppermute(x, axis, [(i, i ^ mask) for i in range(n)])


def in_hbm(x):
    return pltpu.with_memory_space_constraint(x, pltpu.HBM)


def scenario_sums(low):
    return jnp.sum(low.astype(F32), axis=1)


def body(tiles, tile_row, tile_col, tile_count, slot_offset, capacity, plan0, hold0, dual0):
    slots = tiles.shape[0]
    cb = plan0.shape[0] // B
    nf, ns = lax.axis_size("flt"), lax.axis_size("scn")
    scen = dual0.shape[0]
    rb = nf
    scen_all = scen * ns
    small = nf == 8 and ns == 4
    me = lax.axis_index("flt")
    chip, core = me // 2, me % 2
    index = (tile_row, tile_col, tile_count)
    offsets = slot_offset.reshape(cb, B)
    f32 = functools.partial(jax.ShapeDtypeStruct, dtype=F32)
    held = index_scratch(slots)
    chunk = 12 if slots % 12 == 0 else slots

    mine, scol1 = call(
        functools.partial(first_peaks, rb, cb, slots, chunk),
        [f32((2 * rb + scen, B)), f32((cb + 1, B))],
        held
        + [
            pltpu.VMEM((slots, B, B), BF16),
            pltpu.VMEM((rb + 1, B, B), BF16),
            pltpu.VMEM((cb + 1, 16, B), BF16),
            pltpu.VMEM((rb + 1, B, B), F32),
            pltpu.SemaphoreType.DMA((slots // chunk,)),
            pltpu.SemaphoreType.DMA,
        ],
        5,
        0,
    )(in_hbm(tile_row), in_hbm(tile_col), tile_count, in_hbm(tiles), in_hbm(dual0))
    n = 2 * rb
    if small:
        other = flip(mine, "flt", 1)
        even = jnp.where(core == 0, mine[n:], other[n:])
        odd = jnp.where(core == 0, other[n:], mine[n:])
        mine = jnp.concatenate([jnp.maximum(mine[:n], other[:n]), even, odd], axis=0)
        parts = [mine] + [flip(mine, "flt", 2 * m) for m in (1, 2, 3)]
    else:
        gathered = lax.all_gather(mine[n:], "flt", axis=0, tiled=True)
        parts = [jnp.concatenate([lax.pmax(mine[:n], "flt"), gathered], axis=0)]
    peaks, srow2, scol3, dual = call(
        functools.partial(second_peaks, rb, cb, slots, len(parts)),
        [f32((2 * rb, B)), f32((rb, B)), f32((cb, B)), f32((rb, scen, B))],
        held
        + [
            pltpu.VMEM((2 * rb, B, B), F32),
            pltpu.VMEM((cb + 1, 8, B), F32),
            pltpu.VMEM((cb + 1, 8, B), F32),
            pltpu.VMEM((cb + 1, B), F32),
            pltpu.VMEM((cb + 1, B), F32),
            pltpu.VMEM((rb + 1, B, B), F32),
            pltpu.VMEM((rb + 1, B, B), F32),
        ],
        3,
        2 + len(parts),
    )(*index, tiles, scol1, *parts)
    if small:
        mine = jnp.maximum(peaks, flip(peaks, "flt", 1))
        far = [flip(mine, "flt", 2 * m) for m in (1, 2, 3)]
        peak = jnp.maximum(jnp.maximum(mine, far[0]), jnp.maximum(far[1], far[2]))
    else:
        peak = lax.pmax(peaks, "flt")
    srow3 = srow2 / jnp.sqrt(srow2 * peak[:rb] + EPS)
    srow4 = srow3 / jnp.sqrt(srow3 * peak[rb:] + EPS)
    own_row = lax.dynamic_slice_in_dim(srow4, me, 1, 0)
    low = (dual / srow4[:, None, :]).astype(BF16)
    sums = scenario_sums(low)
    own_dual = dual0 / own_row
    gacc = pltpu.VMEM((cb, scen, B), F32)
    mat, scol4, hold1, turn = call(
        functools.partial(build_step, rb, cb, slots),
        [
            jax.ShapeDtypeStruct((slots, B, B), BF16),
            f32((cb, B)),
            f32((scen, cb * B)),
            f32((scen, cb * B)),
        ],
        held
        + [
            pltpu.VMEM((2 * rb, B, B), F32),
            pltpu.VMEM((cb + 1, 8, B), F32),
            pltpu.VMEM((cb, B), F32),
            gacc,
        ],
        3,
        7,
    )(*index, tiles, srow3, srow4, scol3, low, offsets, hold0)
    plan = plan0.reshape(cb, B)
    for step in range(2):
        if step:
            if small:
                half = loads[0] + flip(loads[1], "flt", 1)
                far = [flip(half, "flt", 2 * m) for m in (1, 2, 3)]
                y = jnp.maximum(SIGMA * (half + far[0] + far[1] + far[2]), 0.0)
                low = y.astype(BF16)
                part = scenario_sums(low)
                lows = [low, flip(low, "flt", 1)]
                sums = jnp.concatenate([part, flip(part, "flt", 1)], axis=0)
                own_dual = lax.dynamic_index_in_dim(y, chip, 0, False)
            else:
                y = jnp.maximum(SIGMA * lax.psum(loads[0], "flt"), 0.0)
                lows = [y.astype(BF16)]
                sums = scenario_sums(lows[0])
                own_dual = lax.dynamic_index_in_dim(y, me, 0, False)
            hold, turn = call(
                functools.partial(hold_step, rb, cb, slots, len(lows)),
                [f32((scen, cb * B)), f32((scen, cb * B))],
                held + [pltpu.VMEM((rb, scen, B), BF16), gacc],
                3,
                4 + len(lows),
            )(*index, mat, scol4, offsets, hold1, *lows)
        if small:
            totals = [sums] + [flip(sums, "scn", m) for m in (1, 2, 3)]
        else:
            totals = [lax.psum(sums, "scn")]
        split = 2 if small and not step else 1
        plan, *loads = call(
            functools.partial(
                plan_step, rb, cb, slots, scen_all, len(totals), small and step == 1, split, step == 1
            ),
            [f32((cb, B))] + [f32((rb // split, scen, B))] * split,
            held
            + [
                pltpu.VMEM((rb, 16, B), BF16),
                pltpu.VMEM((cb, 16, B), F32),
                pltpu.VMEM((rb, scen, B), F32),
                pltpu.VMEM((cb, scen, B), BF16),
            ],
            3,
            8 + len(totals),
        )(*index, mat, srow4, scol4, offsets, capacity, plan, turn, own_dual, *totals)
    total = jnp.sum(lax.all_to_all(loads[0], "flt", 0, 0), axis=0)
    dual = jnp.maximum(SIGMA * total, 0.0) * own_row
    return plan.reshape(-1), hold, dual


def solution(mesh):
    return jax.shard_map(
        body,
        mesh=mesh,
        in_specs=(
            P("flt", None, None),
            P("flt"),
            P("flt"),
            P("flt"),
            P("flt"),
            P("scn", "flt"),
            P("flt"),
            P("scn", "flt"),
            P("scn", "flt"),
        ),
        out_specs=(P("flt"), P("scn", "flt"), P("scn", "flt")),
        check_vma=False,
    )
```

time: 220 us -> 62.2 us (0.28)
  blocking collectives: 91.2 us -> 8.13 us
  waiting for transfers between devices: 61.5 us -> 15.3 us
  other arithmetic: 37.7 us -> 0.76 us
  starting transfers between devices: 0.08 us -> 21.8 us
  Pallas kernels: 0 us -> 14.3 us
  between operations: 15.2 us -> 1.64 us
  local copies, waits for them, and re-layouts: 10.8 us -> 0.05 us
  matrix products: 3.11 us -> 0 us
    reduce_scatter x2 -> x0, waiting for transfers between devices: 61.5 us -> none  [body(): lax.psum_scatter(partial_value, 'flt', scatter_dimension=1, tiled=True)]
    pmax x4 -> x0, blocking collectives: 50.5 us -> none  [body(): row_peak = lax.pmax(local_rpeak, 'flt')]
    psum x2 -> x0, blocking collectives: 23.7 us -> none  [body(): mean_grad = lax.psum(jnp.sum(grad, axis=0), 'scn') / scen_all]
    ppermute x0 -> x20, starting transfers between devices: none -> 21.8 us  [flip(): return lax.ppermute(x, axis, [(i, i ^ mask) for i in range(n)])]
    all_gather x2 -> x0, blocking collectives: 17 us -> none  [body(): lax.all_gather(dual.astype(jnp.bfloat16), 'flt', axis=1, tiled=True)]
    ppermute x0 -> x20, waiting for transfers between devices: none -> 15.3 us  [flip(): return lax.ppermute(x, axis, [(i, i ^ mask) for i in range(n)])]
    pallas_call x0 -> x6, Pallas kernels: none -> 14.3 us  [the longest x2 4.6 us: body(): call(functools.partial(plan_step, rb, cb, slots, scen_all, len(totals), s...]
    scatter-add x4 -> x0, other arithmetic: 10.1 us -> none  [the longest x2 5.05 us: pull_columns(): total = jax.ops.segment_sum(product, tile_col, num_segments=col_blocks)]
  transfers between devices with their start and end apart: 2 -> 20, of which waited for: 2 -> 15; matrix products, arithmetic and copies ran while one was open for 0% -> 0% of each run, Pallas kernels for 0% -> 7%
where the time goes in v2:
time: 62.2 us; the launch traced here: 62 us
  starting transfers between devices  21.8 us (35%)
  waiting for transfers between devices  15.3 us (25%)
  Pallas kernels  14.3 us (23%)
  blocking collectives  8.13 us (13%)
  between operations  1.64 us (3%)
  other arithmetic  0.76 us (1%)
    ppermute x20, starting transfers between devices, flip(): return lax.ppermute(x, axis, [(i, i ^ mask) for i in range(n)])  21.8 us
    ppermute x20, waiting for transfers between devices, flip(): return lax.ppermute(x, axis, [(i, i ^ mask) for i in range(n)])  15.3 us
    all_to_all x1, blocking collectives, body(): total = jnp.sum(lax.all_to_all(loads[0], 'flt', 0, 0), axis=0)  8.13 us
    pallas_call x2, Pallas kernels, body(): call(functools.partial(plan_step, rb, cb, slots, scen_all, len(totals), s...  4.6 us
    pallas_call x1, Pallas kernels, body(): call(functools.partial(second_peaks, rb, cb, slots, len(parts)), [f32((2...  2.77 us
    pallas_call x1, Pallas kernels, body(): call(functools.partial(first_peaks, rb, cb, slots, chunk), [f32((2 * rb +...  2.62 us
    pallas_call x1, Pallas kernels, body(): call(functools.partial(build_step, rb, cb, slots), [jax.ShapeDtypeStruct(...  2.51 us
    pallas_call x1, Pallas kernels, body(): call(functools.partial(hold_step, rb, cb, slots, len(lows)), [f32((scen,...  1.81 us
  transfers between devices with their start and end apart: 20, of which 15 were waited for; matrix products, arithmetic and copies ran while one was open for 0% of the time, Pallas kernels for 7%

profile of v2, /device:TPU:0, one launch (start us, length us, event | category | flops | bytes accessed | tf_op | source)
XLA Modules:
  0.0 62.0 jit_solution(393422066096545329)
XLA Ops:
  1.5 2.6 %shard_map.112 = (f32[48,128]{1,0:T(8,128)S(1)}, f32[9,128]{1,0:T(8,128)S(1)}) custom-call(s32[48]{0:T(128)} %refs_0_.11, s32[48]{0:T(128)} %refs_1_.11, s32[1]{0:T(128)S(6)} %copy.12.refs_2_, bf16[48,128,128]{2,1,0:T(8,128)(2,1)} %refs_3_.5, f32[32,128]{1,0:T(8,128)} %refs_4_.1), custom_call_target="tpu_custom_call" | custom-call | tf_op jit(solution)/shard_map/pallas_call | solution.py:364
  4.1 0.5 collective-permute-start
  4.6 0.8 %collective-permute-done = f32[48,128]{1,0:T(8,128)S(1)} collective-permute-done((f32[48,128]{1,0:T(8,128)S(1)}, f32[48,128]{1,0:T(8,128)S(1)}, u32[]{:S(2)}, u32[]{:S(2)}) %collective-permute-start) | collective-permute-done | bytes 24608 | tf_op jit(solution)/shard_map/ppermute | solution.py:337
  5.5 3.9 %collective-permute-start.3 = (f32[80,128]{1,0:T(8,128)S(1)}, f32[80,128]{1,0:T(8,128)S(1)}, u32[]{:S(2)}, u32[]{:S(2)}) collective-permute-start(f32[80,128]{1,0:T(8,128)S(1)} %pad_maximum_fusion.refs_5_), channel_id=1, source_target_pairs={{0,24},{4,28},{8,16},{12,20},{16,8},{20,12},{24,0},{28,4},{1,25},{... | collective-permute-start | bytes 122888 | tf_op jit(solution)/shard_map/ppermute | solution.py:337
  9.3 0.5 collective-permute-start.2
  10.0 1.3 %collective-permute-done.3.refs_8_ = f32[80,128]{1,0:T(8,128)S(1)} collective-permute-done((f32[80,128]{1,0:T(8,128)S(1)}, f32[80,128]{1,0:T(8,128)S(1)}, u32[]{:S(2)}, u32[]{:S(2)}) %collective-permute-start.3) | collective-permute-done | bytes 40992 | tf_op jit(solution)/shard_map/ppermute | solution.py:337
  11.3 2.0 %collective-permute-done.2.refs_7_ = f32[80,128]{1,0:T(8,128)S(1)} collective-permute-done((f32[80,128]{1,0:T(8,128)S(1)}, f32[80,128]{1,0:T(8,128)S(1)}, u32[]{:S(2)}, u32[]{:S(2)}) %collective-permute-start.2) | collective-permute-done | bytes 40992 | tf_op jit(solution)/shard_map/ppermute | solution.py:337
  13.3 0.5 collective-permute-done.1.refs_6_
  13.9 2.8 %shard_map.113 = (f32[16,128]{1,0:T(8,128)S(1)}, f32[8,128]{1,0:T(8,128)S(1)}, f32[8,128]{1,0:T(8,128)S(1)}, f32[8,32,128]{2,1,0:T(8,128)S(1)}) custom-call(s32[48]{0:T(128)S(1)} %copy-done.4, s32[48]{0:T(128)S(1)} %copy-done.5, s32[1]{0:T(128)S(6)} %copy.12.refs_2_, bf16[48,128,128]{2,1,0:T(8,128)(2,1)S(1)} %copy-done, ...), custom_call_target="tpu_custom_call" | custom-call | tf_op jit(solution)/shard_map/pallas_call | solution.py:389
  16.7 1.2 %collective-permute-done.4 = f32[16,128]{1,0:T(8,128)S(1)} collective-permute-done((f32[16,128]{1,0:T(8,128)S(1)}, f32[16,128]{1,0:T(8,128)S(1)}, u32[]{:S(2)}, u32[]{:S(2)}) %collective-permute-start.4) | collective-permute-done | bytes 8224 | tf_op jit(solution)/shard_map/ppermute | solution.py:337
  17.9 1.5 %collective-permute-start.7 = (f32[16,128]{1,0:T(8,128)S(1)}, f32[16,128]{1,0:T(8,128)S(1)}, u32[]{:S(2)}, u32[]{:S(2)}) collective-permute-start(f32[16,128]{1,0:T(8,128)S(1)} %max.28), channel_id=1, source_target_pairs={{0,24},{4,28},{8,16},{12,20},{16,8},{20,12},{24,0},{28,4},{1,25},{... | collective-permute-start | bytes 24584 | tf_op jit(solution)/shard_map/ppermute | solution.py:337
  19.5 1.9 %collective-permute-start.5 = (f32[16,128]{1,0:T(8,128)S(1)}, f32[16,128]{1,0:T(8,128)S(1)}, u32[]{:S(2)}, u32[]{:S(2)}) collective-permute-start(f32[16,128]{1,0:T(8,128)S(1)} %max.28), channel_id=1, source_target_pairs={{0,8},{4,12},{8,0},{12,4},{16,24},{20,28},{24,16},{28,20},{1,9},{5... | collective-permute-start | bytes 24584 | tf_op jit(solution)/shard_map/ppermute | solution.py:337
  21.4 1.1 %collective-permute-done.7 = f32[16,128]{1,0:T(8,128)S(1)} collective-permute-done((f32[16,128]{1,0:T(8,128)S(1)}, f32[16,128]{1,0:T(8,128)S(1)}, u32[]{:S(2)}, u32[]{:S(2)}) %collective-permute-start.7) | collective-permute-done | bytes 8224 | tf_op jit(solution)/shard_map/ppermute | solution.py:337
  22.4 0.6 collective-permute-done.6
  23.2 4.1 %collective-permute-start.10 = (f32[8,128]{1,0:T(8,128)S(1)}, f32[8,128]{1,0:T(8,128)S(1)}, u32[]{:S(2)}, u32[]{:S(2)}) collective-permute-start(f32[8,128]{1,0:T(8,128)S(1)} %get-tuple-element.40.refs_11_), channel_id=1, source_target_pairs={{0,3},{1,2},{2,1},{3,0},{4,7},{5,6},{6,5},{7,4},{8,11},{9,10},{10,... | collective-permute-start | bytes 12296 | tf_op jit(solution)/shard_map/ppermute | solution.py:337
  27.3 0.6 %collective-permute-start.8 = (f32[8,128]{1,0:T(8,128)S(1)}, f32[8,128]{1,0:T(8,128)S(1)}, u32[]{:S(2)}, u32[]{:S(2)}) collective-permute-start(f32[8,128]{1,0:T(8,128)S(1)} %get-tuple-element.40.refs_11_), channel_id=1, source_target_pairs={{0,1},{1,0},{2,3},{3,2},{4,5},{5,4},{6,7},{7,6},{8,9},{9,8},{10,11... | collective-permute-start | bytes 12296 | tf_op jit(solution)/shard_map/ppermute | solution.py:337
  28.0 2.5 %shard_map.114 = (bf16[48,128,128]{2,1,0:T(8,128)(2,1)S(1)}, f32[8,128]{1,0:T(8,128)S(1)}, f32[32,1024]{1,0:T(8,128)S(1)}, f32[32,1024]{1,0:T(8,128)S(1)}) custom-call(s32[48]{0:T(128)S(1)} %copy-done.4, s32[48]{0:T(128)S(1)} %copy-done.5, s32[1]{0:T(128)S(6)} %copy.12.refs_2_, bf16[48,128,128]{2,1,0:T(8,128)(2,1)S(1)} %copy-done, ...), custom_call_target="tpu_custom_call" | custom-call | tf_op jit(solution)/shard_map/pallas_call | solution.py:418
  30.5 1.3 %collective-permute-done.9.refs_13_ = f32[8,128]{1,0:T(8,128)S(1)} collective-permute-done((f32[8,128]{1,0:T(8,128)S(1)}, f32[8,128]{1,0:T(8,128)S(1)}, u32[]{:S(2)}, u32[]{:S(2)}) %collective-permute-start.9) | collective-permute-done | bytes 4128 | tf_op jit(solution)/shard_map/ppermute | solution.py:337
  31.8 2.1 %shard_map.115 = (f32[8,128]{1,0:T(8,128)S(1)}, f32[4,32,128]{2,1,0:T(8,128)S(1)}, f32[4,32,128]{2,1,0:T(8,128)S(1)}) custom-call(s32[48]{0:T(128)S(1)} %copy-done.4, s32[48]{0:T(128)S(1)} %copy-done.5, s32[1]{0:T(128)S(6)} %copy.12.refs_2_, bf16[48,128,128]{2,1,0:T(8,128)(2,1)S(1)} %get-tuple-element.26.refs_3_, ...), custom_call_target="tpu_custom_call" | custom-call | tf_op jit(solution)/shard_map/pallas_call | solution.py:465
  34.0 1.2 %collective-permute-done.11 = f32[4,32,128]{2,1,0:T(8,128)S(1)} collective-permute-done((f32[4,32,128]{2,1,0:T(8,128)S(1)}, f32[4,32,128]{2,1,0:T(8,128)S(1)}, u32[]{:S(2)}, u32[]{:S(2)}) %collective-permute-start.11) | collective-permute-done | bytes 65568 | tf_op jit(solution)/shard_map/ppermute | solution.py:337
  35.2 2.5 %collective-permute-start.14 = (f32[4,32,128]{2,1,0:T(8,128)S(1)}, f32[4,32,128]{2,1,0:T(8,128)S(1)}, u32[]{:S(2)}, u32[]{:S(2)}) collective-permute-start(f32[4,32,128]{2,1,0:T(8,128)S(1)} %add.34), channel_id=1, source_target_pairs={{0,24},{4,28},{8,16},{12,20},{16,8},{20,12},{24,0},{28,4},{1,25},{... | collective-permute-start | bytes 196616 | tf_op jit(solution)/shard_map/ppermute | solution.py:337
  38.2 0.5 collective-permute-start.12
  38.8 1.7 %collective-permute-done.14 = f32[4,32,128]{2,1,0:T(8,128)S(1)} collective-permute-done((f32[4,32,128]{2,1,0:T(8,128)S(1)}, f32[4,32,128]{2,1,0:T(8,128)S(1)}, u32[]{:S(2)}, u32[]{:S(2)}) %collective-permute-start.14) | collective-permute-done | bytes 65568 | tf_op jit(solution)/shard_map/ppermute | solution.py:337
  40.5 1.5 %collective-permute-done.13 = f32[4,32,128]{2,1,0:T(8,128)S(1)} collective-permute-done((f32[4,32,128]{2,1,0:T(8,128)S(1)}, f32[4,32,128]{2,1,0:T(8,128)S(1)}, u32[]{:S(2)}, u32[]{:S(2)}) %collective-permute-start.13) | collective-permute-done | bytes 65568 | tf_op jit(solution)/shard_map/ppermute | solution.py:337
  43.1 0.6 %collective-permute-done.16 = f32[4,128]{1,0:T(4,128)S(1)} collective-permute-done((f32[4,128]{1,0:T(4,128)S(1)}, f32[4,128]{1,0:T(4,128)S(1)}, u32[]{:S(2)}, u32[]{:S(2)}) %collective-permute-start.16) | collective-permute-done | bytes 2080 | tf_op jit(solution)/shard_map/ppermute | solution.py:337
  43.8 2.5 %collective-permute-start.19 = (f32[8,128]{1,0:T(8,128)S(1)}, f32[8,128]{1,0:T(8,128)S(1)}, u32[]{:S(2)}, u32[]{:S(2)}) collective-permute-start(f32[8,128]{1,0:T(8,128)S(1)} %pad_maximum_fusion.1.refs_11_), channel_id=1, source_target_pairs={{0,3},{1,2},{2,1},{3,0},{4,7},{5,6},{6,5},{7,4},{8,11},{9,10},{10,... | collective-permute-start | bytes 12296 | tf_op jit(solution)/shard_map/ppermute | solution.py:337
  46.2 1.9 %collective-permute-start.17 = (f32[8,128]{1,0:T(8,128)S(1)}, f32[8,128]{1,0:T(8,128)S(1)}, u32[]{:S(2)}, u32[]{:S(2)}) collective-permute-start(f32[8,128]{1,0:T(8,128)S(1)} %pad_maximum_fusion.1.refs_11_), channel_id=1, source_target_pairs={{0,1},{1,0},{2,3},{3,2},{4,5},{5,4},{6,7},{7,6},{8,9},{9,8},{10,11... | collective-permute-start | bytes 12296 | tf_op jit(solution)/shard_map/ppermute | solution.py:337
  48.2 1.8 %shard_map.116 = (f32[32,1024]{1,0:T(8,128)}, f32[32,1024]{1,0:T(8,128)S(1)}) custom-call(s32[48]{0:T(128)S(1)} %copy-done.4, s32[48]{0:T(128)S(1)} %copy-done.5, s32[1]{0:T(128)S(6)} %copy.12.refs_2_, bf16[48,128,128]{2,1,0:T(8,128)(2,1)S(1)} %get-tuple-element.26.refs_3_, f32[8,128]{1,0:T(8,128)S(1)} %get-tuple-element.27.refs_5_.refs_4_, ...), custom_call_target="tpu_custom_call" | custom-call | tf_op jit(solution)/shard_map/pallas_call | solution.py:453
  50.0 0.7 %collective-permute-done.18.refs_13_ = f32[8,128]{1,0:T(8,128)S(1)} collective-permute-done((f32[8,128]{1,0:T(8,128)S(1)}, f32[8,128]{1,0:T(8,128)S(1)}, u32[]{:S(2)}, u32[]{:S(2)}) %collective-permute-start.18) | collective-permute-done | bytes 4128 | tf_op jit(solution)/shard_map/ppermute | solution.py:337
  50.8 2.5 %shard_map.117 = (f32[8,128]{1,0:T(8,128)}, f32[8,32,128]{2,1,0:T(8,128)S(1)}) custom-call(s32[48]{0:T(128)S(1)} %copy-done.4, s32[48]{0:T(128)S(1)} %copy-done.5, s32[1]{0:T(128)S(6)} %copy.12.refs_2_, bf16[48,128,128]{2,1,0:T(8,128)(2,1)S(1)} %get-tuple-element.26.refs_3_, f32[8,128]{1,0:T(8,128)S(1)} %get-tuple-element.42.refs_5_.refs_4_, ...), custom_call_target="tpu_custom_call" | custom-call | tf_op jit(solution)/shard_map/pallas_call | solution.py:465
  53.3 8.1 %all_to_all.5 = f32[8,32,128]{2,1,0:T(8,128)S(1)} all-to-all(f32[8,32,128]{2,1,0:T(8,128)S(1)} %get-tuple-element.36), channel_id=1, replica_groups=mesh['flt'=8,'scn'=4] {'flt'}, dimensions={0} | all-to-all | bytes 262144 | tf_op jit(solution)/shard_map/all_to_all | solution.py:480
  61.4 0.6 maximum_multiply_fusion
  (46 shorter events, 2.3 us)
Async XLA Ops:
  0.6 13.2 %copy-start.5 = (s32[48]{0:T(128)S(1)}, s32[48]{0:T(128)}, u32[]{:S(2)}) copy-start(s32[48]{0:T(128)} %refs_1_.11) | copy-start | bytes 580
  0.6 13.2 %copy-start.4 = (s32[48]{0:T(128)S(1)}, s32[48]{0:T(128)}, u32[]{:S(2)}) copy-start(s32[48]{0:T(128)} %refs_0_.11) | copy-start | bytes 580
  0.7 13.2 %copy-start = (bf16[48,128,128]{2,1,0:T(8,128)(2,1)S(1)}, bf16[48,128,128]{2,1,0:T(8,128)(2,1)}, u32[]{:S(2)}) copy-start(bf16[48,128,128]{2,1,0:T(8,128)(2,1)} %refs_3_.5) | copy-start | bytes 4718596
  1.4 26.5 %copy-start.7 = (f32[32,128]{1,0:T(8,128)S(1)}, f32[32,128]{1,0:T(8,128)}, u32[]{:S(2)}) copy-start(f32[32,128]{1,0:T(8,128)} %refs_4_.1) | copy-start | bytes 49156
  1.4 26.5 %copy-start.1 = (f32[32,1024]{1,0:T(8,128)S(1)}, f32[32,1024]{1,0:T(8,128)}, u32[]{:S(2)}) copy-start(f32[32,1024]{1,0:T(8,128)} %refs_9_.1) | copy-start | bytes 393220
  1.4 26.5 %copy-start.3 = (s32[1024]{0:T(1024)S(1)}, s32[1024]{0:T(1024)}, u32[]{:S(2)}) copy-start(s32[1024]{0:T(1024)} %param.13) | copy-start | bytes 12292
  4.1 1.4 %collective-permute-start = (f32[48,128]{1,0:T(8,128)S(1)}, f32[48,128]{1,0:T(8,128)S(1)}, u32[]{:S(2)}, u32[]{:S(2)}) collective-permute-start(f32[48,128]{1,0:T(8,128)S(1)} %get-tuple-element.21), channel_id=1, source_target_pairs={{0,4},{4,0},{8,12},{12,8},{16,20},{20,16},{24,28},{28,24},{1,5},{5... | collective-permute-start | bytes 73736 | tf_op jit(solution)/shard_map/ppermute | solution.py:337
  5.5 5.8 %collective-permute-start.3 = (f32[80,128]{1,0:T(8,128)S(1)}, f32[80,128]{1,0:T(8,128)S(1)}, u32[]{:S(2)}, u32[]{:S(2)}) collective-permute-start(f32[80,128]{1,0:T(8,128)S(1)} %pad_maximum_fusion.refs_5_), channel_id=1, source_target_pairs={{0,24},{4,28},{8,16},{12,20},{16,8},{20,12},{24,0},{28,4},{1,25},{... | collective-permute-start | bytes 122888 | tf_op jit(solution)/shard_map/ppermute | solution.py:337
  9.3 4.0 %collective-permute-start.2 = (f32[80,128]{1,0:T(8,128)S(1)}, f32[80,128]{1,0:T(8,128)S(1)}, u32[]{:S(2)}, u32[]{:S(2)}) collective-permute-start(f32[80,128]{1,0:T(8,128)S(1)} %pad_maximum_fusion.refs_5_), channel_id=1, source_target_pairs={{0,16},{4,20},{8,24},{12,28},{16,0},{20,4},{24,8},{28,12},{1,17},{... | collective-permute-start | bytes 122888 | tf_op jit(solution)/shard_map/ppermute | solution.py:337
  9.8 4.0 %collective-permute-start.1 = (f32[80,128]{1,0:T(8,128)S(1)}, f32[80,128]{1,0:T(8,128)S(1)}, u32[]{:S(2)}, u32[]{:S(2)}) collective-permute-start(f32[80,128]{1,0:T(8,128)S(1)} %pad_maximum_fusion.refs_5_), channel_id=1, source_target_pairs={{0,8},{4,12},{8,0},{12,4},{16,24},{20,28},{24,16},{28,20},{1,9},{5... | collective-permute-start | bytes 122888 | tf_op jit(solution)/shard_map/ppermute | solution.py:337
  13.9 17.9 %copy-start.2 = (s32[32,128]{1,0:T(8,128)S(1)}, s32[32,128]{1,0:T(8,128)}, u32[]{:S(2)}) copy-start(s32[32,128]{1,0:T(8,128)} %refs_7_.3) | copy-start | bytes 49156
  13.9 17.9 %copy-start.6 = (f32[1024]{0:T(1024)S(1)}, f32[1024]{0:T(1024)}, u32[]{:S(2)}) copy-start(f32[1024]{0:T(1024)} %param.15) | copy-start | bytes 12292
  16.7 1.2 %collective-permute-start.4 = (f32[16,128]{1,0:T(8,128)S(1)}, f32[16,128]{1,0:T(8,128)S(1)}, u32[]{:S(2)}, u32[]{:S(2)}) collective-permute-start(f32[16,128]{1,0:T(8,128)S(1)} %get-tuple-element.23), channel_id=1, source_target_pairs={{0,4},{4,0},{8,12},{12,8},{16,20},{20,16},{24,28},{28,24},{1,5},{5... | collective-permute-start | bytes 24584 | tf_op jit(solution)/shard_map/ppermute | solution.py:337
  17.9 4.5 %collective-permute-start.7 = (f32[16,128]{1,0:T(8,128)S(1)}, f32[16,128]{1,0:T(8,128)S(1)}, u32[]{:S(2)}, u32[]{:S(2)}) collective-permute-start(f32[16,128]{1,0:T(8,128)S(1)} %max.28), channel_id=1, source_target_pairs={{0,24},{4,28},{8,16},{12,20},{16,8},{20,12},{24,0},{28,4},{1,25},{... | collective-permute-start | bytes 24584 | tf_op jit(solution)/shard_map/ppermute | solution.py:337
  19.4 3.7 %collective-permute-start.6 = (f32[16,128]{1,0:T(8,128)S(1)}, f32[16,128]{1,0:T(8,128)S(1)}, u32[]{:S(2)}, u32[]{:S(2)}) collective-permute-start(f32[16,128]{1,0:T(8,128)S(1)} %max.28), channel_id=1, source_target_pairs={{0,16},{4,20},{8,24},{12,28},{16,0},{20,4},{24,8},{28,12},{1,17},{... | collective-permute-start | bytes 24584 | tf_op jit(solution)/shard_map/ppermute | solution.py:337
  19.5 3.7 %collective-permute-start.5 = (f32[16,128]{1,0:T(8,128)S(1)}, f32[16,128]{1,0:T(8,128)S(1)}, u32[]{:S(2)}, u32[]{:S(2)}) collective-permute-start(f32[16,128]{1,0:T(8,128)S(1)} %max.28), channel_id=1, source_target_pairs={{0,8},{4,12},{8,0},{12,4},{16,24},{20,28},{24,16},{28,20},{1,9},{5... | collective-permute-start | bytes 24584 | tf_op jit(solution)/shard_map/ppermute | solution.py:337
  23.2 7.3 %collective-permute-start.10 = (f32[8,128]{1,0:T(8,128)S(1)}, f32[8,128]{1,0:T(8,128)S(1)}, u32[]{:S(2)}, u32[]{:S(2)}) collective-permute-start(f32[8,128]{1,0:T(8,128)S(1)} %get-tuple-element.40.refs_11_), channel_id=1, source_target_pairs={{0,3},{1,2},{2,1},{3,0},{4,7},{5,6},{6,5},{7,4},{8,11},{9,10},{10,... | collective-permute-start | bytes 12296 | tf_op jit(solution)/shard_map/ppermute | solution.py:337
  27.3 4.5 %collective-permute-start.9 = (f32[8,128]{1,0:T(8,128)S(1)}, f32[8,128]{1,0:T(8,128)S(1)}, u32[]{:S(2)}, u32[]{:S(2)}) collective-permute-start(f32[8,128]{1,0:T(8,128)S(1)} %get-tuple-element.40.refs_11_), channel_id=1, source_target_pairs={{0,2},{1,3},{2,0},{3,1},{4,6},{5,7},{6,4},{7,5},{8,10},{9,11},{10,... | collective-permute-start | bytes 12296 | tf_op jit(solution)/shard_map/ppermute | solution.py:337
  27.3 4.5 %collective-permute-start.8 = (f32[8,128]{1,0:T(8,128)S(1)}, f32[8,128]{1,0:T(8,128)S(1)}, u32[]{:S(2)}, u32[]{:S(2)}) collective-permute-start(f32[8,128]{1,0:T(8,128)S(1)} %get-tuple-element.40.refs_11_), channel_id=1, source_target_pairs={{0,1},{1,0},{2,3},{3,2},{4,5},{5,4},{6,7},{7,6},{8,9},{9,8},{10,11... | collective-permute-start | bytes 12296 | tf_op jit(solution)/shard_map/ppermute | solution.py:337
  33.9 1.3 %collective-permute-start.11 = (f32[4,32,128]{2,1,0:T(8,128)S(1)}, f32[4,32,128]{2,1,0:T(8,128)S(1)}, u32[]{:S(2)}, u32[]{:S(2)}) collective-permute-start(f32[4,32,128]{2,1,0:T(8,128)S(1)} %get-tuple-element.32), channel_id=1, source_target_pairs={{0,4},{4,0},{8,12},{12,8},{16,20},{20,16},{24,28},{28,24},{1,5},{5... | collective-permute-start | bytes 196616 | tf_op jit(solution)/shard_map/ppermute | solution.py:337
  35.2 5.3 %collective-permute-start.14 = (f32[4,32,128]{2,1,0:T(8,128)S(1)}, f32[4,32,128]{2,1,0:T(8,128)S(1)}, u32[]{:S(2)}, u32[]{:S(2)}) collective-permute-start(f32[4,32,128]{2,1,0:T(8,128)S(1)} %add.34), channel_id=1, source_target_pairs={{0,24},{4,28},{8,16},{12,20},{16,8},{20,12},{24,0},{28,4},{1,25},{... | collective-permute-start | bytes 196616 | tf_op jit(solution)/shard_map/ppermute | solution.py:337
  37.7 4.3 %collective-permute-start.13 = (f32[4,32,128]{2,1,0:T(8,128)S(1)}, f32[4,32,128]{2,1,0:T(8,128)S(1)}, u32[]{:S(2)}, u32[]{:S(2)}) collective-permute-start(f32[4,32,128]{2,1,0:T(8,128)S(1)} %add.34), channel_id=1, source_target_pairs={{0,16},{4,20},{8,24},{12,28},{16,0},{20,4},{24,8},{28,12},{1,17},{... | collective-permute-start | bytes 196616 | tf_op jit(solution)/shard_map/ppermute | solution.py:337
  38.2 4.3 %collective-permute-start.12 = (f32[4,32,128]{2,1,0:T(8,128)S(1)}, f32[4,32,128]{2,1,0:T(8,128)S(1)}, u32[]{:S(2)}, u32[]{:S(2)}) collective-permute-start(f32[4,32,128]{2,1,0:T(8,128)S(1)} %add.34), channel_id=1, source_target_pairs={{0,8},{4,12},{8,0},{12,4},{16,24},{20,28},{24,16},{28,20},{1,9},{5... | collective-permute-start | bytes 196616 | tf_op jit(solution)/shard_map/ppermute | solution.py:337
  42.5 1.2 %collective-permute-start.16 = (f32[4,128]{1,0:T(4,128)S(1)}, f32[4,128]{1,0:T(4,128)S(1)}, u32[]{:S(2)}, u32[]{:S(2)}) collective-permute-start(f32[4,128]{1,0:T(4,128)S(1)} %get-tuple-element.37), channel_id=1, source_target_pairs={{0,4},{4,0},{8,12},{12,8},{16,20},{20,16},{24,28},{28,24},{1,5},{5... | collective-permute-start | bytes 6152 | tf_op jit(solution)/shard_map/ppermute | solution.py:337
  42.6 5.5 %collective-permute-start.15 = (bf16[4,32,128]{2,1,0:T(8,128)(2,1)S(1)}, bf16[4,32,128]{2,1,0:T(8,128)(2,1)S(1)}, u32[]{:S(2)}, u32[]{:S(2)}) collective-permute-start(bf16[4,32,128]{2,1,0:T(8,128)(2,1)S(1)} %get-tuple-element.38.refs_7_), channel_id=1, source_target_pairs={{0,4},{4,0},{8,12},{12,8},{16,20},{20,16},{24,28},{28,24},{1,5},{5... | collective-permute-start | bytes 98312 | tf_op jit(solution)/shard_map/ppermute | solution.py:337
  43.8 6.2 %collective-permute-start.19 = (f32[8,128]{1,0:T(8,128)S(1)}, f32[8,128]{1,0:T(8,128)S(1)}, u32[]{:S(2)}, u32[]{:S(2)}) collective-permute-start(f32[8,128]{1,0:T(8,128)S(1)} %pad_maximum_fusion.1.refs_11_), channel_id=1, source_target_pairs={{0,3},{1,2},{2,1},{3,0},{4,7},{5,6},{6,5},{7,4},{8,11},{9,10},{10,... | collective-permute-start | bytes 12296 | tf_op jit(solution)/shard_map/ppermute | solution.py:337
  46.2 4.5 %collective-permute-start.18 = (f32[8,128]{1,0:T(8,128)S(1)}, f32[8,128]{1,0:T(8,128)S(1)}, u32[]{:S(2)}, u32[]{:S(2)}) collective-permute-start(f32[8,128]{1,0:T(8,128)S(1)} %pad_maximum_fusion.1.refs_11_), channel_id=1, source_target_pairs={{0,2},{1,3},{2,0},{3,1},{4,6},{5,7},{6,4},{7,5},{8,10},{9,11},{10,... | collective-permute-start | bytes 12296 | tf_op jit(solution)/shard_map/ppermute | solution.py:337
  46.2 4.5 %collective-permute-start.17 = (f32[8,128]{1,0:T(8,128)S(1)}, f32[8,128]{1,0:T(8,128)S(1)}, u32[]{:S(2)}, u32[]{:S(2)}) collective-permute-start(f32[8,128]{1,0:T(8,128)S(1)} %pad_maximum_fusion.1.refs_11_), channel_id=1, source_target_pairs={{0,1},{1,0},{2,3},{3,2},{4,5},{5,4},{6,7},{7,6},{8,9},{9,8},{10,11... | collective-permute-start | bytes 12296 | tf_op jit(solution)/shard_map/ppermute | solution.py:337

commit v3 on v2

--- a/solution.py
+++ b/solution.py
@@ -17,7 +17,9 @@
 SIGMA = 0.05
 
 B = 128
-UNROLL = 16
+UNROLL = 48
+FIRST, SECOND = (2, 6), (4, 4)
+FIRST_SCN, SECOND_SCN = (1, 3), (2, 2)
 VMEM = pl.BlockSpec(memory_space=pltpu.VMEM)
 HBM = pl.BlockSpec(memory_space=pltpu.HBM)
 F32 = jnp.float32
@@ -155,7 +157,8 @@
     held, refs = refs[9 + pays : 13 + pays], refs[13 + pays :]
     rep, cacc, dacc, scol2, scol3, racc, racc_b = refs
     wait_index = fetch_index(index, held)
-    chip = lax.axis_index("flt") // 2
+    me = lax.axis_index("flt")
+    chip, core = me // 2, lax.rem(me, 2)
     peak = parts[0][0 : 2 * rb]
     for p in parts[1:]:
         peak = jnp.maximum(peak, p[0 : 2 * rb])
@@ -164,11 +167,16 @@
     scale_row2[...] = srow2
     spread_rows(rep, jnp.concatenate([srow1, srow2], axis=0))
     scen = dual.shape[1]
-    per = rb // pays
-    for k, p in enumerate(parts):
-        for i in range(per):
-            at = i if pays == 1 else 2 * (chip ^ k) + i
-            dual[at] = p[2 * rb + scen * i : 2 * rb + scen * (i + 1)]
+    n = 2 * rb
+    if pays == 1:
+        for i in range(rb):
+            dual[i] = parts[0][n + scen * i : n + scen * (i + 1)]
+    else:
+        mine, first, second, other = [p[n:] for p in parts]
+        got = [mine, jnp.where(core == 0, first, other), second, jnp.where(core == 0, other, first)]
+        for k, g in enumerate(got):
+            for i in range(2):
+                dual[2 * (chip ^ k) + i] = g[scen * i : scen * (i + 1)]
     cacc[...] = jnp.zeros_like(cacc)
     dacc[...] = jnp.zeros_like(dacc)
     racc[...] = jnp.zeros_like(racc)
@@ -259,17 +267,10 @@
     )
 
 
-def hold_step(rb, cb, slots, groups, *refs):
-    index, mat, scol, offsets, hold1, lows = refs[:3], refs[3], refs[4], refs[5], refs[6], refs[7 : 7 + groups]
-    hold2, turn = refs[7 + groups : 9 + groups]
-    held, (low, gacc) = refs[9 + groups : 13 + groups], refs[13 + groups :]
-    wait_index = fetch_index(index, held)
-    core = lax.rem(lax.axis_index("flt"), 2)
-    for k in range(groups):
-        for i in range(rb // groups):
-            at = i if groups == 1 else 2 * i + (core if k == 0 else 1 - core)
-            low[at] = lows[k][i]
-    wait_index()
+def hold_step(rb, cb, slots, *refs):
+    index, (mat, scol, offsets, hold1, low), (hold2, turn) = refs[:3], refs[3:8], refs[8:10]
+    held, gacc = refs[10:14], refs[14]
+    fetch_index(index, held)()
     pull(slots, held, mat, low, gacc)
 
     def write(c, scale, hold, double):
@@ -279,7 +280,7 @@
     holds(cb, gacc, offsets, scol, lambda c, scale: hold1[:, c * B : (c + 1) * B], write)
 
 
-def plan_step(rb, cb, slots, scen_all, means, order, split, last, *refs):
+def plan_step(rb, cb, slots, scen_all, means, split, last, *refs):
     index, refs = refs[:3], refs[3:]
     mat, srow4, scol, offsets, capacity, plan, turn, own_dual = refs[:8]
     sums, refs = refs[8 : 8 + means], refs[8 + means :]
@@ -287,14 +288,13 @@
     held, (lhs, gacc, lacc, mixed) = refs[:4], refs[4:]
     wait_index = fetch_index(index, held)
     me = lax.axis_index("flt")
-    core = lax.rem(me, 2)
+    chip, core = me // 2, lax.rem(me, 2)
     total = sums[0][...]
-    for s in sums[1:]:
-        total = total + s[...]
-    half = rb // 2
+    if means > 1:
+        first, second, other = [s[...] for s in sums[1:]]
+        total = (total + jnp.where(core == 0, first, other)) + (second + jnp.where(core == 0, other, first))
     for b in range(rb):
-        at = b if not order else (2 * b + core if b < half else 2 * (b - half) + 1 - core)
-        lhs[at] = three_terms(total[b : b + 1])
+        lhs[b] = three_terms(total[b : b + 1])
     wait_index()
     pull(slots, held, mat, lhs, gacc)
     for c in range(cb):
@@ -316,9 +316,14 @@
     own = srow4[pl.ds(me, 1), :]
     lacc[me] += own_dual[...] * (1.0 / SIGMA) - CAP_UNIT * capacity[...].astype(F32) * own
     if split == 2:
-        for j in range(half):
-            loads[0][j] = lacc[2 * j + core]
-            loads[1][j] = lacc[2 * j + 1 - core]
+        for k, mine in enumerate((core, 1 - core)):
+            via = chip ^ (1 + 2 * mine)
+            if last:
+                picks = (2 * chip + mine, 2 * via, 2 * via + 1, 2 * (chip ^ 2) + mine)
+            else:
+                picks = [2 * j + mine for j in range(rb // 2)]
+            for j, b in enumerate(picks):
+                loads[k][j] = lacc[b]
     else:
         loads[0][...] = lacc[...]
 
@@ -332,17 +337,33 @@
     return terms.astype(BF16)
 
 
-def flip(x, axis, mask):
-    n = lax.axis_size(axis)
-    return lax.ppermute(x, axis, [(i, i ^ mask) for i in range(n)])
+def cross(x, even, odd):
+    pairs = [(i, i ^ (odd if i % 2 else even)) for i in range(lax.axis_size("flt"))]
+    return lax.ppermute(x, "flt", pairs)
+
+
+def cross_scn(x, even, odd):
+    nf, ns = lax.axis_size("flt"), lax.axis_size("scn")
+    pairs = [(f * ns + s, f * ns + (s ^ (odd if f % 2 else even))) for f in range(nf) for s in range(ns)]
+    return lax.ppermute(x, ("flt", "scn"), pairs)
+
+
+def twin(x):
+    return lax.ppermute(x, "flt", [(i, i ^ 1) for i in range(lax.axis_size("flt"))])
+
+
+def interleave(mine, other, core):
+    even, odd = jnp.where(core == 0, mine, other), jnp.where(core == 0, other, mine)
+    return jnp.stack([even, odd], axis=1).reshape((-1,) + mine.shape[1:])
 
 
 def in_hbm(x):
     return pltpu.with_memory_space_constraint(x, pltpu.HBM)
 
 
-def scenario_sums(low):
-    return jnp.sum(low.astype(F32), axis=1)
+def round_low(y):
+    rounded = lax.reduce_precision(y, 8, 7)
+    return rounded.astype(BF16), jnp.sum(rounded, axis=1)
 
 
 def body(tiles, tile_row, tile_col, tile_count, slot_offset, capacity, plan0, hold0, dual0):
@@ -378,11 +399,13 @@
     )(in_hbm(tile_row), in_hbm(tile_col), tile_count, in_hbm(tiles), in_hbm(dual0))
     n = 2 * rb
     if small:
-        other = flip(mine, "flt", 1)
+        other = twin(mine)
         even = jnp.where(core == 0, mine[n:], other[n:])
         odd = jnp.where(core == 0, other[n:], mine[n:])
         mine = jnp.concatenate([jnp.maximum(mine[:n], other[:n]), even, odd], axis=0)
-        parts = [mine] + [flip(mine, "flt", 2 * m) for m in (1, 2, 3)]
+        first, second = cross(mine, *FIRST), cross(mine, *SECOND)
+        best = jnp.maximum(mine[:n], first[:n])
+        parts = [mine, first, second, twin(jnp.concatenate([best, first[n:]], axis=0))]
     else:
         gathered = lax.all_gather(mine[n:], "flt", axis=0, tiled=True)
         parts = [jnp.concatenate([lax.pmax(mine[:n], "flt"), gathered], axis=0)]
@@ -403,16 +426,15 @@
         2 + len(parts),
     )(*index, tiles, scol1, *parts)
     if small:
-        mine = jnp.maximum(peaks, flip(peaks, "flt", 1))
-        far = [flip(mine, "flt", 2 * m) for m in (1, 2, 3)]
-        peak = jnp.maximum(jnp.maximum(mine, far[0]), jnp.maximum(far[1], far[2]))
+        mine = jnp.maximum(peaks, twin(peaks))
+        best, second = jnp.maximum(mine, cross(mine, *FIRST)), cross(mine, *SECOND)
+        peak = jnp.maximum(jnp.maximum(best, second), twin(best))
     else:
         peak = lax.pmax(peaks, "flt")
     srow3 = srow2 / jnp.sqrt(srow2 * peak[:rb] + EPS)
     srow4 = srow3 / jnp.sqrt(srow3 * peak[rb:] + EPS)
     own_row = lax.dynamic_slice_in_dim(srow4, me, 1, 0)
-    low = (dual / srow4[:, None, :]).astype(BF16)
-    sums = scenario_sums(low)
+    low, sums = round_low(dual / srow4[:, None, :])
     own_dual = dual0 / own_row
     gacc = pltpu.VMEM((cb, scen, B), F32)
     mat, scol4, hold1, turn = call(
@@ -437,34 +459,33 @@
     for step in range(2):
         if step:
             if small:
-                half = loads[0] + flip(loads[1], "flt", 1)
-                far = [flip(half, "flt", 2 * m) for m in (1, 2, 3)]
-                y = jnp.maximum(SIGMA * (half + far[0] + far[1] + far[2]), 0.0)
-                low = y.astype(BF16)
-                part = scenario_sums(low)
-                lows = [low, flip(low, "flt", 1)]
-                sums = jnp.concatenate([part, flip(part, "flt", 1)], axis=0)
+                half = loads[0] + twin(loads[1])
+                far = [cross(half, m, m) for m in (2, 4, 6)]
+                y = jnp.maximum(SIGMA * ((half + far[0]) + (far[1] + far[2])), 0.0)
+                low, sums = round_low(y)
+                low, sums = interleave(low, twin(low), core), interleave(sums, twin(sums), core)
                 own_dual = lax.dynamic_index_in_dim(y, chip, 0, False)
             else:
                 y = jnp.maximum(SIGMA * lax.psum(loads[0], "flt"), 0.0)
-                lows = [y.astype(BF16)]
-                sums = scenario_sums(lows[0])
+                low, sums = round_low(y)
                 own_dual = lax.dynamic_index_in_dim(y, me, 0, False)
             hold, turn = call(
-                functools.partial(hold_step, rb, cb, slots, len(lows)),
+                functools.partial(hold_step, rb, cb, slots),
                 [f32((scen, cb * B)), f32((scen, cb * B))],
-                held + [pltpu.VMEM((rb, scen, B), BF16), gacc],
+                held + [gacc],
                 3,
-                4 + len(lows),
-            )(*index, mat, scol4, offsets, hold1, *lows)
+                5,
+            )(*index, mat, scol4, offsets, hold1, low)
         if small:
-            totals = [sums] + [flip(sums, "scn", m) for m in (1, 2, 3)]
+            first, second = cross_scn(sums, *FIRST_SCN), cross_scn(sums, *SECOND_SCN)
+            first, second, turn = lax.optimization_barrier((first, second, turn))
+            totals = [sums, first, second, twin(first)]
         else:
             totals = [lax.psum(sums, "scn")]
-        split = 2 if small and not step else 1
+        split = 2 if small else 1
         plan, *loads = call(
             functools.partial(
-                plan_step, rb, cb, slots, scen_all, len(totals), small and step == 1, split, step == 1
+                plan_step, rb, cb, slots, scen_all, len(totals), split, step == 1
             ),
             [f32((cb, B))] + [f32((rb // split, scen, B))] * split,
             held
@@ -477,7 +498,13 @@
             3,
             8 + len(totals),
         )(*index, mat, srow4, scol4, offsets, capacity, plan, turn, own_dual, *totals)
-    total = jnp.sum(lax.all_to_all(loads[0], "flt", 0, 0), axis=0)
+    if small:
+        chip_sum = loads[0] + twin(loads[1])
+        first, second = cross(chip_sum[1:3], *FIRST), cross(chip_sum[3], *SECOND)
+        own, other = [lax.dynamic_index_in_dim(first, i, 0, False) for i in (core, 1 - core)]
+        total = (chip_sum[0] + own) + (second + twin(other))
+    else:
+        total = lax.psum_scatter(loads[0], "flt", scatter_dimension=0, tiled=False)
     dual = jnp.maximum(SIGMA * total, 0.0) * own_row
     return plan.reshape(-1), hold, dual
 

time: 62.2 us -> 57.5 us (0.924)
  blocking collectives: 8.13 us -> 0 us
  waiting for transfers between devices: 15.3 us -> 18.7 us
    all_to_all x1 -> x0, blocking collectives: 8.13 us -> none  [body(): total = jnp.sum(lax.all_to_all(loads[0], 'flt', 0, 0), axis=0)]
    ppermute x20 -> x24, waiting for transfers between devices: 15.3 us -> 18.7 us  [the longest x9 10.9 us: cross(): return lax.ppermute(x, 'flt', pairs)]
    ppermute x20 -> x24, starting transfers between devices: 21.8 us -> 22 us  [the longest x9 12.6 us: cross(): return lax.ppermute(x, 'flt', pairs)]
  transfers between devices with their start and end apart: 20 -> 24, of which waited for: 15 -> 18; matrix products, arithmetic and copies ran while one was open for 0% -> 0% of each run, Pallas kernels for 7% -> 7%
where the time goes in v3:
time: 57.5 us; the launch traced here: 57.3 us
  starting transfers between devices  22 us (38%)
  waiting for transfers between devices  18.7 us (33%)
  Pallas kernels  14 us (24%)
  between operations  1.66 us (3%)
  other arithmetic  0.82 us (1%)
    ppermute x9, starting transfers between devices, cross(): return lax.ppermute(x, 'flt', pairs)  12.6 us
    ppermute x9, waiting for transfers between devices, cross(): return lax.ppermute(x, 'flt', pairs)  10.9 us
    ppermute x11, waiting for transfers between devices, twin(): lax.ppermute(x, 'flt', [(i, i ^ 1) for i in range(lax.axis_size('flt'))])  7.4 us
    ppermute x4, starting transfers between devices, cross_scn(): return lax.ppermute(x, ('flt', 'scn'), pairs)  6.47 us
    pallas_call x2, Pallas kernels, body(): call(functools.partial(plan_step, rb, cb, slots, scen_all, len(totals), s...  4.58 us
    ppermute x11, starting transfers between devices, twin(): lax.ppermute(x, 'flt', [(i, i ^ 1) for i in range(lax.axis_size('flt'))])  2.98 us
    pallas_call x1, Pallas kernels, body(): call(functools.partial(second_peaks, rb, cb, slots, len(parts)), [f32((2...  2.89 us
    pallas_call x1, Pallas kernels, body(): call(functools.partial(first_peaks, rb, cb, slots, chunk), [f32((2 * rb +...  2.5 us
  transfers between devices with their start and end apart: 24, of which 18 were waited for; matrix products, arithmetic and copies ran while one was open for 0% of the time, Pallas kernels for 7%

profile of v3, /device:TPU:0, one launch (start us, length us, event | category | flops | bytes accessed | tf_op | source)
XLA Modules:
  0.0 57.3 jit_solution(12107936585303526159)
XLA Ops:
  1.4 2.5 %shard_map.112 = (f32[48,128]{1,0:T(8,128)S(1)}, f32[9,128]{1,0:T(8,128)S(1)}) custom-call(s32[48]{0:T(128)} %refs_0_.11, s32[48]{0:T(128)} %refs_1_.11, s32[1]{0:T(128)S(6)} %copy.14.refs_2_, bf16[48,128,128]{2,1,0:T(8,128)(2,1)} %refs_3_.5, f32[32,128]{1,0:T(8,128)} %refs_4_.1), custom_call_target="tpu_custom_call" | custom-call | tf_op jit(solution)/shard_map/pallas_call | solution.py:385
  4.5 0.8 %collective-permute-done = f32[48,128]{1,0:T(8,128)S(1)} collective-permute-done((f32[48,128]{1,0:T(8,128)S(1)}, f32[48,128]{1,0:T(8,128)S(1)}, u32[]{:S(2)}, u32[]{:S(2)}) %collective-permute-start) | collective-permute-done | bytes 24608 | tf_op jit(solution)/shard_map/ppermute | solution.py:352
  5.4 2.9 %collective-permute-start.1 = (f32[80,128]{1,0:T(8,128)S(1)}, f32[80,128]{1,0:T(8,128)S(1)}, u32[]{:S(2)}, u32[]{:S(2)}) collective-permute-start(f32[80,128]{1,0:T(8,128)S(1)} %pad_maximum_fusion.1.refs_5_), channel_id=1, source_target_pairs={{0,8},{4,28},{8,0},{12,20},{16,24},{20,12},{24,16},{28,4},{1,9},{5... | collective-permute-start | bytes 122888 | tf_op jit(solution)/shard_map/ppermute | solution.py:342
  8.2 1.5 %collective-permute-start.2 = (f32[80,128]{1,0:T(8,128)S(1)}, f32[80,128]{1,0:T(8,128)S(1)}, u32[]{:S(2)}, u32[]{:S(2)}) collective-permute-start(f32[80,128]{1,0:T(8,128)S(1)} %pad_maximum_fusion.1.refs_5_), channel_id=1, source_target_pairs={{0,16},{4,20},{8,24},{12,28},{16,0},{20,4},{24,8},{28,12},{1,17},{... | collective-permute-start | bytes 122888 | tf_op jit(solution)/shard_map/ppermute | solution.py:342
  10.6 2.0 %collective-permute-done.2.refs_7_ = f32[80,128]{1,0:T(8,128)S(1)} collective-permute-done((f32[80,128]{1,0:T(8,128)S(1)}, f32[80,128]{1,0:T(8,128)S(1)}, u32[]{:S(2)}, u32[]{:S(2)}) %collective-permute-start.2) | collective-permute-done | bytes 40992 | tf_op jit(solution)/shard_map/ppermute | solution.py:342
  12.6 2.9 %shard_map.113 = (f32[16,128]{1,0:T(8,128)S(1)}, f32[8,128]{1,0:T(8,128)S(1)}, f32[8,128]{1,0:T(8,128)S(1)}, f32[8,32,128]{2,1,0:T(8,128)S(1)}) custom-call(s32[48]{0:T(128)S(1)} %copy-done.4, s32[48]{0:T(128)S(1)} %copy-done.5, s32[1]{0:T(128)S(6)} %copy.14.refs_2_, bf16[48,128,128]{2,1,0:T(8,128)(2,1)S(1)} %copy-done, ...), custom_call_target="tpu_custom_call" | custom-call | tf_op jit(solution)/shard_map/pallas_call | solution.py:412
  15.6 1.2 %collective-permute-done.4 = f32[16,128]{1,0:T(8,128)S(1)} collective-permute-done((f32[16,128]{1,0:T(8,128)S(1)}, f32[16,128]{1,0:T(8,128)S(1)}, u32[]{:S(2)}, u32[]{:S(2)}) %collective-permute-start.4) | collective-permute-done | bytes 8224 | tf_op jit(solution)/shard_map/ppermute | solution.py:352
  16.8 1.3 %collective-permute-start.5 = (f32[16,128]{1,0:T(8,128)S(1)}, f32[16,128]{1,0:T(8,128)S(1)}, u32[]{:S(2)}, u32[]{:S(2)}) collective-permute-start(f32[16,128]{1,0:T(8,128)S(1)} %max.32), channel_id=1, source_target_pairs={{0,8},{4,28},{8,0},{12,20},{16,24},{20,12},{24,16},{28,4},{1,9},{5... | collective-permute-start | bytes 24584 | tf_op jit(solution)/shard_map/ppermute | solution.py:342
  18.0 1.2 %collective-permute-start.6 = (f32[16,128]{1,0:T(8,128)S(1)}, f32[16,128]{1,0:T(8,128)S(1)}, u32[]{:S(2)}, u32[]{:S(2)}) collective-permute-start(f32[16,128]{1,0:T(8,128)S(1)} %max.32), channel_id=1, source_target_pairs={{0,16},{4,20},{8,24},{12,28},{16,0},{20,4},{24,8},{28,12},{1,17},{... | collective-permute-start | bytes 24584 | tf_op jit(solution)/shard_map/ppermute | solution.py:342
  19.3 1.2 %collective-permute-done.5 = f32[16,128]{1,0:T(8,128)S(1)} collective-permute-done((f32[16,128]{1,0:T(8,128)S(1)}, f32[16,128]{1,0:T(8,128)S(1)}, u32[]{:S(2)}, u32[]{:S(2)}) %collective-permute-start.5) | collective-permute-done | bytes 8224 | tf_op jit(solution)/shard_map/ppermute | solution.py:342
  20.4 1.3 %collective-permute-done.6 = f32[16,128]{1,0:T(8,128)S(1)} collective-permute-done((f32[16,128]{1,0:T(8,128)S(1)}, f32[16,128]{1,0:T(8,128)S(1)}, u32[]{:S(2)}, u32[]{:S(2)}) %collective-permute-start.6) | collective-permute-done | bytes 8224 | tf_op jit(solution)/shard_map/ppermute | solution.py:342
  21.7 2.7 %collective-permute-start.9 = (f32[8,128]{1,0:T(8,128)S(1)}, f32[8,128]{1,0:T(8,128)S(1)}, u32[]{:S(2)}, u32[]{:S(2)}) collective-permute-start(f32[8,128]{1,0:T(8,128)S(1)} %get-tuple-element.55.refs_11_), channel_id=1, source_target_pairs={{0,2},{1,3},{2,0},{3,1},{4,6},{5,7},{6,4},{7,5},{8,10},{9,11},{10,... | collective-permute-start | bytes 12296 | tf_op jit(solution)/shard_map/ppermute | solution.py:348
  24.4 1.6 %collective-permute-start.8 = (f32[8,128]{1,0:T(8,128)S(1)}, f32[8,128]{1,0:T(8,128)S(1)}, u32[]{:S(2)}, u32[]{:S(2)}) collective-permute-start(f32[8,128]{1,0:T(8,128)S(1)} %get-tuple-element.55.refs_11_), channel_id=1, source_target_pairs={{0,1},{1,0},{2,3},{3,2},{4,7},{5,6},{6,5},{7,4},{8,9},{9,8},{10,11... | collective-permute-start | bytes 12296 | tf_op jit(solution)/shard_map/ppermute | solution.py:348
  26.0 2.2 %shard_map.114 = (bf16[48,128,128]{2,1,0:T(8,128)(2,1)S(1)}, f32[8,128]{1,0:T(8,128)S(1)}, f32[32,1024]{1,0:T(8,128)S(1)}, f32[32,1024]{1,0:T(8,128)S(1)}) custom-call(s32[48]{0:T(128)S(1)} %copy-done.4, s32[48]{0:T(128)S(1)} %copy-done.5, s32[1]{0:T(128)S(6)} %copy.14.refs_2_, bf16[48,128,128]{2,1,0:T(8,128)(2,1)S(1)} %copy-done, ...), custom_call_target="tpu_custom_call" | custom-call | tf_op jit(solution)/shard_map/pallas_call | solution.py:440
  28.5 1.0 %collective-permute-done.10.refs_14_ = f32[8,128]{1,0:T(8,128)S(1)} collective-permute-done((f32[8,128]{1,0:T(8,128)S(1)}, f32[8,128]{1,0:T(8,128)S(1)}, u32[]{:S(2)}, u32[]{:S(2)}) %collective-permute-start.10) | collective-permute-done | bytes 4128 | tf_op jit(solution)/shard_map/ppermute | solution.py:352
  29.5 2.1 %shard_map.115 = (f32[8,128]{1,0:T(8,128)S(1)}, f32[4,32,128]{2,1,0:T(8,128)S(1)}, f32[4,32,128]{2,1,0:T(8,128)S(1)}) custom-call(s32[48]{0:T(128)S(1)} %copy-done.4, s32[48]{0:T(128)S(1)} %copy-done.5, s32[1]{0:T(128)S(6)} %copy.14.refs_2_, bf16[48,128,128]{2,1,0:T(8,128)(2,1)S(1)} %get-tuple-element.33.refs_3_, ...), custom_call_target="tpu_custom_call" | custom-call | tf_op jit(solution)/shard_map/pallas_call | solution.py:486
  31.8 1.1 %collective-permute-done.11 = f32[4,32,128]{2,1,0:T(8,128)S(1)} collective-permute-done((f32[4,32,128]{2,1,0:T(8,128)S(1)}, f32[4,32,128]{2,1,0:T(8,128)S(1)}, u32[]{:S(2)}, u32[]{:S(2)}) %collective-permute-start.11) | collective-permute-done | bytes 65568 | tf_op jit(solution)/shard_map/ppermute | solution.py:352
  32.9 1.9 %collective-permute-start.14 = (f32[4,32,128]{2,1,0:T(8,128)S(1)}, f32[4,32,128]{2,1,0:T(8,128)S(1)}, u32[]{:S(2)}, u32[]{:S(2)}) collective-permute-start(f32[4,32,128]{2,1,0:T(8,128)S(1)} %add.57), channel_id=1, source_target_pairs={{0,24},{4,28},{8,16},{12,20},{16,8},{20,12},{24,0},{28,4},{1,25},{... | collective-permute-start | bytes 196616 | tf_op jit(solution)/shard_map/ppermute | solution.py:342
  34.8 0.9 %collective-permute-start.13 = (f32[4,32,128]{2,1,0:T(8,128)S(1)}, f32[4,32,128]{2,1,0:T(8,128)S(1)}, u32[]{:S(2)}, u32[]{:S(2)}) collective-permute-start(f32[4,32,128]{2,1,0:T(8,128)S(1)} %add.57), channel_id=1, source_target_pairs={{0,16},{4,20},{8,24},{12,28},{16,0},{20,4},{24,8},{28,12},{1,17},{... | collective-permute-start | bytes 196616 | tf_op jit(solution)/shard_map/ppermute | solution.py:342
  35.7 0.8 %collective-permute-start.12 = (f32[4,32,128]{2,1,0:T(8,128)S(1)}, f32[4,32,128]{2,1,0:T(8,128)S(1)}, u32[]{:S(2)}, u32[]{:S(2)}) collective-permute-start(f32[4,32,128]{2,1,0:T(8,128)S(1)} %add.57), channel_id=1, source_target_pairs={{0,8},{4,12},{8,0},{12,4},{16,24},{20,28},{24,16},{28,20},{1,9},{5... | collective-permute-start | bytes 196616 | tf_op jit(solution)/shard_map/ppermute | solution.py:342
  36.5 1.8 %collective-permute-done.14 = f32[4,32,128]{2,1,0:T(8,128)S(1)} collective-permute-done((f32[4,32,128]{2,1,0:T(8,128)S(1)}, f32[4,32,128]{2,1,0:T(8,128)S(1)}, u32[]{:S(2)}, u32[]{:S(2)}) %collective-permute-start.14) | collective-permute-done | bytes 65568 | tf_op jit(solution)/shard_map/ppermute | solution.py:342
  38.2 1.2 %collective-permute-done.13 = f32[4,32,128]{2,1,0:T(8,128)S(1)} collective-permute-done((f32[4,32,128]{2,1,0:T(8,128)S(1)}, f32[4,32,128]{2,1,0:T(8,128)S(1)}, u32[]{:S(2)}, u32[]{:S(2)}) %collective-permute-start.13) | collective-permute-done | bytes 65568 | tf_op jit(solution)/shard_map/ppermute | solution.py:342
  41.2 0.8 %collective-permute-start.17 = (f32[8,128]{1,0:T(8,128)S(1)}, f32[8,128]{1,0:T(8,128)S(1)}, u32[]{:S(2)}, u32[]{:S(2)}) collective-permute-start(f32[8,128]{1,0:T(8,128)S(1)} %bitcast.36), channel_id=1, source_target_pairs={{0,2},{1,3},{2,0},{3,1},{4,6},{5,7},{6,4},{7,5},{8,10},{9,11},{10,... | collective-permute-start | bytes 12296 | tf_op jit(solution)/shard_map/ppermute | solution.py:348
  42.0 1.5 %collective-permute-start.16 = (f32[8,128]{1,0:T(8,128)S(1)}, f32[8,128]{1,0:T(8,128)S(1)}, u32[]{:S(2)}, u32[]{:S(2)}) collective-permute-start(f32[8,128]{1,0:T(8,128)S(1)} %bitcast.37), channel_id=1, source_target_pairs={{0,1},{1,0},{2,3},{3,2},{4,7},{5,6},{6,5},{7,4},{8,9},{9,8},{10,11... | collective-permute-start | bytes 12296 | tf_op jit(solution)/shard_map/ppermute | solution.py:348
  43.5 1.8 %shard_map.116 = (f32[32,1024]{1,0:T(8,128)}, f32[32,1024]{1,0:T(8,128)S(1)}) custom-call(s32[48]{0:T(128)S(1)} %copy-done.4, s32[48]{0:T(128)S(1)} %copy-done.5, s32[1]{0:T(128)S(6)} %copy.14.refs_2_, bf16[48,128,128]{2,1,0:T(8,128)(2,1)S(1)} %get-tuple-element.33.refs_3_, f32[8,128]{1,0:T(8,128)S(1)} %get-tuple-element.34.refs_5_.refs_4_, ...), custom_call_target="tpu_custom_call" | custom-call | tf_op jit(solution)/shard_map/pallas_call | solution.py:472
  46.5 0.8 %collective-permute-done.19.refs_14_ = f32[8,128]{1,0:T(8,128)S(1)} collective-permute-done((f32[8,128]{1,0:T(8,128)S(1)}, f32[8,128]{1,0:T(8,128)S(1)}, u32[]{:S(2)}, u32[]{:S(2)}) %collective-permute-start.19) | collective-permute-done | bytes 4128 | tf_op jit(solution)/shard_map/ppermute | solution.py:352
  47.3 2.5 %shard_map.117 = (f32[8,128]{1,0:T(8,128)}, f32[4,32,128]{2,1,0:T(8,128)S(1)}, f32[4,32,128]{2,1,0:T(8,128)S(1)}) custom-call(s32[48]{0:T(128)S(1)} %copy-done.4, s32[48]{0:T(128)S(1)} %copy-done.5, s32[1]{0:T(128)S(6)} %copy.14.refs_2_, bf16[48,128,128]{2,1,0:T(8,128)(2,1)S(1)} %get-tuple-element.33.refs_3_, ...), custom_call_target="tpu_custom_call" | custom-call | tf_op jit(solution)/shard_map/pallas_call | solution.py:486
  50.2 0.9 %collective-permute-done.20 = f32[4,32,128]{2,1,0:T(8,128)S(1)} collective-permute-done((f32[4,32,128]{2,1,0:T(8,128)S(1)}, f32[4,32,128]{2,1,0:T(8,128)S(1)}, u32[]{:S(2)}, u32[]{:S(2)}) %collective-permute-start.20) | collective-permute-done | bytes 65568 | tf_op jit(solution)/shard_map/ppermute | solution.py:352
  51.2 0.9 %collective-permute-start.21 = (f32[2,32,128]{2,1,0:T(8,128)S(1)}, f32[2,32,128]{2,1,0:T(8,128)S(1)}, u32[]{:S(2)}, u32[]{:S(2)}) collective-permute-start(f32[2,32,128]{2,1,0:T(8,128)S(1)} %slice.53), channel_id=1, source_target_pairs={{0,8},{4,28},{8,0},{12,20},{16,24},{20,12},{24,16},{28,4},{1,9},{5... | collective-permute-start | bytes 98312 | tf_op jit(solution)/shard_map/ppermute | solution.py:342
  52.0 1.2 %collective-permute-start.22 = (f32[32,128]{1,0:T(8,128)S(1)}, f32[32,128]{1,0:T(8,128)S(1)}, u32[]{:S(2)}, u32[]{:S(2)}) collective-permute-start(f32[32,128]{1,0:T(8,128)S(1)} %slice_bitcast_fusion), channel_id=1, source_target_pairs={{0,16},{4,20},{8,24},{12,28},{16,0},{20,4},{24,8},{28,12},{1,17},{... | collective-permute-start | bytes 49160 | tf_op jit(solution)/shard_map/ppermute | solution.py:342
  53.3 2.2 %collective-permute-done.21 = f32[2,32,128]{2,1,0:T(8,128)S(1)} collective-permute-done((f32[2,32,128]{2,1,0:T(8,128)S(1)}, f32[2,32,128]{2,1,0:T(8,128)S(1)}, u32[]{:S(2)}, u32[]{:S(2)}) %collective-permute-start.21) | collective-permute-done | bytes 32800 | tf_op jit(solution)/shard_map/ppermute | solution.py:342
  55.8 0.9 %collective-permute-done.23 = f32[32,128]{1,0:T(8,128)S(1)} collective-permute-done((f32[32,128]{1,0:T(8,128)S(1)}, f32[32,128]{1,0:T(8,128)S(1)}, u32[]{:S(2)}, u32[]{:S(2)}) %collective-permute-start.23) | collective-permute-done | bytes 16416 | tf_op jit(solution)/shard_map/ppermute | solution.py:352
  (65 shorter events, 6.2 us)
Async XLA Ops:
  0.6 11.9 %copy-start.5 = (s32[48]{0:T(128)S(1)}, s32[48]{0:T(128)}, u32[]{:S(2)}) copy-start(s32[48]{0:T(128)} %refs_1_.11) | copy-start | bytes 580
  0.6 11.9 %copy-start.4 = (s32[48]{0:T(128)S(1)}, s32[48]{0:T(128)}, u32[]{:S(2)}) copy-start(s32[48]{0:T(128)} %refs_0_.11) | copy-start | bytes 580
  0.7 11.9 %copy-start = (bf16[48,128,128]{2,1,0:T(8,128)(2,1)S(1)}, bf16[48,128,128]{2,1,0:T(8,128)(2,1)}, u32[]{:S(2)}) copy-start(bf16[48,128,128]{2,1,0:T(8,128)(2,1)} %refs_3_.5) | copy-start | bytes 4718596
  3.9 22.0 %copy-start.1 = (f32[32,1024]{1,0:T(8,128)S(1)}, f32[32,1024]{1,0:T(8,128)}, u32[]{:S(2)}) copy-start(f32[32,1024]{1,0:T(8,128)} %refs_9_.1) | copy-start | bytes 393220
  3.9 22.0 %copy-start.3 = (s32[1024]{0:T(1024)S(1)}, s32[1024]{0:T(1024)}, u32[]{:S(2)}) copy-start(s32[1024]{0:T(1024)} %param.13) | copy-start | bytes 12292
  4.0 1.4 %collective-permute-start = (f32[48,128]{1,0:T(8,128)S(1)}, f32[48,128]{1,0:T(8,128)S(1)}, u32[]{:S(2)}, u32[]{:S(2)}) collective-permute-start(f32[48,128]{1,0:T(8,128)S(1)} %get-tuple-element.28), channel_id=1, source_target_pairs={{0,4},{4,0},{8,12},{12,8},{16,20},{20,16},{24,28},{28,24},{1,5},{5... | collective-permute-start | bytes 73736 | tf_op jit(solution)/shard_map/ppermute | solution.py:352
  5.4 4.9 %collective-permute-start.1 = (f32[80,128]{1,0:T(8,128)S(1)}, f32[80,128]{1,0:T(8,128)S(1)}, u32[]{:S(2)}, u32[]{:S(2)}) collective-permute-start(f32[80,128]{1,0:T(8,128)S(1)} %pad_maximum_fusion.1.refs_5_), channel_id=1, source_target_pairs={{0,8},{4,28},{8,0},{12,20},{16,24},{20,12},{24,16},{28,4},{1,9},{5... | collective-permute-start | bytes 122888 | tf_op jit(solution)/shard_map/ppermute | solution.py:342
  8.2 4.3 %collective-permute-start.2 = (f32[80,128]{1,0:T(8,128)S(1)}, f32[80,128]{1,0:T(8,128)S(1)}, u32[]{:S(2)}, u32[]{:S(2)}) collective-permute-start(f32[80,128]{1,0:T(8,128)S(1)} %pad_maximum_fusion.1.refs_5_), channel_id=1, source_target_pairs={{0,16},{4,20},{8,24},{12,28},{16,0},{20,4},{24,8},{28,12},{1,17},{... | collective-permute-start | bytes 122888 | tf_op jit(solution)/shard_map/ppermute | solution.py:342
  10.2 2.3 %collective-permute-start.3 = (f32[80,128]{1,0:T(8,128)S(1)}, f32[80,128]{1,0:T(8,128)S(1)}, u32[]{:S(2)}, u32[]{:S(2)}) collective-permute-start(f32[80,128]{1,0:T(8,128)S(1)} %pad_maximum_fusion.2), channel_id=1, source_target_pairs={{0,4},{4,0},{8,12},{12,8},{16,20},{20,16},{24,28},{28,24},{1,5},{5... | collective-permute-start | bytes 122888 | tf_op jit(solution)/shard_map/ppermute | solution.py:352
  12.6 15.9 %copy-start.7 = (f32[32,128]{1,0:T(8,128)S(1)}, f32[32,128]{1,0:T(8,128)}, u32[]{:S(2)}) copy-start(f32[32,128]{1,0:T(8,128)} %refs_4_.1) | copy-start | bytes 49156
  12.6 16.9 %copy-start.2 = (s32[32,128]{1,0:T(8,128)S(1)}, s32[32,128]{1,0:T(8,128)}, u32[]{:S(2)}) copy-start(s32[32,128]{1,0:T(8,128)} %refs_7_.3) | copy-start | bytes 49156
  12.6 16.9 %copy-start.6 = (f32[1024]{0:T(1024)S(1)}, f32[1024]{0:T(1024)}, u32[]{:S(2)}) copy-start(f32[1024]{0:T(1024)} %param.15) | copy-start | bytes 12292
  15.5 1.2 %collective-permute-start.4 = (f32[16,128]{1,0:T(8,128)S(1)}, f32[16,128]{1,0:T(8,128)S(1)}, u32[]{:S(2)}, u32[]{:S(2)}) collective-permute-start(f32[16,128]{1,0:T(8,128)S(1)} %get-tuple-element.30), channel_id=1, source_target_pairs={{0,4},{4,0},{8,12},{12,8},{16,20},{20,16},{24,28},{28,24},{1,5},{5... | collective-permute-start | bytes 24584 | tf_op jit(solution)/shard_map/ppermute | solution.py:352
  16.8 3.7 %collective-permute-start.5 = (f32[16,128]{1,0:T(8,128)S(1)}, f32[16,128]{1,0:T(8,128)S(1)}, u32[]{:S(2)}, u32[]{:S(2)}) collective-permute-start(f32[16,128]{1,0:T(8,128)S(1)} %max.32), channel_id=1, source_target_pairs={{0,8},{4,28},{8,0},{12,20},{16,24},{20,12},{24,16},{28,4},{1,9},{5... | collective-permute-start | bytes 24584 | tf_op jit(solution)/shard_map/ppermute | solution.py:342
  18.0 3.7 %collective-permute-start.6 = (f32[16,128]{1,0:T(8,128)S(1)}, f32[16,128]{1,0:T(8,128)S(1)}, u32[]{:S(2)}, u32[]{:S(2)}) collective-permute-start(f32[16,128]{1,0:T(8,128)S(1)} %max.32), channel_id=1, source_target_pairs={{0,16},{4,20},{8,24},{12,28},{16,0},{20,4},{24,8},{28,12},{1,17},{... | collective-permute-start | bytes 24584 | tf_op jit(solution)/shard_map/ppermute | solution.py:342
  20.4 1.3 %collective-permute-start.7 = (f32[16,128]{1,0:T(8,128)S(1)}, f32[16,128]{1,0:T(8,128)S(1)}, u32[]{:S(2)}, u32[]{:S(2)}) collective-permute-start(f32[16,128]{1,0:T(8,128)S(1)} %max.33), channel_id=1, source_target_pairs={{0,4},{4,0},{8,12},{12,8},{16,20},{20,16},{24,28},{28,24},{1,5},{5... | collective-permute-start | bytes 24584 | tf_op jit(solution)/shard_map/ppermute | solution.py:352
  21.7 6.5 %collective-permute-start.9 = (f32[8,128]{1,0:T(8,128)S(1)}, f32[8,128]{1,0:T(8,128)S(1)}, u32[]{:S(2)}, u32[]{:S(2)}) collective-permute-start(f32[8,128]{1,0:T(8,128)S(1)} %get-tuple-element.55.refs_11_), channel_id=1, source_target_pairs={{0,2},{1,3},{2,0},{3,1},{4,6},{5,7},{6,4},{7,5},{8,10},{9,11},{10,... | collective-permute-start | bytes 12296 | tf_op jit(solution)/shard_map/ppermute | solution.py:348
  24.4 3.8 %collective-permute-start.8 = (f32[8,128]{1,0:T(8,128)S(1)}, f32[8,128]{1,0:T(8,128)S(1)}, u32[]{:S(2)}, u32[]{:S(2)}) collective-permute-start(f32[8,128]{1,0:T(8,128)S(1)} %get-tuple-element.55.refs_11_), channel_id=1, source_target_pairs={{0,1},{1,0},{2,3},{3,2},{4,7},{5,6},{6,5},{7,4},{8,9},{9,8},{10,11... | collective-permute-start | bytes 12296 | tf_op jit(solution)/shard_map/ppermute | solution.py:348
  28.2 1.2 %collective-permute-start.10 = (f32[8,128]{1,0:T(8,128)S(1)}, f32[8,128]{1,0:T(8,128)S(1)}, u32[]{:S(2)}, u32[]{:S(2)}) collective-permute-start(f32[8,128]{1,0:T(8,128)S(1)} %collective-permute-done.8.refs_12_), channel_id=1, source_target_pairs={{0,4},{4,0},{8,12},{12,8},{16,20},{20,16},{24,28},{28,24},{1,5},{5... | collective-permute-start | bytes 12296 | tf_op jit(solution)/shard_map/ppermute | solution.py:352
  31.6 1.3 %collective-permute-start.11 = (f32[4,32,128]{2,1,0:T(8,128)S(1)}, f32[4,32,128]{2,1,0:T(8,128)S(1)}, u32[]{:S(2)}, u32[]{:S(2)}) collective-permute-start(f32[4,32,128]{2,1,0:T(8,128)S(1)} %get-tuple-element.41), channel_id=1, source_target_pairs={{0,4},{4,0},{8,12},{12,8},{16,20},{20,16},{24,28},{28,24},{1,5},{5... | collective-permute-start | bytes 196616 | tf_op jit(solution)/shard_map/ppermute | solution.py:352
  32.9 5.3 %collective-permute-start.14 = (f32[4,32,128]{2,1,0:T(8,128)S(1)}, f32[4,32,128]{2,1,0:T(8,128)S(1)}, u32[]{:S(2)}, u32[]{:S(2)}) collective-permute-start(f32[4,32,128]{2,1,0:T(8,128)S(1)} %add.57), channel_id=1, source_target_pairs={{0,24},{4,28},{8,16},{12,20},{16,8},{20,12},{24,0},{28,4},{1,25},{... | collective-permute-start | bytes 196616 | tf_op jit(solution)/shard_map/ppermute | solution.py:342
  34.8 4.7 %collective-permute-start.13 = (f32[4,32,128]{2,1,0:T(8,128)S(1)}, f32[4,32,128]{2,1,0:T(8,128)S(1)}, u32[]{:S(2)}, u32[]{:S(2)}) collective-permute-start(f32[4,32,128]{2,1,0:T(8,128)S(1)} %add.57), channel_id=1, source_target_pairs={{0,16},{4,20},{8,24},{12,28},{16,0},{20,4},{24,8},{28,12},{1,17},{... | collective-permute-start | bytes 196616 | tf_op jit(solution)/shard_map/ppermute | solution.py:342
  35.7 4.3 %collective-permute-start.12 = (f32[4,32,128]{2,1,0:T(8,128)S(1)}, f32[4,32,128]{2,1,0:T(8,128)S(1)}, u32[]{:S(2)}, u32[]{:S(2)}) collective-permute-start(f32[4,32,128]{2,1,0:T(8,128)S(1)} %add.57), channel_id=1, source_target_pairs={{0,8},{4,12},{8,0},{12,4},{16,24},{20,28},{24,16},{28,20},{1,9},{5... | collective-permute-start | bytes 196616 | tf_op jit(solution)/shard_map/ppermute | solution.py:342
  40.0 1.2 %collective-permute-start.15 = (f32[4,128]{1,0:T(4,128)S(1)}, f32[4,128]{1,0:T(4,128)S(1)}, u32[]{:S(2)}, u32[]{:S(2)}) collective-permute-start(f32[4,128]{1,0:T(4,128)S(1)} %reduce-precision_reduce_fusion), channel_id=1, source_target_pairs={{0,4},{4,0},{8,12},{12,8},{16,20},{20,16},{24,28},{28,24},{1,5},{5... | collective-permute-start | bytes 6152 | tf_op jit(solution)/shard_map/ppermute | solution.py:352
  40.1 3.4 %collective-permute-start.18 = (bf16[4,32,128]{2,1,0:T(8,128)(2,1)S(1)}, bf16[4,32,128]{2,1,0:T(8,128)(2,1)S(1)}, u32[]{:S(2)}, u32[]{:S(2)}) collective-permute-start(bf16[4,32,128]{2,1,0:T(8,128)(2,1)S(1)} %get-tuple-element.51), channel_id=1, source_target_pairs={{0,4},{4,0},{8,12},{12,8},{16,20},{20,16},{24,28},{28,24},{1,5},{5... | collective-permute-start | bytes 98312 | tf_op jit(solution)/shard_map/ppermute | solution.py:352
  41.2 4.6 %collective-permute-start.17 = (f32[8,128]{1,0:T(8,128)S(1)}, f32[8,128]{1,0:T(8,128)S(1)}, u32[]{:S(2)}, u32[]{:S(2)}) collective-permute-start(f32[8,128]{1,0:T(8,128)S(1)} %bitcast.36), channel_id=1, source_target_pairs={{0,2},{1,3},{2,0},{3,1},{4,6},{5,7},{6,4},{7,5},{8,10},{9,11},{10,... | collective-permute-start | bytes 12296 | tf_op jit(solution)/shard_map/ppermute | solution.py:348
  42.0 3.8 %collective-permute-start.16 = (f32[8,128]{1,0:T(8,128)S(1)}, f32[8,128]{1,0:T(8,128)S(1)}, u32[]{:S(2)}, u32[]{:S(2)}) collective-permute-start(f32[8,128]{1,0:T(8,128)S(1)} %bitcast.37), channel_id=1, source_target_pairs={{0,1},{1,0},{2,3},{3,2},{4,7},{5,6},{6,5},{7,4},{8,9},{9,8},{10,11... | collective-permute-start | bytes 12296 | tf_op jit(solution)/shard_map/ppermute | solution.py:348
  45.8 1.5 %collective-permute-start.19 = (f32[8,128]{1,0:T(8,128)S(1)}, f32[8,128]{1,0:T(8,128)S(1)}, u32[]{:S(2)}, u32[]{:S(2)}) collective-permute-start(f32[8,128]{1,0:T(8,128)S(1)} %collective-permute-done.16.refs_12_), channel_id=1, source_target_pairs={{0,4},{4,0},{8,12},{12,8},{16,20},{20,16},{24,28},{28,24},{1,5},{5... | collective-permute-start | bytes 12296 | tf_op jit(solution)/shard_map/ppermute | solution.py:352
  49.8 1.3 %collective-permute-start.20 = (f32[4,32,128]{2,1,0:T(8,128)S(1)}, f32[4,32,128]{2,1,0:T(8,128)S(1)}, u32[]{:S(2)}, u32[]{:S(2)}) collective-permute-start(f32[4,32,128]{2,1,0:T(8,128)S(1)} %get-tuple-element.50), channel_id=1, source_target_pairs={{0,4},{4,0},{8,12},{12,8},{16,20},{20,16},{24,28},{28,24},{1,5},{5... | collective-permute-start | bytes 196616 | tf_op jit(solution)/shard_map/ppermute | solution.py:352
  51.2 4.3 %collective-permute-start.21 = (f32[2,32,128]{2,1,0:T(8,128)S(1)}, f32[2,32,128]{2,1,0:T(8,128)S(1)}, u32[]{:S(2)}, u32[]{:S(2)}) collective-permute-start(f32[2,32,128]{2,1,0:T(8,128)S(1)} %slice.53), channel_id=1, source_target_pairs={{0,8},{4,28},{8,0},{12,20},{16,24},{20,12},{24,16},{28,4},{1,9},{5... | collective-permute-start | bytes 98312 | tf_op jit(solution)/shard_map/ppermute | solution.py:342
  52.0 3.7 %collective-permute-start.22 = (f32[32,128]{1,0:T(8,128)S(1)}, f32[32,128]{1,0:T(8,128)S(1)}, u32[]{:S(2)}, u32[]{:S(2)}) collective-permute-start(f32[32,128]{1,0:T(8,128)S(1)} %slice_bitcast_fusion), channel_id=1, source_target_pairs={{0,16},{4,20},{8,24},{12,28},{16,0},{20,4},{24,8},{28,12},{1,17},{... | collective-permute-start | bytes 49160 | tf_op jit(solution)/shard_map/ppermute | solution.py:342
  55.5 1.2 %collective-permute-start.23 = (f32[32,128]{1,0:T(8,128)S(1)}, f32[32,128]{1,0:T(8,128)S(1)}, u32[]{:S(2)}, u32[]{:S(2)}) collective-permute-start(f32[32,128]{1,0:T(8,128)S(1)} %dynamic-slice_bitcast_fusion), channel_id=1, source_target_pairs={{0,4},{4,0},{8,12},{12,8},{16,20},{20,16},{24,28},{28,24},{1,5},{5... | collective-permute-start | bytes 49160 | tf_op jit(solution)/shard_map/ppermute | solution.py:352

commit v4 on v3

--- a/solution.py
+++ b/solution.py
@@ -26,11 +26,11 @@
 BF16 = jnp.bfloat16
 
 
-def call(body, out_shape, scratch, n_hbm, n_vmem, limit=24 * 1024 * 1024):
+def call(body, out_shape, scratch, in_specs, limit=24 * 1024 * 1024):
     return pl.pallas_call(
         body,
         out_shape=out_shape,
-        in_specs=[HBM] * n_hbm + [VMEM] * n_vmem,
+        in_specs=in_specs,
         out_specs=[VMEM] * len(out_shape),
         scratch_shapes=scratch,
         compiler_params=pltpu.CompilerParams(vmem_limit_bytes=limit),
@@ -53,31 +53,20 @@
         step(t)
 
 
-def index_scratch(slots):
-    return [
-        pltpu.SMEM((slots,), jnp.int32),
-        pltpu.SMEM((slots,), jnp.int32),
-        pltpu.SMEM((1,), jnp.int32),
-        pltpu.SemaphoreType.DMA((3,)),
-    ]
-
-
-def fetch_index(sources, held):
-    sems = held[3]
-    copies = [pltpu.make_async_copy(s, held[i], sems.at[i]) for i, s in enumerate(sources)]
-    for c in copies:
-        c.start()
-
-    def wait():
-        for c in copies:
-            c.wait()
-
-    return wait
-
-
-def position(held, rb, cb, t):
-    live = t < held[2][0]
-    return jnp.where(live, held[0][t], rb), jnp.where(live, held[1][t], cb)
+def read_codes(codes, held):
+    row = codes[0:1, :]
+    for t in range(held.shape[0]):
+        held[t] = row[0, t]
+
+
+def position(held, t):
+    code = held[t]
+    return code & 255, (code >> 8) & 255
+
+
+def given(held, t):
+    code = held[t]
+    return (code >> 16) & 255, code >> 24
 
 
 def fold_rows(a):
@@ -106,27 +95,39 @@
 
 
 def first_peaks(rb, cb, slots, chunk, *refs):
-    index, tiles_hbm, dual_hbm, payload, scale_col = refs[:3], refs[3], refs[4], refs[5], refs[6]
-    held, (tiles, racc16, cacc16, racc, sems, dual_sem) = refs[7:11], refs[11:]
-    wait_index = fetch_index(index, held)
+    count, row_hbm, col_hbm, tiles_hbm, dual_hbm = refs[:5]
+    payload, scale_col, codes = refs[5:8]
+    row, col, held, tiles, racc16, cacc16, racc, sems, index_sems, dual_sem = refs[8:]
+    index_copies = [
+        pltpu.make_async_copy(row_hbm, row, index_sems.at[0]),
+        pltpu.make_async_copy(col_hbm, col, index_sems.at[1]),
+    ]
     copies = [
         pltpu.make_async_copy(
             tiles_hbm.at[pl.ds(i * chunk, chunk)], tiles.at[pl.ds(i * chunk, chunk)], sems.at[i]
         )
         for i in range(slots // chunk)
     ]
-    for c in copies:
+    dual_copy = pltpu.make_async_copy(dual_hbm, payload.at[pl.ds(2 * rb, dual_hbm.shape[0])], dual_sem)
+    for c in index_copies + copies + [dual_copy]:
         c.start()
-    dual_copy = pltpu.make_async_copy(dual_hbm, payload.at[pl.ds(2 * rb, dual_hbm.shape[0])], dual_sem)
-    dual_copy.start()
     racc16[...] = jnp.zeros_like(racc16)
     cacc16[...] = jnp.zeros_like(cacc16)
     racc[...] = jnp.zeros_like(racc)
-    wait_index()
+    for c in index_copies:
+        c.wait()
+    lane = lax.broadcasted_iota(jnp.int32, codes.shape, 1)
+    packed = jnp.zeros(codes.shape, jnp.int32)
+    for t in range(slots):
+        r, c = row[t], col[t]
+        code = jnp.where(t < count[0], r + (c << 8), rb + (cb << 8)) + (r << 16) + (c << 24)
+        held[t] = code
+        packed = jnp.where(lane == t, code, packed)
+    codes[...] = packed
 
     def plain(t):
         a = jnp.abs(tiles[t])
-        r, c = position(held, rb, cb, t)
+        r, c = position(held, t)
         racc16[r] = jnp.maximum(racc16[r], a)
         cacc16[c] = jnp.maximum(cacc16[c], jnp.max(a.reshape(B // 16, 16, B), axis=0))
 
@@ -141,7 +142,7 @@
 
     def scaled(t):
         a = jnp.abs(tiles[t].astype(F32))
-        r, c = position(held, rb, cb, t)
+        r, c = position(held, t)
         racc[r] = jnp.maximum(racc[r], a * scale_col[pl.ds(c, 1), :])
 
     loop(0, slots, UNROLL, scaled)
@@ -152,11 +153,10 @@
 
 
 def second_peaks(rb, cb, slots, pays, *refs):
-    index, tiles, scale_col1, parts = refs[:3], refs[3], refs[4], refs[5 : 5 + pays]
-    peaks, scale_row2, scale_col3, dual = refs[5 + pays : 9 + pays]
-    held, refs = refs[9 + pays : 13 + pays], refs[13 + pays :]
-    rep, cacc, dacc, scol2, scol3, racc, racc_b = refs
-    wait_index = fetch_index(index, held)
+    codes, tiles, scale_col1, parts = refs[0], refs[1], refs[2], refs[3 : 3 + pays]
+    peaks, scale_row2, scale_col3, dual = refs[3 + pays : 7 + pays]
+    held, rep, cacc, dacc, scol2, scol3, racc, racc_b = refs[7 + pays :]
+    read_codes(codes, held)
     me = lax.axis_index("flt")
     chip, core = me // 2, lax.rem(me, 2)
     peak = parts[0][0 : 2 * rb]
@@ -181,11 +181,10 @@
     dacc[...] = jnp.zeros_like(dacc)
     racc[...] = jnp.zeros_like(racc)
     racc_b[...] = jnp.zeros_like(racc_b)
-    wait_index()
 
     def columns(t):
         a = jnp.abs(tiles[t].astype(F32))
-        r, c = position(held, 0, cb, t)
+        r, c = given(held, t)[0], position(held, t)[1]
         cacc[c] = jnp.maximum(cacc[c], fold_rows(a * rep[r]))
         dacc[c] = jnp.maximum(dacc[c], fold_rows(a * rep[r + rb]))
 
@@ -201,7 +200,7 @@
 
     def rows(t):
         a = jnp.abs(tiles[t].astype(F32))
-        r, c = position(held, rb, cb, t)
+        r, c = position(held, t)
         racc[r] = jnp.maximum(racc[r], a * scol2[pl.ds(c, 1), :])
         racc_b[r] = jnp.maximum(racc_b[r], a * scol3[pl.ds(c, 1), :])
 
@@ -215,7 +214,8 @@
     gacc[...] = jnp.zeros_like(gacc)
 
     def step(t):
-        gacc[held[1][t]] += jnp.dot(lhs[held[0][t]], mat[t], preferred_element_type=F32)
+        r, c = given(held, t)
+        gacc[c] += jnp.dot(lhs[r], mat[t], preferred_element_type=F32)
 
     loop(0, slots, slots, step)
 
@@ -230,17 +230,15 @@
 
 
 def build_step(rb, cb, slots, *refs):
-    index, refs = refs[:3], refs[3:]
-    tiles, srow3, srow4, scale_col3, low, offsets, hold0, mat, scale_col4, hold1, turn = refs[:11]
-    held, (rep, cacc, scol, gacc) = refs[11:15], refs[15:]
-    wait_index = fetch_index(index, held)
+    codes, tiles, srow3, srow4, scale_col3, low, offsets, hold0 = refs[:8]
+    mat, scale_col4, hold1, turn, held, rep, cacc, scol, gacc = refs[8:]
+    read_codes(codes, held)
     spread_rows(rep, jnp.concatenate([srow3[...], srow4[...]], axis=0))
     cacc[...] = jnp.zeros_like(cacc)
-    wait_index()
 
     def columns(t):
         a = jnp.abs(tiles[t].astype(F32))
-        r, c = position(held, 0, cb, t)
+        r, c = given(held, t)[0], position(held, t)[1]
         cacc[c] = jnp.maximum(cacc[c], fold_rows(a * rep[r]))
 
     loop(0, slots, UNROLL, columns)
@@ -250,8 +248,8 @@
     scol[0:cb] = c4
 
     def build(t):
-        live = (t < held[2][0]).astype(F32)
-        r, c = held[0][t], held[1][t]
+        r, c = given(held, t)
+        live = (position(held, t)[0] < rb).astype(F32)
         value = tiles[t].astype(F32) * live * rep[r + rb] * scol[pl.ds(c, 1), :]
         mat[t] = value.astype(BF16)
 
@@ -268,9 +266,8 @@
 
 
 def hold_step(rb, cb, slots, *refs):
-    index, (mat, scol, offsets, hold1, low), (hold2, turn) = refs[:3], refs[3:8], refs[8:10]
-    held, gacc = refs[10:14], refs[14]
-    fetch_index(index, held)()
+    codes, mat, scol, offsets, hold1, low, hold2, turn, held, gacc = refs
+    read_codes(codes, held)
     pull(slots, held, mat, low, gacc)
 
     def write(c, scale, hold, double):
@@ -281,12 +278,11 @@
 
 
 def plan_step(rb, cb, slots, scen_all, means, split, last, *refs):
-    index, refs = refs[:3], refs[3:]
-    mat, srow4, scol, offsets, capacity, plan, turn, own_dual = refs[:8]
-    sums, refs = refs[8 : 8 + means], refs[8 + means :]
-    plan_next, loads, refs = refs[0], refs[1 : 1 + split], refs[1 + split :]
-    held, (lhs, gacc, lacc, mixed) = refs[:4], refs[4:]
-    wait_index = fetch_index(index, held)
+    codes, mat, srow4, scol, offsets, capacity, plan, turn, own_dual = refs[:9]
+    sums, refs = refs[9 : 9 + means], refs[9 + means :]
+    plan_next, loads = refs[0], refs[1 : 1 + split]
+    held, lhs, gacc, lacc, mixed = refs[1 + split :]
+    read_codes(codes, held)
     me = lax.axis_index("flt")
     chip, core = me // 2, lax.rem(me, 2)
     total = sums[0][...]
@@ -295,7 +291,6 @@
         total = (total + jnp.where(core == 0, first, other)) + (second + jnp.where(core == 0, other, first))
     for b in range(rb):
         lhs[b] = three_terms(total[b : b + 1])
-    wait_index()
     pull(slots, held, mat, lhs, gacc)
     for c in range(cb):
         scale = scol[c : c + 1]
@@ -304,12 +299,13 @@
         x = plan[c : c + 1] if last else plan[c : c + 1] / scale
         x_next = jnp.clip(x - TAU_PLAN * (cost + mean_grad), 0.0, 1.0 / scale)
         mixed[c] = ((2.0 * x_next - x) + turn[:, c * B : (c + 1) * B]).astype(BF16)
-        plan_next[c : c + 1] = x_next * scale if last else x_next
+        plan_next[c : c + 1] = x_next
     lacc[...] = jnp.zeros_like(lacc)
 
     def push(t):
-        lacc[held[0][t]] += lax.dot_general(
-            mixed[held[1][t]], mat[t], (((1,), (1,)), ((), ())), preferred_element_type=F32
+        r, c = given(held, t)
+        lacc[r] += lax.dot_general(
+            mixed[c], mat[t], (((1,), (1,)), ((), ())), preferred_element_type=F32
         )
 
     loop(0, slots, slots, push)
@@ -376,27 +372,26 @@
     small = nf == 8 and ns == 4
     me = lax.axis_index("flt")
     chip, core = me // 2, me % 2
-    index = (tile_row, tile_col, tile_count)
     offsets = slot_offset.reshape(cb, B)
     f32 = functools.partial(jax.ShapeDtypeStruct, dtype=F32)
-    held = index_scratch(slots)
+    held = [pltpu.SMEM((slots,), jnp.int32)]
     chunk = 12 if slots % 12 == 0 else slots
 
-    mine, scol1 = call(
+    mine, scol1, codes = call(
         functools.partial(first_peaks, rb, cb, slots, chunk),
-        [f32((2 * rb + scen, B)), f32((cb + 1, B))],
-        held
+        [f32((2 * rb + scen, B)), f32((cb + 1, B)), jax.ShapeDtypeStruct((8, B), jnp.int32)],
+        held * 3
         + [
             pltpu.VMEM((slots, B, B), BF16),
             pltpu.VMEM((rb + 1, B, B), BF16),
             pltpu.VMEM((cb + 1, 16, B), BF16),
             pltpu.VMEM((rb + 1, B, B), F32),
             pltpu.SemaphoreType.DMA((slots // chunk,)),
+            pltpu.SemaphoreType.DMA((2,)),
             pltpu.SemaphoreType.DMA,
         ],
-        5,
-        0,
-    )(in_hbm(tile_row), in_hbm(tile_col), tile_count, in_hbm(tiles), in_hbm(dual0))
+        [pl.BlockSpec(memory_space=pltpu.SMEM)] + [HBM] * 4,
+    )(tile_count, in_hbm(tile_row), in_hbm(tile_col), in_hbm(tiles), in_hbm(dual0))
     n = 2 * rb
     if small:
         other = twin(mine)
@@ -422,9 +417,8 @@
             pltpu.VMEM((rb + 1, B, B), F32),
             pltpu.VMEM((rb + 1, B, B), F32),
         ],
-        3,
-        2 + len(parts),
-    )(*index, tiles, scol1, *parts)
+        [VMEM] * (3 + len(parts)),
+    )(codes, tiles, scol1, *parts)
     if small:
         mine = jnp.maximum(peaks, twin(peaks))
         best, second = jnp.maximum(mine, cross(mine, *FIRST)), cross(mine, *SECOND)
@@ -452,9 +446,8 @@
             pltpu.VMEM((cb, B), F32),
             gacc,
         ],
-        3,
-        7,
-    )(*index, tiles, srow3, srow4, scol3, low, offsets, hold0)
+        [VMEM] * 8,
+    )(codes, tiles, srow3, srow4, scol3, low, offsets, hold0)
     plan = plan0.reshape(cb, B)
     for step in range(2):
         if step:
@@ -473,9 +466,8 @@
                 functools.partial(hold_step, rb, cb, slots),
                 [f32((scen, cb * B)), f32((scen, cb * B))],
                 held + [gacc],
-                3,
-                5,
-            )(*index, mat, scol4, offsets, hold1, low)
+                [VMEM] * 6,
+            )(codes, mat, scol4, offsets, hold1, low)
         if small:
             first, second = cross_scn(sums, *FIRST_SCN), cross_scn(sums, *SECOND_SCN)
             first, second, turn = lax.optimization_barrier((first, second, turn))
@@ -495,9 +487,8 @@
                 pltpu.VMEM((rb, scen, B), F32),
                 pltpu.VMEM((cb, scen, B), BF16),
             ],
-            3,
-            8 + len(totals),
-        )(*index, mat, srow4, scol4, offsets, capacity, plan, turn, own_dual, *totals)
+            [VMEM] * (9 + len(totals)),
+        )(codes, mat, srow4, scol4, offsets, capacity, plan, turn, own_dual, *totals)
     if small:
         chip_sum = loads[0] + twin(loads[1])
         first, second = cross(chip_sum[1:3], *FIRST), cross(chip_sum[3], *SECOND)
@@ -506,7 +497,7 @@
     else:
         total = lax.psum_scatter(loads[0], "flt", scatter_dimension=0, tiled=False)
     dual = jnp.maximum(SIGMA * total, 0.0) * own_row
-    return plan.reshape(-1), hold, dual
+    return (plan * scol4).reshape(-1), hold, dual
 
 
 def solution(mesh):

time: 57.5 us -> 55.2 us (0.960)
  Pallas kernels: 14 us -> 11.5 us
  other arithmetic: 0.82 us -> 1.41 us
    pallas_call x2, Pallas kernels: 4.58 us -> 3.19 us  [body(): call(functools.partial(plan_step, rb, cb, slots, scen_all, len(totals), s...]
    ppermute x11, waiting for transfers between devices: 7.4 us -> 6.71 us  [twin(): lax.ppermute(x, 'flt', [(i, i ^ 1) for i in range(lax.axis_size('flt'))])]
    reshape x0 -> x1, other arithmetic: none -> 0.6 us  [body(): return ((plan * scol4).reshape(-1), hold, dual)]
  transfers between devices with their start and end apart: 24 -> 24, of which waited for: 18 -> 18; matrix products, arithmetic and copies ran while one was open for 0% -> 1% of each run, Pallas kernels for 7% -> 6%
where the time goes in v4:
time: 55.2 us; the launch traced here: 55.1 us
  starting transfers between devices  22.2 us (40%)
  waiting for transfers between devices  18.3 us (33%)
  Pallas kernels  11.5 us (21%)
  between operations  1.6 us (3%)
  other arithmetic  1.41 us (3%)
    ppermute x9, starting transfers between devices, cross(): return lax.ppermute(x, 'flt', pairs)  12.6 us
    ppermute x9, waiting for transfers between devices, cross(): return lax.ppermute(x, 'flt', pairs)  10.5 us
    ppermute x11, waiting for transfers between devices, twin(): lax.ppermute(x, 'flt', [(i, i ^ 1) for i in range(lax.axis_size('flt'))])  6.71 us
    ppermute x4, starting transfers between devices, cross_scn(): return lax.ppermute(x, ('flt', 'scn'), pairs)  6.58 us
    pallas_call x2, Pallas kernels, body(): call(functools.partial(plan_step, rb, cb, slots, scen_all, len(totals), s...  3.19 us
    ppermute x11, starting transfers between devices, twin(): lax.ppermute(x, 'flt', [(i, i ^ 1) for i in range(lax.axis_size('flt'))])  3.06 us
    pallas_call x1, Pallas kernels, body(): call(functools.partial(first_peaks, rb, cb, slots, chunk), [f32((2 * rb +...  2.62 us
    pallas_call x1, Pallas kernels, body(): call(functools.partial(second_peaks, rb, cb, slots, len(parts)), [f32((2...  2.55 us
  transfers between devices with their start and end apart: 24, of which 18 were waited for; matrix products, arithmetic and copies ran while one was open for 1% of the time, Pallas kernels for 6%

profile of v4, /device:TPU:0, one launch (start us, length us, event | category | flops | bytes accessed | tf_op | source)
XLA Modules:
  0.0 55.1 jit_solution(16018838374896827621)
XLA Ops:
  1.4 2.6 %shard_map.112 = (f32[48,128]{1,0:T(8,128)S(1)}, f32[9,128]{1,0:T(8,128)S(1)}, s32[8,128]{1,0:T(8,128)S(1)}) custom-call(s32[1]{0:T(128)S(6)} %copy.14.refs_0_, s32[48]{0:T(128)} %refs_1_.3, s32[48]{0:T(128)} %refs_2_.1, bf16[48,128,128]{2,1,0:T(8,128)(2,1)} %refs_1_.5, f32[32,128]{1,0:T(8,128)} %refs_4_.1), custom_call_target="tpu_custom_call" | custom-call | tf_op jit(solution)/shard_map/pallas_call | solution.py:380
  4.6 0.8 %collective-permute-done = f32[48,128]{1,0:T(8,128)S(1)} collective-permute-done((f32[48,128]{1,0:T(8,128)S(1)}, f32[48,128]{1,0:T(8,128)S(1)}, u32[]{:S(2)}, u32[]{:S(2)}) %collective-permute-start) | collective-permute-done | bytes 24608 | tf_op jit(solution)/shard_map/ppermute | solution.py:348
  5.4 2.9 %collective-permute-start.1 = (f32[80,128]{1,0:T(8,128)S(1)}, f32[80,128]{1,0:T(8,128)S(1)}, u32[]{:S(2)}, u32[]{:S(2)}) collective-permute-start(f32[80,128]{1,0:T(8,128)S(1)} %pad_maximum_fusion.1.refs_3_), channel_id=1, source_target_pairs={{0,8},{4,28},{8,0},{12,20},{16,24},{20,12},{24,16},{28,4},{1,9},{5... | collective-permute-start | bytes 122888 | tf_op jit(solution)/shard_map/ppermute | solution.py:338
  8.3 1.5 %collective-permute-start.2 = (f32[80,128]{1,0:T(8,128)S(1)}, f32[80,128]{1,0:T(8,128)S(1)}, u32[]{:S(2)}, u32[]{:S(2)}) collective-permute-start(f32[80,128]{1,0:T(8,128)S(1)} %pad_maximum_fusion.1.refs_3_), channel_id=1, source_target_pairs={{0,16},{4,20},{8,24},{12,28},{16,0},{20,4},{24,8},{28,12},{1,17},{... | collective-permute-start | bytes 122888 | tf_op jit(solution)/shard_map/ppermute | solution.py:338
  10.7 2.0 %collective-permute-done.2.refs_5_ = f32[80,128]{1,0:T(8,128)S(1)} collective-permute-done((f32[80,128]{1,0:T(8,128)S(1)}, f32[80,128]{1,0:T(8,128)S(1)}, u32[]{:S(2)}, u32[]{:S(2)}) %collective-permute-start.2) | collective-permute-done | bytes 40992 | tf_op jit(solution)/shard_map/ppermute | solution.py:338
  12.7 2.5 %shard_map.113 = (f32[16,128]{1,0:T(8,128)S(1)}, f32[8,128]{1,0:T(8,128)S(1)}, f32[8,128]{1,0:T(8,128)S(1)}, f32[8,32,128]{2,1,0:T(8,128)S(1)}) custom-call(s32[8,128]{1,0:T(8,128)S(1)} %get-tuple-element.28.refs_0_, bf16[48,128,128]{2,1,0:T(8,128)(2,1)S(1)} %copy-done, f32[9,128]{1,0:T(8,128)S(1)} %get-tuple-element.29.refs_2_, ...), custom_call_target="tpu_custom_call" | custom-call | tf_op jit(solution)/shard_map/pallas_call | solution.py:407
  15.3 1.2 %collective-permute-done.4 = f32[16,128]{1,0:T(8,128)S(1)} collective-permute-done((f32[16,128]{1,0:T(8,128)S(1)}, f32[16,128]{1,0:T(8,128)S(1)}, u32[]{:S(2)}, u32[]{:S(2)}) %collective-permute-start.4) | collective-permute-done | bytes 8224 | tf_op jit(solution)/shard_map/ppermute | solution.py:348
  16.5 1.2 %collective-permute-start.5 = (f32[16,128]{1,0:T(8,128)S(1)}, f32[16,128]{1,0:T(8,128)S(1)}, u32[]{:S(2)}, u32[]{:S(2)}) collective-permute-start(f32[16,128]{1,0:T(8,128)S(1)} %max.32), channel_id=1, source_target_pairs={{0,8},{4,28},{8,0},{12,20},{16,24},{20,12},{24,16},{28,4},{1,9},{5... | collective-permute-start | bytes 24584 | tf_op jit(solution)/shard_map/ppermute | solution.py:338
  17.7 1.3 %collective-permute-start.6 = (f32[16,128]{1,0:T(8,128)S(1)}, f32[16,128]{1,0:T(8,128)S(1)}, u32[]{:S(2)}, u32[]{:S(2)}) collective-permute-start(f32[16,128]{1,0:T(8,128)S(1)} %max.32), channel_id=1, source_target_pairs={{0,16},{4,20},{8,24},{12,28},{16,0},{20,4},{24,8},{28,12},{1,17},{... | collective-permute-start | bytes 24584 | tf_op jit(solution)/shard_map/ppermute | solution.py:338
  18.9 1.2 %collective-permute-done.5 = f32[16,128]{1,0:T(8,128)S(1)} collective-permute-done((f32[16,128]{1,0:T(8,128)S(1)}, f32[16,128]{1,0:T(8,128)S(1)}, u32[]{:S(2)}, u32[]{:S(2)}) %collective-permute-start.5) | collective-permute-done | bytes 8224 | tf_op jit(solution)/shard_map/ppermute | solution.py:338
  20.1 1.2 %collective-permute-done.6 = f32[16,128]{1,0:T(8,128)S(1)} collective-permute-done((f32[16,128]{1,0:T(8,128)S(1)}, f32[16,128]{1,0:T(8,128)S(1)}, u32[]{:S(2)}, u32[]{:S(2)}) %collective-permute-start.6) | collective-permute-done | bytes 8224 | tf_op jit(solution)/shard_map/ppermute | solution.py:338
  21.4 2.7 %collective-permute-start.9 = (f32[8,128]{1,0:T(8,128)S(1)}, f32[8,128]{1,0:T(8,128)S(1)}, u32[]{:S(2)}, u32[]{:S(2)}) collective-permute-start(f32[8,128]{1,0:T(8,128)S(1)} %get-tuple-element.57.refs_9_), channel_id=1, source_target_pairs={{0,2},{1,3},{2,0},{3,1},{4,6},{5,7},{6,4},{7,5},{8,10},{9,11},{10,... | collective-permute-start | bytes 12296 | tf_op jit(solution)/shard_map/ppermute | solution.py:344
  24.1 1.6 %collective-permute-start.8 = (f32[8,128]{1,0:T(8,128)S(1)}, f32[8,128]{1,0:T(8,128)S(1)}, u32[]{:S(2)}, u32[]{:S(2)}) collective-permute-start(f32[8,128]{1,0:T(8,128)S(1)} %get-tuple-element.57.refs_9_), channel_id=1, source_target_pairs={{0,1},{1,0},{2,3},{3,2},{4,7},{5,6},{6,5},{7,4},{8,9},{9,8},{10,11... | collective-permute-start | bytes 12296 | tf_op jit(solution)/shard_map/ppermute | solution.py:344
  25.6 1.8 %shard_map.114 = (bf16[48,128,128]{2,1,0:T(8,128)(2,1)S(1)}, f32[8,128]{1,0:T(8,128)S(1)}, f32[32,1024]{1,0:T(8,128)S(1)}, f32[32,1024]{1,0:T(8,128)S(1)}) custom-call(s32[8,128]{1,0:T(8,128)S(1)} %get-tuple-element.28.refs_0_, bf16[48,128,128]{2,1,0:T(8,128)(2,1)S(1)} %copy-done, f32[8,128]{1,0:T(8,128)S(1)} %get-tuple-element.56.refs_2_, ...), custom_call_target="tpu_custom_call" | custom-call | tf_op jit(solution)/shard_map/pallas_call | solution.py:434
  28.2 0.8 %collective-permute-done.10.refs_12_ = f32[8,128]{1,0:T(8,128)S(1)} collective-permute-done((f32[8,128]{1,0:T(8,128)S(1)}, f32[8,128]{1,0:T(8,128)S(1)}, u32[]{:S(2)}, u32[]{:S(2)}) %collective-permute-start.10) | collective-permute-done | bytes 4128 | tf_op jit(solution)/shard_map/ppermute | solution.py:348
  29.0 1.6 %shard_map.115 = (f32[8,128]{1,0:T(8,128)S(1)}, f32[4,32,128]{2,1,0:T(8,128)S(1)}, f32[4,32,128]{2,1,0:T(8,128)S(1)}) custom-call(s32[8,128]{1,0:T(8,128)S(1)} %get-tuple-element.28.refs_0_, bf16[48,128,128]{2,1,0:T(8,128)(2,1)S(1)} %get-tuple-element.35.refs_1_, f32[8,128]{1,0:T(8,128)S(1)} %get-tuple-element.55.refs_3_.refs_2_, ...), custom_call_target="tpu_custom_call" | custom-call | tf_op jit(solution)/shard_map/pallas_call | solution.py:478
  31.0 0.9 %collective-permute-done.11 = f32[4,32,128]{2,1,0:T(8,128)S(1)} collective-permute-done((f32[4,32,128]{2,1,0:T(8,128)S(1)}, f32[4,32,128]{2,1,0:T(8,128)S(1)}, u32[]{:S(2)}, u32[]{:S(2)}) %collective-permute-start.11) | collective-permute-done | bytes 65568 | tf_op jit(solution)/shard_map/ppermute | solution.py:348
  31.9 2.0 %collective-permute-start.14 = (f32[4,32,128]{2,1,0:T(8,128)S(1)}, f32[4,32,128]{2,1,0:T(8,128)S(1)}, u32[]{:S(2)}, u32[]{:S(2)}) collective-permute-start(f32[4,32,128]{2,1,0:T(8,128)S(1)} %add.57), channel_id=1, source_target_pairs={{0,24},{4,28},{8,16},{12,20},{16,8},{20,12},{24,0},{28,4},{1,25},{... | collective-permute-start | bytes 196616 | tf_op jit(solution)/shard_map/ppermute | solution.py:338
  33.9 0.8 %collective-permute-start.13 = (f32[4,32,128]{2,1,0:T(8,128)S(1)}, f32[4,32,128]{2,1,0:T(8,128)S(1)}, u32[]{:S(2)}, u32[]{:S(2)}) collective-permute-start(f32[4,32,128]{2,1,0:T(8,128)S(1)} %add.57), channel_id=1, source_target_pairs={{0,16},{4,20},{8,24},{12,28},{16,0},{20,4},{24,8},{28,12},{1,17},{... | collective-permute-start | bytes 196616 | tf_op jit(solution)/shard_map/ppermute | solution.py:338
  34.7 0.7 %collective-permute-start.12 = (f32[4,32,128]{2,1,0:T(8,128)S(1)}, f32[4,32,128]{2,1,0:T(8,128)S(1)}, u32[]{:S(2)}, u32[]{:S(2)}) collective-permute-start(f32[4,32,128]{2,1,0:T(8,128)S(1)} %add.57), channel_id=1, source_target_pairs={{0,8},{4,12},{8,0},{12,4},{16,24},{20,28},{24,16},{28,20},{1,9},{5... | collective-permute-start | bytes 196616 | tf_op jit(solution)/shard_map/ppermute | solution.py:338
  35.5 1.8 %collective-permute-done.14 = f32[4,32,128]{2,1,0:T(8,128)S(1)} collective-permute-done((f32[4,32,128]{2,1,0:T(8,128)S(1)}, f32[4,32,128]{2,1,0:T(8,128)S(1)}, u32[]{:S(2)}, u32[]{:S(2)}) %collective-permute-start.14) | collective-permute-done | bytes 65568 | tf_op jit(solution)/shard_map/ppermute | solution.py:338
  37.3 1.3 %collective-permute-done.13 = f32[4,32,128]{2,1,0:T(8,128)S(1)} collective-permute-done((f32[4,32,128]{2,1,0:T(8,128)S(1)}, f32[4,32,128]{2,1,0:T(8,128)S(1)}, u32[]{:S(2)}, u32[]{:S(2)}) %collective-permute-start.13) | collective-permute-done | bytes 65568 | tf_op jit(solution)/shard_map/ppermute | solution.py:338
  40.3 0.8 %collective-permute-start.17 = (f32[8,128]{1,0:T(8,128)S(1)}, f32[8,128]{1,0:T(8,128)S(1)}, u32[]{:S(2)}, u32[]{:S(2)}) collective-permute-start(f32[8,128]{1,0:T(8,128)S(1)} %bitcast.37), channel_id=1, source_target_pairs={{0,2},{1,3},{2,0},{3,1},{4,6},{5,7},{6,4},{7,5},{8,10},{9,11},{10,... | collective-permute-start | bytes 12296 | tf_op jit(solution)/shard_map/ppermute | solution.py:344
  41.1 1.6 %collective-permute-start.16 = (f32[8,128]{1,0:T(8,128)S(1)}, f32[8,128]{1,0:T(8,128)S(1)}, u32[]{:S(2)}, u32[]{:S(2)}) collective-permute-start(f32[8,128]{1,0:T(8,128)S(1)} %bitcast.38), channel_id=1, source_target_pairs={{0,1},{1,0},{2,3},{3,2},{4,7},{5,6},{6,5},{7,4},{8,9},{9,8},{10,11... | collective-permute-start | bytes 12296 | tf_op jit(solution)/shard_map/ppermute | solution.py:344
  42.7 1.4 %shard_map.116 = (f32[32,1024]{1,0:T(8,128)}, f32[32,1024]{1,0:T(8,128)S(1)}) custom-call(s32[8,128]{1,0:T(8,128)S(1)} %get-tuple-element.28.refs_0_, bf16[48,128,128]{2,1,0:T(8,128)(2,1)S(1)} %get-tuple-element.35.refs_1_, f32[8,128]{1,0:T(8,128)S(1)} %get-tuple-element.36.refs_3_.refs_2_, s32[8,128]{1,0:T(8,128)S(1)} %bitcast.35, ...), custom_call_target="tpu_custom_call" | custom-call | tf_op jit(solution)/shard_map/pallas_call | solution.py:465
  44.0 0.8 %collective-permute-done.17.refs_11_ = f32[8,128]{1,0:T(8,128)S(1)} collective-permute-done((f32[8,128]{1,0:T(8,128)S(1)}, f32[8,128]{1,0:T(8,128)S(1)}, u32[]{:S(2)}, u32[]{:S(2)}) %collective-permute-start.17) | collective-permute-done | bytes 4128 | tf_op jit(solution)/shard_map/ppermute | solution.py:344
  45.2 0.8 %collective-permute-done.19.refs_12_ = f32[8,128]{1,0:T(8,128)S(1)} collective-permute-done((f32[8,128]{1,0:T(8,128)S(1)}, f32[8,128]{1,0:T(8,128)S(1)}, u32[]{:S(2)}, u32[]{:S(2)}) %collective-permute-start.19) | collective-permute-done | bytes 4128 | tf_op jit(solution)/shard_map/ppermute | solution.py:348
  46.0 1.6 %shard_map.117 = (f32[8,128]{1,0:T(8,128)S(1)}, f32[4,32,128]{2,1,0:T(8,128)S(1)}, f32[4,32,128]{2,1,0:T(8,128)S(1)}) custom-call(s32[8,128]{1,0:T(8,128)S(1)} %get-tuple-element.28.refs_0_, bf16[48,128,128]{2,1,0:T(8,128)(2,1)S(1)} %get-tuple-element.35.refs_1_, f32[8,128]{1,0:T(8,128)S(1)} %get-tuple-element.55.refs_3_.refs_2_, ...), custom_call_target="tpu_custom_call" | custom-call | tf_op jit(solution)/shard_map/pallas_call | solution.py:478
  48.0 0.9 %collective-permute-done.20 = f32[4,32,128]{2,1,0:T(8,128)S(1)} collective-permute-done((f32[4,32,128]{2,1,0:T(8,128)S(1)}, f32[4,32,128]{2,1,0:T(8,128)S(1)}, u32[]{:S(2)}, u32[]{:S(2)}) %collective-permute-start.20) | collective-permute-done | bytes 65568 | tf_op jit(solution)/shard_map/ppermute | solution.py:348
  49.0 1.0 %collective-permute-start.21 = (f32[2,32,128]{2,1,0:T(8,128)S(1)}, f32[2,32,128]{2,1,0:T(8,128)S(1)}, u32[]{:S(2)}, u32[]{:S(2)}) collective-permute-start(f32[2,32,128]{2,1,0:T(8,128)S(1)} %slice.53), channel_id=1, source_target_pairs={{0,8},{4,28},{8,0},{12,20},{16,24},{20,12},{24,16},{28,4},{1,9},{5... | collective-permute-start | bytes 98312 | tf_op jit(solution)/shard_map/ppermute | solution.py:338
  50.0 1.1 %collective-permute-start.22 = (f32[32,128]{1,0:T(8,128)S(1)}, f32[32,128]{1,0:T(8,128)S(1)}, u32[]{:S(2)}, u32[]{:S(2)}) collective-permute-start(f32[32,128]{1,0:T(8,128)S(1)} %slice_bitcast_fusion), channel_id=1, source_target_pairs={{0,16},{4,20},{8,24},{12,28},{16,0},{20,4},{24,8},{28,12},{1,17},{... | collective-permute-start | bytes 49160 | tf_op jit(solution)/shard_map/ppermute | solution.py:338
  51.1 2.2 %collective-permute-done.21 = f32[2,32,128]{2,1,0:T(8,128)S(1)} collective-permute-done((f32[2,32,128]{2,1,0:T(8,128)S(1)}, f32[2,32,128]{2,1,0:T(8,128)S(1)}, u32[]{:S(2)}, u32[]{:S(2)}) %collective-permute-start.21) | collective-permute-done | bytes 32800 | tf_op jit(solution)/shard_map/ppermute | solution.py:338
  (62 shorter events, 6.8 us)
Async XLA Ops:
  0.6 12.0 %copy-start = (bf16[48,128,128]{2,1,0:T(8,128)(2,1)S(1)}, bf16[48,128,128]{2,1,0:T(8,128)(2,1)}, u32[]{:S(2)}) copy-start(bf16[48,128,128]{2,1,0:T(8,128)(2,1)} %refs_1_.5) | copy-start | bytes 4718596
  4.0 21.6 %copy-start.1 = (f32[32,1024]{1,0:T(8,128)S(1)}, f32[32,1024]{1,0:T(8,128)}, u32[]{:S(2)}) copy-start(f32[32,1024]{1,0:T(8,128)} %refs_7_.1) | copy-start | bytes 393220
  4.0 21.6 %copy-start.3 = (s32[1024]{0:T(1024)S(1)}, s32[1024]{0:T(1024)}, u32[]{:S(2)}) copy-start(s32[1024]{0:T(1024)} %param.13) | copy-start | bytes 12292
  4.1 1.4 %collective-permute-start = (f32[48,128]{1,0:T(8,128)S(1)}, f32[48,128]{1,0:T(8,128)S(1)}, u32[]{:S(2)}, u32[]{:S(2)}) collective-permute-start(f32[48,128]{1,0:T(8,128)S(1)} %get-tuple-element.30), channel_id=1, source_target_pairs={{0,4},{4,0},{8,12},{12,8},{16,20},{20,16},{24,28},{28,24},{1,5},{5... | collective-permute-start | bytes 73736 | tf_op jit(solution)/shard_map/ppermute | solution.py:348
  5.4 4.9 %collective-permute-start.1 = (f32[80,128]{1,0:T(8,128)S(1)}, f32[80,128]{1,0:T(8,128)S(1)}, u32[]{:S(2)}, u32[]{:S(2)}) collective-permute-start(f32[80,128]{1,0:T(8,128)S(1)} %pad_maximum_fusion.1.refs_3_), channel_id=1, source_target_pairs={{0,8},{4,28},{8,0},{12,20},{16,24},{20,12},{24,16},{28,4},{1,9},{5... | collective-permute-start | bytes 122888 | tf_op jit(solution)/shard_map/ppermute | solution.py:338
  8.3 4.3 %collective-permute-start.2 = (f32[80,128]{1,0:T(8,128)S(1)}, f32[80,128]{1,0:T(8,128)S(1)}, u32[]{:S(2)}, u32[]{:S(2)}) collective-permute-start(f32[80,128]{1,0:T(8,128)S(1)} %pad_maximum_fusion.1.refs_3_), channel_id=1, source_target_pairs={{0,16},{4,20},{8,24},{12,28},{16,0},{20,4},{24,8},{28,12},{1,17},{... | collective-permute-start | bytes 122888 | tf_op jit(solution)/shard_map/ppermute | solution.py:338
  10.3 2.3 %collective-permute-start.3 = (f32[80,128]{1,0:T(8,128)S(1)}, f32[80,128]{1,0:T(8,128)S(1)}, u32[]{:S(2)}, u32[]{:S(2)}) collective-permute-start(f32[80,128]{1,0:T(8,128)S(1)} %pad_maximum_fusion.2), channel_id=1, source_target_pairs={{0,4},{4,0},{8,12},{12,8},{16,20},{20,16},{24,28},{28,24},{1,5},{5... | collective-permute-start | bytes 122888 | tf_op jit(solution)/shard_map/ppermute | solution.py:348
  12.7 15.5 %copy-start.5 = (f32[32,128]{1,0:T(8,128)S(1)}, f32[32,128]{1,0:T(8,128)}, u32[]{:S(2)}) copy-start(f32[32,128]{1,0:T(8,128)} %refs_4_.1) | copy-start | bytes 49156
  12.7 16.3 %copy-start.2 = (s32[32,128]{1,0:T(8,128)S(1)}, s32[32,128]{1,0:T(8,128)}, u32[]{:S(2)}) copy-start(s32[32,128]{1,0:T(8,128)} %refs_5_.3) | copy-start | bytes 49156
  12.7 16.3 %copy-start.4 = (f32[1024]{0:T(1024)S(1)}, f32[1024]{0:T(1024)}, u32[]{:S(2)}) copy-start(f32[1024]{0:T(1024)} %param.15) | copy-start | bytes 12292
  15.2 1.2 %collective-permute-start.4 = (f32[16,128]{1,0:T(8,128)S(1)}, f32[16,128]{1,0:T(8,128)S(1)}, u32[]{:S(2)}, u32[]{:S(2)}) collective-permute-start(f32[16,128]{1,0:T(8,128)S(1)} %get-tuple-element.32), channel_id=1, source_target_pairs={{0,4},{4,0},{8,12},{12,8},{16,20},{20,16},{24,28},{28,24},{1,5},{5... | collective-permute-start | bytes 24584 | tf_op jit(solution)/shard_map/ppermute | solution.py:348
  16.5 3.7 %collective-permute-start.5 = (f32[16,128]{1,0:T(8,128)S(1)}, f32[16,128]{1,0:T(8,128)S(1)}, u32[]{:S(2)}, u32[]{:S(2)}) collective-permute-start(f32[16,128]{1,0:T(8,128)S(1)} %max.32), channel_id=1, source_target_pairs={{0,8},{4,28},{8,0},{12,20},{16,24},{20,12},{24,16},{28,4},{1,9},{5... | collective-permute-start | bytes 24584 | tf_op jit(solution)/shard_map/ppermute | solution.py:338
  17.7 3.7 %collective-permute-start.6 = (f32[16,128]{1,0:T(8,128)S(1)}, f32[16,128]{1,0:T(8,128)S(1)}, u32[]{:S(2)}, u32[]{:S(2)}) collective-permute-start(f32[16,128]{1,0:T(8,128)S(1)} %max.32), channel_id=1, source_target_pairs={{0,16},{4,20},{8,24},{12,28},{16,0},{20,4},{24,8},{28,12},{1,17},{... | collective-permute-start | bytes 24584 | tf_op jit(solution)/shard_map/ppermute | solution.py:338
  20.1 1.2 %collective-permute-start.7 = (f32[16,128]{1,0:T(8,128)S(1)}, f32[16,128]{1,0:T(8,128)S(1)}, u32[]{:S(2)}, u32[]{:S(2)}) collective-permute-start(f32[16,128]{1,0:T(8,128)S(1)} %max.33), channel_id=1, source_target_pairs={{0,4},{4,0},{8,12},{12,8},{16,20},{20,16},{24,28},{28,24},{1,5},{5... | collective-permute-start | bytes 24584 | tf_op jit(solution)/shard_map/ppermute | solution.py:348
  21.4 6.0 %collective-permute-start.9 = (f32[8,128]{1,0:T(8,128)S(1)}, f32[8,128]{1,0:T(8,128)S(1)}, u32[]{:S(2)}, u32[]{:S(2)}) collective-permute-start(f32[8,128]{1,0:T(8,128)S(1)} %get-tuple-element.57.refs_9_), channel_id=1, source_target_pairs={{0,2},{1,3},{2,0},{3,1},{4,6},{5,7},{6,4},{7,5},{8,10},{9,11},{10,... | collective-permute-start | bytes 12296 | tf_op jit(solution)/shard_map/ppermute | solution.py:344
  24.1 3.6 %collective-permute-start.8 = (f32[8,128]{1,0:T(8,128)S(1)}, f32[8,128]{1,0:T(8,128)S(1)}, u32[]{:S(2)}, u32[]{:S(2)}) collective-permute-start(f32[8,128]{1,0:T(8,128)S(1)} %get-tuple-element.57.refs_9_), channel_id=1, source_target_pairs={{0,1},{1,0},{2,3},{3,2},{4,7},{5,6},{6,5},{7,4},{8,9},{9,8},{10,11... | collective-permute-start | bytes 12296 | tf_op jit(solution)/shard_map/ppermute | solution.py:344
  27.7 1.3 %collective-permute-start.10 = (f32[8,128]{1,0:T(8,128)S(1)}, f32[8,128]{1,0:T(8,128)S(1)}, u32[]{:S(2)}, u32[]{:S(2)}) collective-permute-start(f32[8,128]{1,0:T(8,128)S(1)} %collective-permute-done.8.refs_10_), channel_id=1, source_target_pairs={{0,4},{4,0},{8,12},{12,8},{16,20},{20,16},{24,28},{28,24},{1,5},{5... | collective-permute-start | bytes 12296 | tf_op jit(solution)/shard_map/ppermute | solution.py:348
  30.6 1.3 %collective-permute-start.11 = (f32[4,32,128]{2,1,0:T(8,128)S(1)}, f32[4,32,128]{2,1,0:T(8,128)S(1)}, u32[]{:S(2)}, u32[]{:S(2)}) collective-permute-start(f32[4,32,128]{2,1,0:T(8,128)S(1)} %get-tuple-element.43), channel_id=1, source_target_pairs={{0,4},{4,0},{8,12},{12,8},{16,20},{20,16},{24,28},{28,24},{1,5},{5... | collective-permute-start | bytes 196616 | tf_op jit(solution)/shard_map/ppermute | solution.py:348
  31.9 5.4 %collective-permute-start.14 = (f32[4,32,128]{2,1,0:T(8,128)S(1)}, f32[4,32,128]{2,1,0:T(8,128)S(1)}, u32[]{:S(2)}, u32[]{:S(2)}) collective-permute-start(f32[4,32,128]{2,1,0:T(8,128)S(1)} %add.57), channel_id=1, source_target_pairs={{0,24},{4,28},{8,16},{12,20},{16,8},{20,12},{24,0},{28,4},{1,25},{... | collective-permute-start | bytes 196616 | tf_op jit(solution)/shard_map/ppermute | solution.py:338
  33.9 4.7 %collective-permute-start.13 = (f32[4,32,128]{2,1,0:T(8,128)S(1)}, f32[4,32,128]{2,1,0:T(8,128)S(1)}, u32[]{:S(2)}, u32[]{:S(2)}) collective-permute-start(f32[4,32,128]{2,1,0:T(8,128)S(1)} %add.57), channel_id=1, source_target_pairs={{0,16},{4,20},{8,24},{12,28},{16,0},{20,4},{24,8},{28,12},{1,17},{... | collective-permute-start | bytes 196616 | tf_op jit(solution)/shard_map/ppermute | solution.py:338
  34.7 4.3 %collective-permute-start.12 = (f32[4,32,128]{2,1,0:T(8,128)S(1)}, f32[4,32,128]{2,1,0:T(8,128)S(1)}, u32[]{:S(2)}, u32[]{:S(2)}) collective-permute-start(f32[4,32,128]{2,1,0:T(8,128)S(1)} %add.57), channel_id=1, source_target_pairs={{0,8},{4,12},{8,0},{12,4},{16,24},{20,28},{24,16},{28,20},{1,9},{5... | collective-permute-start | bytes 196616 | tf_op jit(solution)/shard_map/ppermute | solution.py:338
  39.0 1.2 %collective-permute-start.15 = (f32[4,128]{1,0:T(4,128)S(1)}, f32[4,128]{1,0:T(4,128)S(1)}, u32[]{:S(2)}, u32[]{:S(2)}) collective-permute-start(f32[4,128]{1,0:T(4,128)S(1)} %reduce-precision_reduce_fusion), channel_id=1, source_target_pairs={{0,4},{4,0},{8,12},{12,8},{16,20},{20,16},{24,28},{28,24},{1,5},{5... | collective-permute-start | bytes 6152 | tf_op jit(solution)/shard_map/ppermute | solution.py:348
  39.1 3.5 %collective-permute-start.18 = (bf16[4,32,128]{2,1,0:T(8,128)(2,1)S(1)}, bf16[4,32,128]{2,1,0:T(8,128)(2,1)S(1)}, u32[]{:S(2)}, u32[]{:S(2)}) collective-permute-start(bf16[4,32,128]{2,1,0:T(8,128)(2,1)S(1)} %get-tuple-element.53), channel_id=1, source_target_pairs={{0,4},{4,0},{8,12},{12,8},{16,20},{20,16},{24,28},{28,24},{1,5},{5... | collective-permute-start | bytes 98312 | tf_op jit(solution)/shard_map/ppermute | solution.py:348
  40.3 4.6 %collective-permute-start.17 = (f32[8,128]{1,0:T(8,128)S(1)}, f32[8,128]{1,0:T(8,128)S(1)}, u32[]{:S(2)}, u32[]{:S(2)}) collective-permute-start(f32[8,128]{1,0:T(8,128)S(1)} %bitcast.37), channel_id=1, source_target_pairs={{0,2},{1,3},{2,0},{3,1},{4,6},{5,7},{6,4},{7,5},{8,10},{9,11},{10,... | collective-permute-start | bytes 12296 | tf_op jit(solution)/shard_map/ppermute | solution.py:344
  41.1 3.8 %collective-permute-start.16 = (f32[8,128]{1,0:T(8,128)S(1)}, f32[8,128]{1,0:T(8,128)S(1)}, u32[]{:S(2)}, u32[]{:S(2)}) collective-permute-start(f32[8,128]{1,0:T(8,128)S(1)} %bitcast.38), channel_id=1, source_target_pairs={{0,1},{1,0},{2,3},{3,2},{4,7},{5,6},{6,5},{7,4},{8,9},{9,8},{10,11... | collective-permute-start | bytes 12296 | tf_op jit(solution)/shard_map/ppermute | solution.py:344
  44.9 1.2 %collective-permute-start.19 = (f32[8,128]{1,0:T(8,128)S(1)}, f32[8,128]{1,0:T(8,128)S(1)}, u32[]{:S(2)}, u32[]{:S(2)}) collective-permute-start(f32[8,128]{1,0:T(8,128)S(1)} %collective-permute-done.16.refs_10_), channel_id=1, source_target_pairs={{0,4},{4,0},{8,12},{12,8},{16,20},{20,16},{24,28},{28,24},{1,5},{5... | collective-permute-start | bytes 12296 | tf_op jit(solution)/shard_map/ppermute | solution.py:348
  47.6 1.3 %collective-permute-start.20 = (f32[4,32,128]{2,1,0:T(8,128)S(1)}, f32[4,32,128]{2,1,0:T(8,128)S(1)}, u32[]{:S(2)}, u32[]{:S(2)}) collective-permute-start(f32[4,32,128]{2,1,0:T(8,128)S(1)} %get-tuple-element.52), channel_id=1, source_target_pairs={{0,4},{4,0},{8,12},{12,8},{16,20},{20,16},{24,28},{28,24},{1,5},{5... | collective-permute-start | bytes 196616 | tf_op jit(solution)/shard_map/ppermute | solution.py:348
  49.0 4.3 %collective-permute-start.21 = (f32[2,32,128]{2,1,0:T(8,128)S(1)}, f32[2,32,128]{2,1,0:T(8,128)S(1)}, u32[]{:S(2)}, u32[]{:S(2)}) collective-permute-start(f32[2,32,128]{2,1,0:T(8,128)S(1)} %slice.53), channel_id=1, source_target_pairs={{0,8},{4,28},{8,0},{12,20},{16,24},{20,12},{24,16},{28,4},{1,9},{5... | collective-permute-start | bytes 98312 | tf_op jit(solution)/shard_map/ppermute | solution.py:338
  50.0 3.9 %collective-permute-start.22 = (f32[32,128]{1,0:T(8,128)S(1)}, f32[32,128]{1,0:T(8,128)S(1)}, u32[]{:S(2)}, u32[]{:S(2)}) collective-permute-start(f32[32,128]{1,0:T(8,128)S(1)} %slice_bitcast_fusion), channel_id=1, source_target_pairs={{0,16},{4,20},{8,24},{12,28},{16,0},{20,4},{24,8},{28,12},{1,17},{... | collective-permute-start | bytes 49160 | tf_op jit(solution)/shard_map/ppermute | solution.py:338
  53.3 1.2 %collective-permute-start.23 = (f32[32,128]{1,0:T(8,128)S(1)}, f32[32,128]{1,0:T(8,128)S(1)}, u32[]{:S(2)}, u32[]{:S(2)}) collective-permute-start(f32[32,128]{1,0:T(8,128)S(1)} %dynamic-slice_bitcast_fusion), channel_id=1, source_target_pairs={{0,4},{4,0},{8,12},{12,8},{16,20},{20,16},{24,28},{28,24},{1,5},{5... | collective-permute-start | bytes 49160 | tf_op jit(solution)/shard_map/ppermute | solution.py:348

commit v5 on v4

--- a/solution.py
+++ b/solution.py
@@ -188,7 +188,7 @@
         cacc[c] = jnp.maximum(cacc[c], fold_rows(a * rep[r]))
         dacc[c] = jnp.maximum(dacc[c], fold_rows(a * rep[r + rb]))
 
-    loop(0, slots, UNROLL, columns)
+    loop(0, slots, 24, columns)
     c1 = scale_col1[0:cb]
     c2 = c1 / jnp.sqrt(c1 * col_peaks(cacc, cb) + EPS)
     c3 = c2 / jnp.sqrt(c2 * col_peaks(dacc, cb) + EPS)
@@ -204,7 +204,7 @@
         racc[r] = jnp.maximum(racc[r], a * scol2[pl.ds(c, 1), :])
         racc_b[r] = jnp.maximum(racc_b[r], a * scol3[pl.ds(c, 1), :])
 
-    loop(0, slots, UNROLL, rows)
+    loop(0, slots, 24, rows)
     packed = lane_peaks(racc, rb, 0, jnp.zeros((B, B), F32))
     packed = lane_peaks(racc_b, rb, rb, packed)
     peaks[...] = packed.T[0 : 2 * rb]

time: 55.2 us -> 55 us (level)
  no operation moved by 1% of the time
where the time goes in v5:
time: 55 us; the launch traced here: 54.9 us
  starting transfers between devices  22.1 us (40%)
  waiting for transfers between devices  18.4 us (33%)
  Pallas kernels  11.2 us (20%)
  between operations  1.6 us (3%)
  other arithmetic  1.41 us (3%)
    ppermute x9, starting transfers between devices, cross(): return lax.ppermute(x, 'flt', pairs)  12.5 us
    ppermute x9, waiting for transfers between devices, cross(): return lax.ppermute(x, 'flt', pairs)  10.7 us
    ppermute x11, waiting for transfers between devices, twin(): lax.ppermute(x, 'flt', [(i, i ^ 1) for i in range(lax.axis_size('flt'))])  6.7 us
    ppermute x4, starting transfers between devices, cross_scn(): return lax.ppermute(x, ('flt', 'scn'), pairs)  6.58 us
    pallas_call x2, Pallas kernels, body(): call(functools.partial(plan_step, rb, cb, slots, scen_all, len(totals), s...  3.19 us
    ppermute x11, starting transfers between devices, twin(): lax.ppermute(x, 'flt', [(i, i ^ 1) for i in range(lax.axis_size('flt'))])  3.04 us
    pallas_call x1, Pallas kernels, body(): call(functools.partial(first_peaks, rb, cb, slots, chunk), [f32((2 * rb +...  2.61 us
    pallas_call x1, Pallas kernels, body(): call(functools.partial(second_peaks, rb, cb, slots, len(parts)), [f32((2...  2.28 us
  transfers between devices with their start and end apart: 24, of which 18 were waited for; matrix products, arithmetic and copies ran while one was open for 1% of the time, Pallas kernels for 6%

profile of v5, /device:TPU:0, one launch (start us, length us, event | category | flops | bytes accessed | tf_op | source)
XLA Modules:
  0.0 54.9 jit_solution(17495087992032677545)
XLA Ops:
  1.4 2.6 %shard_map.112 = (f32[48,128]{1,0:T(8,128)S(1)}, f32[9,128]{1,0:T(8,128)S(1)}, s32[8,128]{1,0:T(8,128)S(1)}) custom-call(s32[1]{0:T(128)S(6)} %copy.14.refs_0_, s32[48]{0:T(128)} %refs_1_.3, s32[48]{0:T(128)} %refs_2_.1, bf16[48,128,128]{2,1,0:T(8,128)(2,1)} %refs_1_.5, f32[32,128]{1,0:T(8,128)} %refs_4_.1), custom_call_target="tpu_custom_call" | custom-call | tf_op jit(solution)/shard_map/pallas_call | solution.py:380
  4.6 0.8 %collective-permute-done = f32[48,128]{1,0:T(8,128)S(1)} collective-permute-done((f32[48,128]{1,0:T(8,128)S(1)}, f32[48,128]{1,0:T(8,128)S(1)}, u32[]{:S(2)}, u32[]{:S(2)}) %collective-permute-start) | collective-permute-done | bytes 24608 | tf_op jit(solution)/shard_map/ppermute | solution.py:348
  5.5 2.9 %collective-permute-start.1 = (f32[80,128]{1,0:T(8,128)S(1)}, f32[80,128]{1,0:T(8,128)S(1)}, u32[]{:S(2)}, u32[]{:S(2)}) collective-permute-start(f32[80,128]{1,0:T(8,128)S(1)} %pad_maximum_fusion.1.refs_3_), channel_id=1, source_target_pairs={{0,8},{4,28},{8,0},{12,20},{16,24},{20,12},{24,16},{28,4},{1,9},{5... | collective-permute-start | bytes 122888 | tf_op jit(solution)/shard_map/ppermute | solution.py:338
  8.3 1.5 %collective-permute-start.2 = (f32[80,128]{1,0:T(8,128)S(1)}, f32[80,128]{1,0:T(8,128)S(1)}, u32[]{:S(2)}, u32[]{:S(2)}) collective-permute-start(f32[80,128]{1,0:T(8,128)S(1)} %pad_maximum_fusion.1.refs_3_), channel_id=1, source_target_pairs={{0,16},{4,20},{8,24},{12,28},{16,0},{20,4},{24,8},{28,12},{1,17},{... | collective-permute-start | bytes 122888 | tf_op jit(solution)/shard_map/ppermute | solution.py:338
  10.7 2.0 %collective-permute-done.2.refs_5_ = f32[80,128]{1,0:T(8,128)S(1)} collective-permute-done((f32[80,128]{1,0:T(8,128)S(1)}, f32[80,128]{1,0:T(8,128)S(1)}, u32[]{:S(2)}, u32[]{:S(2)}) %collective-permute-start.2) | collective-permute-done | bytes 40992 | tf_op jit(solution)/shard_map/ppermute | solution.py:338
  12.7 2.3 %shard_map.113 = (f32[16,128]{1,0:T(8,128)S(1)}, f32[8,128]{1,0:T(8,128)S(1)}, f32[8,128]{1,0:T(8,128)S(1)}, f32[8,32,128]{2,1,0:T(8,128)S(1)}) custom-call(s32[8,128]{1,0:T(8,128)S(1)} %get-tuple-element.28.refs_0_, bf16[48,128,128]{2,1,0:T(8,128)(2,1)S(1)} %copy-done, f32[9,128]{1,0:T(8,128)S(1)} %get-tuple-element.29.refs_2_, ...), custom_call_target="tpu_custom_call" | custom-call | tf_op jit(solution)/shard_map/pallas_call | solution.py:407
  15.0 1.2 %collective-permute-done.4 = f32[16,128]{1,0:T(8,128)S(1)} collective-permute-done((f32[16,128]{1,0:T(8,128)S(1)}, f32[16,128]{1,0:T(8,128)S(1)}, u32[]{:S(2)}, u32[]{:S(2)}) %collective-permute-start.4) | collective-permute-done | bytes 8224 | tf_op jit(solution)/shard_map/ppermute | solution.py:348
  16.2 1.3 %collective-permute-start.5 = (f32[16,128]{1,0:T(8,128)S(1)}, f32[16,128]{1,0:T(8,128)S(1)}, u32[]{:S(2)}, u32[]{:S(2)}) collective-permute-start(f32[16,128]{1,0:T(8,128)S(1)} %max.32), channel_id=1, source_target_pairs={{0,8},{4,28},{8,0},{12,20},{16,24},{20,12},{24,16},{28,4},{1,9},{5... | collective-permute-start | bytes 24584 | tf_op jit(solution)/shard_map/ppermute | solution.py:338
  17.4 1.2 %collective-permute-start.6 = (f32[16,128]{1,0:T(8,128)S(1)}, f32[16,128]{1,0:T(8,128)S(1)}, u32[]{:S(2)}, u32[]{:S(2)}) collective-permute-start(f32[16,128]{1,0:T(8,128)S(1)} %max.32), channel_id=1, source_target_pairs={{0,16},{4,20},{8,24},{12,28},{16,0},{20,4},{24,8},{28,12},{1,17},{... | collective-permute-start | bytes 24584 | tf_op jit(solution)/shard_map/ppermute | solution.py:338
  18.7 1.2 %collective-permute-done.5 = f32[16,128]{1,0:T(8,128)S(1)} collective-permute-done((f32[16,128]{1,0:T(8,128)S(1)}, f32[16,128]{1,0:T(8,128)S(1)}, u32[]{:S(2)}, u32[]{:S(2)}) %collective-permute-start.5) | collective-permute-done | bytes 8224 | tf_op jit(solution)/shard_map/ppermute | solution.py:338
  19.8 1.3 %collective-permute-done.6 = f32[16,128]{1,0:T(8,128)S(1)} collective-permute-done((f32[16,128]{1,0:T(8,128)S(1)}, f32[16,128]{1,0:T(8,128)S(1)}, u32[]{:S(2)}, u32[]{:S(2)}) %collective-permute-start.6) | collective-permute-done | bytes 8224 | tf_op jit(solution)/shard_map/ppermute | solution.py:338
  21.2 2.7 %collective-permute-start.9 = (f32[8,128]{1,0:T(8,128)S(1)}, f32[8,128]{1,0:T(8,128)S(1)}, u32[]{:S(2)}, u32[]{:S(2)}) collective-permute-start(f32[8,128]{1,0:T(8,128)S(1)} %get-tuple-element.57.refs_9_), channel_id=1, source_target_pairs={{0,2},{1,3},{2,0},{3,1},{4,6},{5,7},{6,4},{7,5},{8,10},{9,11},{10,... | collective-permute-start | bytes 12296 | tf_op jit(solution)/shard_map/ppermute | solution.py:344
  23.8 1.6 %collective-permute-start.8 = (f32[8,128]{1,0:T(8,128)S(1)}, f32[8,128]{1,0:T(8,128)S(1)}, u32[]{:S(2)}, u32[]{:S(2)}) collective-permute-start(f32[8,128]{1,0:T(8,128)S(1)} %get-tuple-element.57.refs_9_), channel_id=1, source_target_pairs={{0,1},{1,0},{2,3},{3,2},{4,7},{5,6},{6,5},{7,4},{8,9},{9,8},{10,11... | collective-permute-start | bytes 12296 | tf_op jit(solution)/shard_map/ppermute | solution.py:344
  25.4 1.8 %shard_map.114 = (bf16[48,128,128]{2,1,0:T(8,128)(2,1)S(1)}, f32[8,128]{1,0:T(8,128)S(1)}, f32[32,1024]{1,0:T(8,128)S(1)}, f32[32,1024]{1,0:T(8,128)S(1)}) custom-call(s32[8,128]{1,0:T(8,128)S(1)} %get-tuple-element.28.refs_0_, bf16[48,128,128]{2,1,0:T(8,128)(2,1)S(1)} %copy-done, f32[8,128]{1,0:T(8,128)S(1)} %get-tuple-element.56.refs_2_, ...), custom_call_target="tpu_custom_call" | custom-call | tf_op jit(solution)/shard_map/pallas_call | solution.py:434
  27.9 0.8 %collective-permute-done.10.refs_12_ = f32[8,128]{1,0:T(8,128)S(1)} collective-permute-done((f32[8,128]{1,0:T(8,128)S(1)}, f32[8,128]{1,0:T(8,128)S(1)}, u32[]{:S(2)}, u32[]{:S(2)}) %collective-permute-start.10) | collective-permute-done | bytes 4128 | tf_op jit(solution)/shard_map/ppermute | solution.py:348
  28.7 1.6 %shard_map.115 = (f32[8,128]{1,0:T(8,128)S(1)}, f32[4,32,128]{2,1,0:T(8,128)S(1)}, f32[4,32,128]{2,1,0:T(8,128)S(1)}) custom-call(s32[8,128]{1,0:T(8,128)S(1)} %get-tuple-element.28.refs_0_, bf16[48,128,128]{2,1,0:T(8,128)(2,1)S(1)} %get-tuple-element.35.refs_1_, f32[8,128]{1,0:T(8,128)S(1)} %get-tuple-element.55.refs_3_.refs_2_, ...), custom_call_target="tpu_custom_call" | custom-call | tf_op jit(solution)/shard_map/pallas_call | solution.py:478
  30.7 0.9 %collective-permute-done.11 = f32[4,32,128]{2,1,0:T(8,128)S(1)} collective-permute-done((f32[4,32,128]{2,1,0:T(8,128)S(1)}, f32[4,32,128]{2,1,0:T(8,128)S(1)}, u32[]{:S(2)}, u32[]{:S(2)}) %collective-permute-start.11) | collective-permute-done | bytes 65568 | tf_op jit(solution)/shard_map/ppermute | solution.py:348
  31.6 2.0 %collective-permute-start.14 = (f32[4,32,128]{2,1,0:T(8,128)S(1)}, f32[4,32,128]{2,1,0:T(8,128)S(1)}, u32[]{:S(2)}, u32[]{:S(2)}) collective-permute-start(f32[4,32,128]{2,1,0:T(8,128)S(1)} %add.57), channel_id=1, source_target_pairs={{0,24},{4,28},{8,16},{12,20},{16,8},{20,12},{24,0},{28,4},{1,25},{... | collective-permute-start | bytes 196616 | tf_op jit(solution)/shard_map/ppermute | solution.py:338
  33.6 0.9 %collective-permute-start.13 = (f32[4,32,128]{2,1,0:T(8,128)S(1)}, f32[4,32,128]{2,1,0:T(8,128)S(1)}, u32[]{:S(2)}, u32[]{:S(2)}) collective-permute-start(f32[4,32,128]{2,1,0:T(8,128)S(1)} %add.57), channel_id=1, source_target_pairs={{0,16},{4,20},{8,24},{12,28},{16,0},{20,4},{24,8},{28,12},{1,17},{... | collective-permute-start | bytes 196616 | tf_op jit(solution)/shard_map/ppermute | solution.py:338
  34.5 0.7 %collective-permute-start.12 = (f32[4,32,128]{2,1,0:T(8,128)S(1)}, f32[4,32,128]{2,1,0:T(8,128)S(1)}, u32[]{:S(2)}, u32[]{:S(2)}) collective-permute-start(f32[4,32,128]{2,1,0:T(8,128)S(1)} %add.57), channel_id=1, source_target_pairs={{0,8},{4,12},{8,0},{12,4},{16,24},{20,28},{24,16},{28,20},{1,9},{5... | collective-permute-start | bytes 196616 | tf_op jit(solution)/shard_map/ppermute | solution.py:338
  35.2 1.8 %collective-permute-done.14 = f32[4,32,128]{2,1,0:T(8,128)S(1)} collective-permute-done((f32[4,32,128]{2,1,0:T(8,128)S(1)}, f32[4,32,128]{2,1,0:T(8,128)S(1)}, u32[]{:S(2)}, u32[]{:S(2)}) %collective-permute-start.14) | collective-permute-done | bytes 65568 | tf_op jit(solution)/shard_map/ppermute | solution.py:338
  37.0 1.3 %collective-permute-done.13 = f32[4,32,128]{2,1,0:T(8,128)S(1)} collective-permute-done((f32[4,32,128]{2,1,0:T(8,128)S(1)}, f32[4,32,128]{2,1,0:T(8,128)S(1)}, u32[]{:S(2)}, u32[]{:S(2)}) %collective-permute-start.13) | collective-permute-done | bytes 65568 | tf_op jit(solution)/shard_map/ppermute | solution.py:338
  40.1 0.8 %collective-permute-start.17 = (f32[8,128]{1,0:T(8,128)S(1)}, f32[8,128]{1,0:T(8,128)S(1)}, u32[]{:S(2)}, u32[]{:S(2)}) collective-permute-start(f32[8,128]{1,0:T(8,128)S(1)} %bitcast.37), channel_id=1, source_target_pairs={{0,2},{1,3},{2,0},{3,1},{4,6},{5,7},{6,4},{7,5},{8,10},{9,11},{10,... | collective-permute-start | bytes 12296 | tf_op jit(solution)/shard_map/ppermute | solution.py:344
  40.9 1.6 %collective-permute-start.16 = (f32[8,128]{1,0:T(8,128)S(1)}, f32[8,128]{1,0:T(8,128)S(1)}, u32[]{:S(2)}, u32[]{:S(2)}) collective-permute-start(f32[8,128]{1,0:T(8,128)S(1)} %bitcast.38), channel_id=1, source_target_pairs={{0,1},{1,0},{2,3},{3,2},{4,7},{5,6},{6,5},{7,4},{8,9},{9,8},{10,11... | collective-permute-start | bytes 12296 | tf_op jit(solution)/shard_map/ppermute | solution.py:344
  42.5 1.4 %shard_map.116 = (f32[32,1024]{1,0:T(8,128)}, f32[32,1024]{1,0:T(8,128)S(1)}) custom-call(s32[8,128]{1,0:T(8,128)S(1)} %get-tuple-element.28.refs_0_, bf16[48,128,128]{2,1,0:T(8,128)(2,1)S(1)} %get-tuple-element.35.refs_1_, f32[8,128]{1,0:T(8,128)S(1)} %get-tuple-element.36.refs_3_.refs_2_, s32[8,128]{1,0:T(8,128)S(1)} %bitcast.35, ...), custom_call_target="tpu_custom_call" | custom-call | tf_op jit(solution)/shard_map/pallas_call | solution.py:465
  43.8 0.8 %collective-permute-done.17.refs_11_ = f32[8,128]{1,0:T(8,128)S(1)} collective-permute-done((f32[8,128]{1,0:T(8,128)S(1)}, f32[8,128]{1,0:T(8,128)S(1)}, u32[]{:S(2)}, u32[]{:S(2)}) %collective-permute-start.17) | collective-permute-done | bytes 4128 | tf_op jit(solution)/shard_map/ppermute | solution.py:344
  45.0 0.8 %collective-permute-done.19.refs_12_ = f32[8,128]{1,0:T(8,128)S(1)} collective-permute-done((f32[8,128]{1,0:T(8,128)S(1)}, f32[8,128]{1,0:T(8,128)S(1)}, u32[]{:S(2)}, u32[]{:S(2)}) %collective-permute-start.19) | collective-permute-done | bytes 4128 | tf_op jit(solution)/shard_map/ppermute | solution.py:348
  45.8 1.6 %shard_map.117 = (f32[8,128]{1,0:T(8,128)S(1)}, f32[4,32,128]{2,1,0:T(8,128)S(1)}, f32[4,32,128]{2,1,0:T(8,128)S(1)}) custom-call(s32[8,128]{1,0:T(8,128)S(1)} %get-tuple-element.28.refs_0_, bf16[48,128,128]{2,1,0:T(8,128)(2,1)S(1)} %get-tuple-element.35.refs_1_, f32[8,128]{1,0:T(8,128)S(1)} %get-tuple-element.55.refs_3_.refs_2_, ...), custom_call_target="tpu_custom_call" | custom-call | tf_op jit(solution)/shard_map/pallas_call | solution.py:478
  47.8 0.9 %collective-permute-done.20 = f32[4,32,128]{2,1,0:T(8,128)S(1)} collective-permute-done((f32[4,32,128]{2,1,0:T(8,128)S(1)}, f32[4,32,128]{2,1,0:T(8,128)S(1)}, u32[]{:S(2)}, u32[]{:S(2)}) %collective-permute-start.20) | collective-permute-done | bytes 65568 | tf_op jit(solution)/shard_map/ppermute | solution.py:348
  48.8 1.0 %collective-permute-start.21 = (f32[2,32,128]{2,1,0:T(8,128)S(1)}, f32[2,32,128]{2,1,0:T(8,128)S(1)}, u32[]{:S(2)}, u32[]{:S(2)}) collective-permute-start(f32[2,32,128]{2,1,0:T(8,128)S(1)} %slice.53), channel_id=1, source_target_pairs={{0,8},{4,28},{8,0},{12,20},{16,24},{20,12},{24,16},{28,4},{1,9},{5... | collective-permute-start | bytes 98312 | tf_op jit(solution)/shard_map/ppermute | solution.py:338
  49.8 1.1 %collective-permute-start.22 = (f32[32,128]{1,0:T(8,128)S(1)}, f32[32,128]{1,0:T(8,128)S(1)}, u32[]{:S(2)}, u32[]{:S(2)}) collective-permute-start(f32[32,128]{1,0:T(8,128)S(1)} %slice_bitcast_fusion), channel_id=1, source_target_pairs={{0,16},{4,20},{8,24},{12,28},{16,0},{20,4},{24,8},{28,12},{1,17},{... | collective-permute-start | bytes 49160 | tf_op jit(solution)/shard_map/ppermute | solution.py:338
  50.8 2.2 %collective-permute-done.21 = f32[2,32,128]{2,1,0:T(8,128)S(1)} collective-permute-done((f32[2,32,128]{2,1,0:T(8,128)S(1)}, f32[2,32,128]{2,1,0:T(8,128)S(1)}, u32[]{:S(2)}, u32[]{:S(2)}) %collective-permute-start.21) | collective-permute-done | bytes 32800 | tf_op jit(solution)/shard_map/ppermute | solution.py:338
  (62 shorter events, 6.9 us)
Async XLA Ops:
  0.6 12.0 %copy-start = (bf16[48,128,128]{2,1,0:T(8,128)(2,1)S(1)}, bf16[48,128,128]{2,1,0:T(8,128)(2,1)}, u32[]{:S(2)}) copy-start(bf16[48,128,128]{2,1,0:T(8,128)(2,1)} %refs_1_.5) | copy-start | bytes 4718596
  4.0 21.4 %copy-start.1 = (f32[32,1024]{1,0:T(8,128)S(1)}, f32[32,1024]{1,0:T(8,128)}, u32[]{:S(2)}) copy-start(f32[32,1024]{1,0:T(8,128)} %refs_7_.1) | copy-start | bytes 393220
  4.0 21.4 %copy-start.3 = (s32[1024]{0:T(1024)S(1)}, s32[1024]{0:T(1024)}, u32[]{:S(2)}) copy-start(s32[1024]{0:T(1024)} %param.13) | copy-start | bytes 12292
  4.1 1.4 %collective-permute-start = (f32[48,128]{1,0:T(8,128)S(1)}, f32[48,128]{1,0:T(8,128)S(1)}, u32[]{:S(2)}, u32[]{:S(2)}) collective-permute-start(f32[48,128]{1,0:T(8,128)S(1)} %get-tuple-element.30), channel_id=1, source_target_pairs={{0,4},{4,0},{8,12},{12,8},{16,20},{20,16},{24,28},{28,24},{1,5},{5... | collective-permute-start | bytes 73736 | tf_op jit(solution)/shard_map/ppermute | solution.py:348
  5.5 4.9 %collective-permute-start.1 = (f32[80,128]{1,0:T(8,128)S(1)}, f32[80,128]{1,0:T(8,128)S(1)}, u32[]{:S(2)}, u32[]{:S(2)}) collective-permute-start(f32[80,128]{1,0:T(8,128)S(1)} %pad_maximum_fusion.1.refs_3_), channel_id=1, source_target_pairs={{0,8},{4,28},{8,0},{12,20},{16,24},{20,12},{24,16},{28,4},{1,9},{5... | collective-permute-start | bytes 122888 | tf_op jit(solution)/shard_map/ppermute | solution.py:338
  8.3 4.3 %collective-permute-start.2 = (f32[80,128]{1,0:T(8,128)S(1)}, f32[80,128]{1,0:T(8,128)S(1)}, u32[]{:S(2)}, u32[]{:S(2)}) collective-permute-start(f32[80,128]{1,0:T(8,128)S(1)} %pad_maximum_fusion.1.refs_3_), channel_id=1, source_target_pairs={{0,16},{4,20},{8,24},{12,28},{16,0},{20,4},{24,8},{28,12},{1,17},{... | collective-permute-start | bytes 122888 | tf_op jit(solution)/shard_map/ppermute | solution.py:338
  10.3 2.3 %collective-permute-start.3 = (f32[80,128]{1,0:T(8,128)S(1)}, f32[80,128]{1,0:T(8,128)S(1)}, u32[]{:S(2)}, u32[]{:S(2)}) collective-permute-start(f32[80,128]{1,0:T(8,128)S(1)} %pad_maximum_fusion.2), channel_id=1, source_target_pairs={{0,4},{4,0},{8,12},{12,8},{16,20},{20,16},{24,28},{28,24},{1,5},{5... | collective-permute-start | bytes 122888 | tf_op jit(solution)/shard_map/ppermute | solution.py:348
  12.7 15.2 %copy-start.5 = (f32[32,128]{1,0:T(8,128)S(1)}, f32[32,128]{1,0:T(8,128)}, u32[]{:S(2)}) copy-start(f32[32,128]{1,0:T(8,128)} %refs_4_.1) | copy-start | bytes 49156
  12.7 16.0 %copy-start.2 = (s32[32,128]{1,0:T(8,128)S(1)}, s32[32,128]{1,0:T(8,128)}, u32[]{:S(2)}) copy-start(s32[32,128]{1,0:T(8,128)} %refs_5_.3) | copy-start | bytes 49156
  12.7 16.0 %copy-start.4 = (f32[1024]{0:T(1024)S(1)}, f32[1024]{0:T(1024)}, u32[]{:S(2)}) copy-start(f32[1024]{0:T(1024)} %param.15) | copy-start | bytes 12292
  15.0 1.2 %collective-permute-start.4 = (f32[16,128]{1,0:T(8,128)S(1)}, f32[16,128]{1,0:T(8,128)S(1)}, u32[]{:S(2)}, u32[]{:S(2)}) collective-permute-start(f32[16,128]{1,0:T(8,128)S(1)} %get-tuple-element.32), channel_id=1, source_target_pairs={{0,4},{4,0},{8,12},{12,8},{16,20},{20,16},{24,28},{28,24},{1,5},{5... | collective-permute-start | bytes 24584 | tf_op jit(solution)/shard_map/ppermute | solution.py:348
  16.2 3.7 %collective-permute-start.5 = (f32[16,128]{1,0:T(8,128)S(1)}, f32[16,128]{1,0:T(8,128)S(1)}, u32[]{:S(2)}, u32[]{:S(2)}) collective-permute-start(f32[16,128]{1,0:T(8,128)S(1)} %max.32), channel_id=1, source_target_pairs={{0,8},{4,28},{8,0},{12,20},{16,24},{20,12},{24,16},{28,4},{1,9},{5... | collective-permute-start | bytes 24584 | tf_op jit(solution)/shard_map/ppermute | solution.py:338
  17.4 3.7 %collective-permute-start.6 = (f32[16,128]{1,0:T(8,128)S(1)}, f32[16,128]{1,0:T(8,128)S(1)}, u32[]{:S(2)}, u32[]{:S(2)}) collective-permute-start(f32[16,128]{1,0:T(8,128)S(1)} %max.32), channel_id=1, source_target_pairs={{0,16},{4,20},{8,24},{12,28},{16,0},{20,4},{24,8},{28,12},{1,17},{... | collective-permute-start | bytes 24584 | tf_op jit(solution)/shard_map/ppermute | solution.py:338
  19.8 1.3 %collective-permute-start.7 = (f32[16,128]{1,0:T(8,128)S(1)}, f32[16,128]{1,0:T(8,128)S(1)}, u32[]{:S(2)}, u32[]{:S(2)}) collective-permute-start(f32[16,128]{1,0:T(8,128)S(1)} %max.33), channel_id=1, source_target_pairs={{0,4},{4,0},{8,12},{12,8},{16,20},{20,16},{24,28},{28,24},{1,5},{5... | collective-permute-start | bytes 24584 | tf_op jit(solution)/shard_map/ppermute | solution.py:348
  21.2 6.0 %collective-permute-start.9 = (f32[8,128]{1,0:T(8,128)S(1)}, f32[8,128]{1,0:T(8,128)S(1)}, u32[]{:S(2)}, u32[]{:S(2)}) collective-permute-start(f32[8,128]{1,0:T(8,128)S(1)} %get-tuple-element.57.refs_9_), channel_id=1, source_target_pairs={{0,2},{1,3},{2,0},{3,1},{4,6},{5,7},{6,4},{7,5},{8,10},{9,11},{10,... | collective-permute-start | bytes 12296 | tf_op jit(solution)/shard_map/ppermute | solution.py:344
  23.8 3.6 %collective-permute-start.8 = (f32[8,128]{1,0:T(8,128)S(1)}, f32[8,128]{1,0:T(8,128)S(1)}, u32[]{:S(2)}, u32[]{:S(2)}) collective-permute-start(f32[8,128]{1,0:T(8,128)S(1)} %get-tuple-element.57.refs_9_), channel_id=1, source_target_pairs={{0,1},{1,0},{2,3},{3,2},{4,7},{5,6},{6,5},{7,4},{8,9},{9,8},{10,11... | collective-permute-start | bytes 12296 | tf_op jit(solution)/shard_map/ppermute | solution.py:344
  27.4 1.3 %collective-permute-start.10 = (f32[8,128]{1,0:T(8,128)S(1)}, f32[8,128]{1,0:T(8,128)S(1)}, u32[]{:S(2)}, u32[]{:S(2)}) collective-permute-start(f32[8,128]{1,0:T(8,128)S(1)} %collective-permute-done.8.refs_10_), channel_id=1, source_target_pairs={{0,4},{4,0},{8,12},{12,8},{16,20},{20,16},{24,28},{28,24},{1,5},{5... | collective-permute-start | bytes 12296 | tf_op jit(solution)/shard_map/ppermute | solution.py:348
  30.3 1.3 %collective-permute-start.11 = (f32[4,32,128]{2,1,0:T(8,128)S(1)}, f32[4,32,128]{2,1,0:T(8,128)S(1)}, u32[]{:S(2)}, u32[]{:S(2)}) collective-permute-start(f32[4,32,128]{2,1,0:T(8,128)S(1)} %get-tuple-element.43), channel_id=1, source_target_pairs={{0,4},{4,0},{8,12},{12,8},{16,20},{20,16},{24,28},{28,24},{1,5},{5... | collective-permute-start | bytes 196616 | tf_op jit(solution)/shard_map/ppermute | solution.py:348
  31.6 5.4 %collective-permute-start.14 = (f32[4,32,128]{2,1,0:T(8,128)S(1)}, f32[4,32,128]{2,1,0:T(8,128)S(1)}, u32[]{:S(2)}, u32[]{:S(2)}) collective-permute-start(f32[4,32,128]{2,1,0:T(8,128)S(1)} %add.57), channel_id=1, source_target_pairs={{0,24},{4,28},{8,16},{12,20},{16,8},{20,12},{24,0},{28,4},{1,25},{... | collective-permute-start | bytes 196616 | tf_op jit(solution)/shard_map/ppermute | solution.py:338
  33.6 4.7 %collective-permute-start.13 = (f32[4,32,128]{2,1,0:T(8,128)S(1)}, f32[4,32,128]{2,1,0:T(8,128)S(1)}, u32[]{:S(2)}, u32[]{:S(2)}) collective-permute-start(f32[4,32,128]{2,1,0:T(8,128)S(1)} %add.57), channel_id=1, source_target_pairs={{0,16},{4,20},{8,24},{12,28},{16,0},{20,4},{24,8},{28,12},{1,17},{... | collective-permute-start | bytes 196616 | tf_op jit(solution)/shard_map/ppermute | solution.py:338
  34.5 4.3 %collective-permute-start.12 = (f32[4,32,128]{2,1,0:T(8,128)S(1)}, f32[4,32,128]{2,1,0:T(8,128)S(1)}, u32[]{:S(2)}, u32[]{:S(2)}) collective-permute-start(f32[4,32,128]{2,1,0:T(8,128)S(1)} %add.57), channel_id=1, source_target_pairs={{0,8},{4,12},{8,0},{12,4},{16,24},{20,28},{24,16},{28,20},{1,9},{5... | collective-permute-start | bytes 196616 | tf_op jit(solution)/shard_map/ppermute | solution.py:338
  38.8 1.2 %collective-permute-start.15 = (f32[4,128]{1,0:T(4,128)S(1)}, f32[4,128]{1,0:T(4,128)S(1)}, u32[]{:S(2)}, u32[]{:S(2)}) collective-permute-start(f32[4,128]{1,0:T(4,128)S(1)} %reduce-precision_reduce_fusion), channel_id=1, source_target_pairs={{0,4},{4,0},{8,12},{12,8},{16,20},{20,16},{24,28},{28,24},{1,5},{5... | collective-permute-start | bytes 6152 | tf_op jit(solution)/shard_map/ppermute | solution.py:348
  38.9 3.5 %collective-permute-start.18 = (bf16[4,32,128]{2,1,0:T(8,128)(2,1)S(1)}, bf16[4,32,128]{2,1,0:T(8,128)(2,1)S(1)}, u32[]{:S(2)}, u32[]{:S(2)}) collective-permute-start(bf16[4,32,128]{2,1,0:T(8,128)(2,1)S(1)} %get-tuple-element.53), channel_id=1, source_target_pairs={{0,4},{4,0},{8,12},{12,8},{16,20},{20,16},{24,28},{28,24},{1,5},{5... | collective-permute-start | bytes 98312 | tf_op jit(solution)/shard_map/ppermute | solution.py:348
  40.1 4.6 %collective-permute-start.17 = (f32[8,128]{1,0:T(8,128)S(1)}, f32[8,128]{1,0:T(8,128)S(1)}, u32[]{:S(2)}, u32[]{:S(2)}) collective-permute-start(f32[8,128]{1,0:T(8,128)S(1)} %bitcast.37), channel_id=1, source_target_pairs={{0,2},{1,3},{2,0},{3,1},{4,6},{5,7},{6,4},{7,5},{8,10},{9,11},{10,... | collective-permute-start | bytes 12296 | tf_op jit(solution)/shard_map/ppermute | solution.py:344
  40.9 3.8 %collective-permute-start.16 = (f32[8,128]{1,0:T(8,128)S(1)}, f32[8,128]{1,0:T(8,128)S(1)}, u32[]{:S(2)}, u32[]{:S(2)}) collective-permute-start(f32[8,128]{1,0:T(8,128)S(1)} %bitcast.38), channel_id=1, source_target_pairs={{0,1},{1,0},{2,3},{3,2},{4,7},{5,6},{6,5},{7,4},{8,9},{9,8},{10,11... | collective-permute-start | bytes 12296 | tf_op jit(solution)/shard_map/ppermute | solution.py:344
  44.7 1.2 %collective-permute-start.19 = (f32[8,128]{1,0:T(8,128)S(1)}, f32[8,128]{1,0:T(8,128)S(1)}, u32[]{:S(2)}, u32[]{:S(2)}) collective-permute-start(f32[8,128]{1,0:T(8,128)S(1)} %collective-permute-done.16.refs_10_), channel_id=1, source_target_pairs={{0,4},{4,0},{8,12},{12,8},{16,20},{20,16},{24,28},{28,24},{1,5},{5... | collective-permute-start | bytes 12296 | tf_op jit(solution)/shard_map/ppermute | solution.py:348
  47.4 1.3 %collective-permute-start.20 = (f32[4,32,128]{2,1,0:T(8,128)S(1)}, f32[4,32,128]{2,1,0:T(8,128)S(1)}, u32[]{:S(2)}, u32[]{:S(2)}) collective-permute-start(f32[4,32,128]{2,1,0:T(8,128)S(1)} %get-tuple-element.52), channel_id=1, source_target_pairs={{0,4},{4,0},{8,12},{12,8},{16,20},{20,16},{24,28},{28,24},{1,5},{5... | collective-permute-start | bytes 196616 | tf_op jit(solution)/shard_map/ppermute | solution.py:348
  48.8 4.3 %collective-permute-start.21 = (f32[2,32,128]{2,1,0:T(8,128)S(1)}, f32[2,32,128]{2,1,0:T(8,128)S(1)}, u32[]{:S(2)}, u32[]{:S(2)}) collective-permute-start(f32[2,32,128]{2,1,0:T(8,128)S(1)} %slice.53), channel_id=1, source_target_pairs={{0,8},{4,28},{8,0},{12,20},{16,24},{20,12},{24,16},{28,4},{1,9},{5... | collective-permute-start | bytes 98312 | tf_op jit(solution)/shard_map/ppermute | solution.py:338
  49.8 3.9 %collective-permute-start.22 = (f32[32,128]{1,0:T(8,128)S(1)}, f32[32,128]{1,0:T(8,128)S(1)}, u32[]{:S(2)}, u32[]{:S(2)}) collective-permute-start(f32[32,128]{1,0:T(8,128)S(1)} %slice_bitcast_fusion), channel_id=1, source_target_pairs={{0,16},{4,20},{8,24},{12,28},{16,0},{20,4},{24,8},{28,12},{1,17},{... | collective-permute-start | bytes 49160 | tf_op jit(solution)/shard_map/ppermute | solution.py:338
  53.1 1.2 %collective-permute-start.23 = (f32[32,128]{1,0:T(8,128)S(1)}, f32[32,128]{1,0:T(8,128)S(1)}, u32[]{:S(2)}, u32[]{:S(2)}) collective-permute-start(f32[32,128]{1,0:T(8,128)S(1)} %dynamic-slice_bitcast_fusion), channel_id=1, source_target_pairs={{0,4},{4,0},{8,12},{12,8},{16,20},{20,16},{24,28},{28,24},{1,5},{5... | collective-permute-start | bytes 49160 | tf_op jit(solution)/shard_map/ppermute | solution.py:348

commit v6 on v5

--- a/solution.py
+++ b/solution.py
@@ -455,8 +455,9 @@
                 half = loads[0] + twin(loads[1])
                 far = [cross(half, m, m) for m in (2, 4, 6)]
                 y = jnp.maximum(SIGMA * ((half + far[0]) + (far[1] + far[2])), 0.0)
-                low, sums = round_low(y)
-                low, sums = interleave(low, twin(low), core), interleave(sums, twin(sums), core)
+                low = y.astype(BF16)
+                low = lax.optimization_barrier(interleave(low, twin(low), core))
+                sums = jnp.sum(low.astype(F32), axis=1)
                 own_dual = lax.dynamic_index_in_dim(y, chip, 0, False)
             else:
                 y = jnp.maximum(SIGMA * lax.psum(loads[0], "flt"), 0.0)

time: 55 us -> 55.1 us (level)
  waiting for transfers between devices: 18.4 us -> 19 us
    ppermute x11 -> x10, waiting for transfers between devices: 6.7 us -> 7.28 us  [twin(): lax.ppermute(x, 'flt', [(i, i ^ 1) for i in range(lax.axis_size('flt'))])]
    ppermute x11 -> x10, starting transfers between devices: 3.04 us -> 2.54 us  [twin(): lax.ppermute(x, 'flt', [(i, i ^ 1) for i in range(lax.axis_size('flt'))])]
  transfers between devices with their start and end apart: 24 -> 23, of which waited for: 18 -> 18; matrix products, arithmetic and copies ran while one was open for 1% -> 1% of each run, Pallas kernels for 6% -> 6%
where the time goes in v6:
time: 55.1 us; the launch traced here: 54.9 us
  starting transfers between devices  21.7 us (39%)
  waiting for transfers between devices  19 us (34%)
  Pallas kernels  11.2 us (20%)
  between operations  1.59 us (3%)
  other arithmetic  1.39 us (3%)
    ppermute x9, starting transfers between devices, cross(): return lax.ppermute(x, 'flt', pairs)  12.5 us
    ppermute x9, waiting for transfers between devices, cross(): return lax.ppermute(x, 'flt', pairs)  10.6 us
    ppermute x10, waiting for transfers between devices, twin(): lax.ppermute(x, 'flt', [(i, i ^ 1) for i in range(lax.axis_size('flt'))])  7.28 us
    ppermute x4, starting transfers between devices, cross_scn(): return lax.ppermute(x, ('flt', 'scn'), pairs)  6.58 us
    pallas_call x2, Pallas kernels, body(): call(functools.partial(plan_step, rb, cb, slots, scen_all, len(totals), s...  3.19 us
    pallas_call x1, Pallas kernels, body(): call(functools.partial(first_peaks, rb, cb, slots, chunk), [f32((2 * rb +...  2.62 us
    ppermute x10, starting transfers between devices, twin(): lax.ppermute(x, 'flt', [(i, i ^ 1) for i in range(lax.axis_size('flt'))])  2.54 us
    pallas_call x1, Pallas kernels, body(): call(functools.partial(second_peaks, rb, cb, slots, len(parts)), [f32((2...  2.29 us
  transfers between devices with their start and end apart: 23, of which 18 were waited for; matrix products, arithmetic and copies ran while one was open for 1% of the time, Pallas kernels for 6%

profile of v6, /device:TPU:0, one launch (start us, length us, event | category | flops | bytes accessed | tf_op | source)
XLA Modules:
  0.0 54.9 jit_solution(1845191325717541462)
XLA Ops:
  1.4 2.6 %shard_map.112 = (f32[48,128]{1,0:T(8,128)S(1)}, f32[9,128]{1,0:T(8,128)S(1)}, s32[8,128]{1,0:T(8,128)S(1)}) custom-call(s32[1]{0:T(128)S(6)} %copy.13.refs_0_, s32[48]{0:T(128)} %refs_1_.3, s32[48]{0:T(128)} %refs_2_.1, bf16[48,128,128]{2,1,0:T(8,128)(2,1)} %refs_1_.5, f32[32,128]{1,0:T(8,128)} %refs_4_.1), custom_call_target="tpu_custom_call" | custom-call | tf_op jit(solution)/shard_map/pallas_call | solution.py:380
  4.6 0.8 %collective-permute-done = f32[48,128]{1,0:T(8,128)S(1)} collective-permute-done((f32[48,128]{1,0:T(8,128)S(1)}, f32[48,128]{1,0:T(8,128)S(1)}, u32[]{:S(2)}, u32[]{:S(2)}) %collective-permute-start) | collective-permute-done | bytes 24608 | tf_op jit(solution)/shard_map/ppermute | solution.py:348
  5.4 2.9 %collective-permute-start.1 = (f32[80,128]{1,0:T(8,128)S(1)}, f32[80,128]{1,0:T(8,128)S(1)}, u32[]{:S(2)}, u32[]{:S(2)}) collective-permute-start(f32[80,128]{1,0:T(8,128)S(1)} %pad_maximum_fusion.1.refs_3_), channel_id=1, source_target_pairs={{0,8},{4,28},{8,0},{12,20},{16,24},{20,12},{24,16},{28,4},{1,9},{5... | collective-permute-start | bytes 122888 | tf_op jit(solution)/shard_map/ppermute | solution.py:338
  8.3 1.5 %collective-permute-start.2 = (f32[80,128]{1,0:T(8,128)S(1)}, f32[80,128]{1,0:T(8,128)S(1)}, u32[]{:S(2)}, u32[]{:S(2)}) collective-permute-start(f32[80,128]{1,0:T(8,128)S(1)} %pad_maximum_fusion.1.refs_3_), channel_id=1, source_target_pairs={{0,16},{4,20},{8,24},{12,28},{16,0},{20,4},{24,8},{28,12},{1,17},{... | collective-permute-start | bytes 122888 | tf_op jit(solution)/shard_map/ppermute | solution.py:338
  10.7 2.0 %collective-permute-done.2.refs_5_ = f32[80,128]{1,0:T(8,128)S(1)} collective-permute-done((f32[80,128]{1,0:T(8,128)S(1)}, f32[80,128]{1,0:T(8,128)S(1)}, u32[]{:S(2)}, u32[]{:S(2)}) %collective-permute-start.2) | collective-permute-done | bytes 40992 | tf_op jit(solution)/shard_map/ppermute | solution.py:338
  12.7 2.3 %shard_map.113 = (f32[16,128]{1,0:T(8,128)S(1)}, f32[8,128]{1,0:T(8,128)S(1)}, f32[8,128]{1,0:T(8,128)S(1)}, f32[8,32,128]{2,1,0:T(8,128)S(1)}) custom-call(s32[8,128]{1,0:T(8,128)S(1)} %get-tuple-element.28.refs_0_, bf16[48,128,128]{2,1,0:T(8,128)(2,1)S(1)} %copy-done, f32[9,128]{1,0:T(8,128)S(1)} %get-tuple-element.29.refs_2_, ...), custom_call_target="tpu_custom_call" | custom-call | tf_op jit(solution)/shard_map/pallas_call | solution.py:407
  15.0 1.2 %collective-permute-done.4 = f32[16,128]{1,0:T(8,128)S(1)} collective-permute-done((f32[16,128]{1,0:T(8,128)S(1)}, f32[16,128]{1,0:T(8,128)S(1)}, u32[]{:S(2)}, u32[]{:S(2)}) %collective-permute-start.4) | collective-permute-done | bytes 8224 | tf_op jit(solution)/shard_map/ppermute | solution.py:348
  16.2 1.2 %collective-permute-start.5 = (f32[16,128]{1,0:T(8,128)S(1)}, f32[16,128]{1,0:T(8,128)S(1)}, u32[]{:S(2)}, u32[]{:S(2)}) collective-permute-start(f32[16,128]{1,0:T(8,128)S(1)} %max.32), channel_id=1, source_target_pairs={{0,8},{4,28},{8,0},{12,20},{16,24},{20,12},{24,16},{28,4},{1,9},{5... | collective-permute-start | bytes 24584 | tf_op jit(solution)/shard_map/ppermute | solution.py:338
  17.4 1.2 %collective-permute-start.6 = (f32[16,128]{1,0:T(8,128)S(1)}, f32[16,128]{1,0:T(8,128)S(1)}, u32[]{:S(2)}, u32[]{:S(2)}) collective-permute-start(f32[16,128]{1,0:T(8,128)S(1)} %max.32), channel_id=1, source_target_pairs={{0,16},{4,20},{8,24},{12,28},{16,0},{20,4},{24,8},{28,12},{1,17},{... | collective-permute-start | bytes 24584 | tf_op jit(solution)/shard_map/ppermute | solution.py:338
  18.7 1.2 %collective-permute-done.5 = f32[16,128]{1,0:T(8,128)S(1)} collective-permute-done((f32[16,128]{1,0:T(8,128)S(1)}, f32[16,128]{1,0:T(8,128)S(1)}, u32[]{:S(2)}, u32[]{:S(2)}) %collective-permute-start.5) | collective-permute-done | bytes 8224 | tf_op jit(solution)/shard_map/ppermute | solution.py:338
  19.9 1.2 %collective-permute-done.6 = f32[16,128]{1,0:T(8,128)S(1)} collective-permute-done((f32[16,128]{1,0:T(8,128)S(1)}, f32[16,128]{1,0:T(8,128)S(1)}, u32[]{:S(2)}, u32[]{:S(2)}) %collective-permute-start.6) | collective-permute-done | bytes 8224 | tf_op jit(solution)/shard_map/ppermute | solution.py:338
  21.2 2.7 %collective-permute-start.9 = (f32[8,128]{1,0:T(8,128)S(1)}, f32[8,128]{1,0:T(8,128)S(1)}, u32[]{:S(2)}, u32[]{:S(2)}) collective-permute-start(f32[8,128]{1,0:T(8,128)S(1)} %get-tuple-element.57.refs_9_), channel_id=1, source_target_pairs={{0,2},{1,3},{2,0},{3,1},{4,6},{5,7},{6,4},{7,5},{8,10},{9,11},{10,... | collective-permute-start | bytes 12296 | tf_op jit(solution)/shard_map/ppermute | solution.py:344
  23.8 1.6 %collective-permute-start.8 = (f32[8,128]{1,0:T(8,128)S(1)}, f32[8,128]{1,0:T(8,128)S(1)}, u32[]{:S(2)}, u32[]{:S(2)}) collective-permute-start(f32[8,128]{1,0:T(8,128)S(1)} %get-tuple-element.57.refs_9_), channel_id=1, source_target_pairs={{0,1},{1,0},{2,3},{3,2},{4,7},{5,6},{6,5},{7,4},{8,9},{9,8},{10,11... | collective-permute-start | bytes 12296 | tf_op jit(solution)/shard_map/ppermute | solution.py:344
  25.4 1.8 %shard_map.114 = (bf16[48,128,128]{2,1,0:T(8,128)(2,1)S(1)}, f32[8,128]{1,0:T(8,128)S(1)}, f32[32,1024]{1,0:T(8,128)S(1)}, f32[32,1024]{1,0:T(8,128)S(1)}) custom-call(s32[8,128]{1,0:T(8,128)S(1)} %get-tuple-element.28.refs_0_, bf16[48,128,128]{2,1,0:T(8,128)(2,1)S(1)} %copy-done, f32[8,128]{1,0:T(8,128)S(1)} %get-tuple-element.56.refs_2_, ...), custom_call_target="tpu_custom_call" | custom-call | tf_op jit(solution)/shard_map/pallas_call | solution.py:434
  27.9 0.8 %collective-permute-done.10.refs_12_ = f32[8,128]{1,0:T(8,128)S(1)} collective-permute-done((f32[8,128]{1,0:T(8,128)S(1)}, f32[8,128]{1,0:T(8,128)S(1)}, u32[]{:S(2)}, u32[]{:S(2)}) %collective-permute-start.10) | collective-permute-done | bytes 4128 | tf_op jit(solution)/shard_map/ppermute | solution.py:348
  28.7 1.6 %shard_map.115 = (f32[8,128]{1,0:T(8,128)S(1)}, f32[4,32,128]{2,1,0:T(8,128)S(1)}, f32[4,32,128]{2,1,0:T(8,128)S(1)}) custom-call(s32[8,128]{1,0:T(8,128)S(1)} %get-tuple-element.28.refs_0_, bf16[48,128,128]{2,1,0:T(8,128)(2,1)S(1)} %get-tuple-element.35.refs_1_, f32[8,128]{1,0:T(8,128)S(1)} %get-tuple-element.55.refs_3_.refs_2_, ...), custom_call_target="tpu_custom_call" | custom-call | tf_op jit(solution)/shard_map/pallas_call | solution.py:479
  30.7 0.9 %collective-permute-done.11 = f32[4,32,128]{2,1,0:T(8,128)S(1)} collective-permute-done((f32[4,32,128]{2,1,0:T(8,128)S(1)}, f32[4,32,128]{2,1,0:T(8,128)S(1)}, u32[]{:S(2)}, u32[]{:S(2)}) %collective-permute-start.11) | collective-permute-done | bytes 65568 | tf_op jit(solution)/shard_map/ppermute | solution.py:348
  31.7 2.0 %collective-permute-start.14 = (f32[4,32,128]{2,1,0:T(8,128)S(1)}, f32[4,32,128]{2,1,0:T(8,128)S(1)}, u32[]{:S(2)}, u32[]{:S(2)}) collective-permute-start(f32[4,32,128]{2,1,0:T(8,128)S(1)} %add.57), channel_id=1, source_target_pairs={{0,24},{4,28},{8,16},{12,20},{16,8},{20,12},{24,0},{28,4},{1,25},{... | collective-permute-start | bytes 196616 | tf_op jit(solution)/shard_map/ppermute | solution.py:338
  33.6 0.9 %collective-permute-start.13 = (f32[4,32,128]{2,1,0:T(8,128)S(1)}, f32[4,32,128]{2,1,0:T(8,128)S(1)}, u32[]{:S(2)}, u32[]{:S(2)}) collective-permute-start(f32[4,32,128]{2,1,0:T(8,128)S(1)} %add.57), channel_id=1, source_target_pairs={{0,16},{4,20},{8,24},{12,28},{16,0},{20,4},{24,8},{28,12},{1,17},{... | collective-permute-start | bytes 196616 | tf_op jit(solution)/shard_map/ppermute | solution.py:338
  35.2 1.8 %collective-permute-done.14 = f32[4,32,128]{2,1,0:T(8,128)S(1)} collective-permute-done((f32[4,32,128]{2,1,0:T(8,128)S(1)}, f32[4,32,128]{2,1,0:T(8,128)S(1)}, u32[]{:S(2)}, u32[]{:S(2)}) %collective-permute-start.14) | collective-permute-done | bytes 65568 | tf_op jit(solution)/shard_map/ppermute | solution.py:338
  37.0 1.3 %collective-permute-done.13 = f32[4,32,128]{2,1,0:T(8,128)S(1)} collective-permute-done((f32[4,32,128]{2,1,0:T(8,128)S(1)}, f32[4,32,128]{2,1,0:T(8,128)S(1)}, u32[]{:S(2)}, u32[]{:S(2)}) %collective-permute-start.13) | collective-permute-done | bytes 65568 | tf_op jit(solution)/shard_map/ppermute | solution.py:338
  38.9 1.2 %collective-permute-done.15 = bf16[4,32,128]{2,1,0:T(8,128)(2,1)S(1)} collective-permute-done((bf16[4,32,128]{2,1,0:T(8,128)(2,1)S(1)}, bf16[4,32,128]{2,1,0:T(8,128)(2,1)S(1)}, u32[]{:S(2)}, u32[]{:S(2)}) %collective-permute-start.15) | collective-permute-done | bytes 32800 | tf_op jit(solution)/shard_map/ppermute | solution.py:348
  40.1 0.8 %collective-permute-start.17 = (f32[8,128]{1,0:T(8,128)S(1)}, f32[8,128]{1,0:T(8,128)S(1)}, u32[]{:S(2)}, u32[]{:S(2)}) collective-permute-start(f32[8,128]{1,0:T(8,128)S(1)} %convert_reduce_fusion.refs_9_), channel_id=1, source_target_pairs={{0,2},{1,3},{2,0},{3,1},{4,6},{5,7},{6,4},{7,5},{8,10},{9,11},{10,... | collective-permute-start | bytes 12296 | tf_op jit(solution)/shard_map/ppermute | solution.py:344
  40.9 1.6 %collective-permute-start.16 = (f32[8,128]{1,0:T(8,128)S(1)}, f32[8,128]{1,0:T(8,128)S(1)}, u32[]{:S(2)}, u32[]{:S(2)}) collective-permute-start(f32[8,128]{1,0:T(8,128)S(1)} %convert_reduce_fusion.refs_9_), channel_id=1, source_target_pairs={{0,1},{1,0},{2,3},{3,2},{4,7},{5,6},{6,5},{7,4},{8,9},{9,8},{10,11... | collective-permute-start | bytes 12296 | tf_op jit(solution)/shard_map/ppermute | solution.py:344
  42.5 1.4 %shard_map.116 = (f32[32,1024]{1,0:T(8,128)}, f32[32,1024]{1,0:T(8,128)S(1)}) custom-call(s32[8,128]{1,0:T(8,128)S(1)} %get-tuple-element.28.refs_0_, bf16[48,128,128]{2,1,0:T(8,128)(2,1)S(1)} %get-tuple-element.35.refs_1_, f32[8,128]{1,0:T(8,128)S(1)} %get-tuple-element.36.refs_3_.refs_2_, s32[8,128]{1,0:T(8,128)S(1)} %bitcast.31, ...), custom_call_target="tpu_custom_call" | custom-call | tf_op jit(solution)/shard_map/pallas_call | solution.py:466
  43.8 0.9 %collective-permute-done.17.refs_11_ = f32[8,128]{1,0:T(8,128)S(1)} collective-permute-done((f32[8,128]{1,0:T(8,128)S(1)}, f32[8,128]{1,0:T(8,128)S(1)}, u32[]{:S(2)}, u32[]{:S(2)}) %collective-permute-start.17) | collective-permute-done | bytes 4128 | tf_op jit(solution)/shard_map/ppermute | solution.py:344
  45.1 0.8 %collective-permute-done.18.refs_12_ = f32[8,128]{1,0:T(8,128)S(1)} collective-permute-done((f32[8,128]{1,0:T(8,128)S(1)}, f32[8,128]{1,0:T(8,128)S(1)}, u32[]{:S(2)}, u32[]{:S(2)}) %collective-permute-start.18) | collective-permute-done | bytes 4128 | tf_op jit(solution)/shard_map/ppermute | solution.py:348
  45.9 1.6 %shard_map.117 = (f32[8,128]{1,0:T(8,128)S(1)}, f32[4,32,128]{2,1,0:T(8,128)S(1)}, f32[4,32,128]{2,1,0:T(8,128)S(1)}) custom-call(s32[8,128]{1,0:T(8,128)S(1)} %get-tuple-element.28.refs_0_, bf16[48,128,128]{2,1,0:T(8,128)(2,1)S(1)} %get-tuple-element.35.refs_1_, f32[8,128]{1,0:T(8,128)S(1)} %get-tuple-element.55.refs_3_.refs_2_, ...), custom_call_target="tpu_custom_call" | custom-call | tf_op jit(solution)/shard_map/pallas_call | solution.py:479
  47.9 0.9 %collective-permute-done.19 = f32[4,32,128]{2,1,0:T(8,128)S(1)} collective-permute-done((f32[4,32,128]{2,1,0:T(8,128)S(1)}, f32[4,32,128]{2,1,0:T(8,128)S(1)}, u32[]{:S(2)}, u32[]{:S(2)}) %collective-permute-start.19) | collective-permute-done | bytes 65568 | tf_op jit(solution)/shard_map/ppermute | solution.py:348
  48.8 1.0 %collective-permute-start.20 = (f32[2,32,128]{2,1,0:T(8,128)S(1)}, f32[2,32,128]{2,1,0:T(8,128)S(1)}, u32[]{:S(2)}, u32[]{:S(2)}) collective-permute-start(f32[2,32,128]{2,1,0:T(8,128)S(1)} %slice.53), channel_id=1, source_target_pairs={{0,8},{4,28},{8,0},{12,20},{16,24},{20,12},{24,16},{28,4},{1,9},{5... | collective-permute-start | bytes 98312 | tf_op jit(solution)/shard_map/ppermute | solution.py:338
  49.8 1.1 %collective-permute-start.21 = (f32[32,128]{1,0:T(8,128)S(1)}, f32[32,128]{1,0:T(8,128)S(1)}, u32[]{:S(2)}, u32[]{:S(2)}) collective-permute-start(f32[32,128]{1,0:T(8,128)S(1)} %slice_bitcast_fusion), channel_id=1, source_target_pairs={{0,16},{4,20},{8,24},{12,28},{16,0},{20,4},{24,8},{28,12},{1,17},{... | collective-permute-start | bytes 49160 | tf_op jit(solution)/shard_map/ppermute | solution.py:338
  50.9 2.2 %collective-permute-done.20 = f32[2,32,128]{2,1,0:T(8,128)S(1)} collective-permute-done((f32[2,32,128]{2,1,0:T(8,128)S(1)}, f32[2,32,128]{2,1,0:T(8,128)S(1)}, u32[]{:S(2)}, u32[]{:S(2)}) %collective-permute-start.20) | collective-permute-done | bytes 32800 | tf_op jit(solution)/shard_map/ppermute | solution.py:338
  (58 shorter events, 6.4 us)
Async XLA Ops:
  0.6 12.0 %copy-start = (bf16[48,128,128]{2,1,0:T(8,128)(2,1)S(1)}, bf16[48,128,128]{2,1,0:T(8,128)(2,1)}, u32[]{:S(2)}) copy-start(bf16[48,128,128]{2,1,0:T(8,128)(2,1)} %refs_1_.5) | copy-start | bytes 4718596
  4.0 21.4 %copy-start.1 = (f32[32,1024]{1,0:T(8,128)S(1)}, f32[32,1024]{1,0:T(8,128)}, u32[]{:S(2)}) copy-start(f32[32,1024]{1,0:T(8,128)} %refs_7_.1) | copy-start | bytes 393220
  4.0 21.4 %copy-start.3 = (s32[1024]{0:T(1024)S(1)}, s32[1024]{0:T(1024)}, u32[]{:S(2)}) copy-start(s32[1024]{0:T(1024)} %param.13) | copy-start | bytes 12292
  4.1 1.4 %collective-permute-start = (f32[48,128]{1,0:T(8,128)S(1)}, f32[48,128]{1,0:T(8,128)S(1)}, u32[]{:S(2)}, u32[]{:S(2)}) collective-permute-start(f32[48,128]{1,0:T(8,128)S(1)} %get-tuple-element.30), channel_id=1, source_target_pairs={{0,4},{4,0},{8,12},{12,8},{16,20},{20,16},{24,28},{28,24},{1,5},{5... | collective-permute-start | bytes 73736 | tf_op jit(solution)/shard_map/ppermute | solution.py:348
  5.4 4.9 %collective-permute-start.1 = (f32[80,128]{1,0:T(8,128)S(1)}, f32[80,128]{1,0:T(8,128)S(1)}, u32[]{:S(2)}, u32[]{:S(2)}) collective-permute-start(f32[80,128]{1,0:T(8,128)S(1)} %pad_maximum_fusion.1.refs_3_), channel_id=1, source_target_pairs={{0,8},{4,28},{8,0},{12,20},{16,24},{20,12},{24,16},{28,4},{1,9},{5... | collective-permute-start | bytes 122888 | tf_op jit(solution)/shard_map/ppermute | solution.py:338
  8.3 4.3 %collective-permute-start.2 = (f32[80,128]{1,0:T(8,128)S(1)}, f32[80,128]{1,0:T(8,128)S(1)}, u32[]{:S(2)}, u32[]{:S(2)}) collective-permute-start(f32[80,128]{1,0:T(8,128)S(1)} %pad_maximum_fusion.1.refs_3_), channel_id=1, source_target_pairs={{0,16},{4,20},{8,24},{12,28},{16,0},{20,4},{24,8},{28,12},{1,17},{... | collective-permute-start | bytes 122888 | tf_op jit(solution)/shard_map/ppermute | solution.py:338
  10.3 2.3 %collective-permute-start.3 = (f32[80,128]{1,0:T(8,128)S(1)}, f32[80,128]{1,0:T(8,128)S(1)}, u32[]{:S(2)}, u32[]{:S(2)}) collective-permute-start(f32[80,128]{1,0:T(8,128)S(1)} %pad_maximum_fusion.2), channel_id=1, source_target_pairs={{0,4},{4,0},{8,12},{12,8},{16,20},{20,16},{24,28},{28,24},{1,5},{5... | collective-permute-start | bytes 122888 | tf_op jit(solution)/shard_map/ppermute | solution.py:348
  12.7 15.2 %copy-start.5 = (f32[32,128]{1,0:T(8,128)S(1)}, f32[32,128]{1,0:T(8,128)}, u32[]{:S(2)}) copy-start(f32[32,128]{1,0:T(8,128)} %refs_4_.1) | copy-start | bytes 49156
  12.7 16.0 %copy-start.2 = (s32[32,128]{1,0:T(8,128)S(1)}, s32[32,128]{1,0:T(8,128)}, u32[]{:S(2)}) copy-start(s32[32,128]{1,0:T(8,128)} %refs_5_.3) | copy-start | bytes 49156
  12.7 16.0 %copy-start.4 = (f32[1024]{0:T(1024)S(1)}, f32[1024]{0:T(1024)}, u32[]{:S(2)}) copy-start(f32[1024]{0:T(1024)} %param.15) | copy-start | bytes 12292
  15.0 1.2 %collective-permute-start.4 = (f32[16,128]{1,0:T(8,128)S(1)}, f32[16,128]{1,0:T(8,128)S(1)}, u32[]{:S(2)}, u32[]{:S(2)}) collective-permute-start(f32[16,128]{1,0:T(8,128)S(1)} %get-tuple-element.32), channel_id=1, source_target_pairs={{0,4},{4,0},{8,12},{12,8},{16,20},{20,16},{24,28},{28,24},{1,5},{5... | collective-permute-start | bytes 24584 | tf_op jit(solution)/shard_map/ppermute | solution.py:348
  16.2 3.7 %collective-permute-start.5 = (f32[16,128]{1,0:T(8,128)S(1)}, f32[16,128]{1,0:T(8,128)S(1)}, u32[]{:S(2)}, u32[]{:S(2)}) collective-permute-start(f32[16,128]{1,0:T(8,128)S(1)} %max.32), channel_id=1, source_target_pairs={{0,8},{4,28},{8,0},{12,20},{16,24},{20,12},{24,16},{28,4},{1,9},{5... | collective-permute-start | bytes 24584 | tf_op jit(solution)/shard_map/ppermute | solution.py:338
  17.4 3.7 %collective-permute-start.6 = (f32[16,128]{1,0:T(8,128)S(1)}, f32[16,128]{1,0:T(8,128)S(1)}, u32[]{:S(2)}, u32[]{:S(2)}) collective-permute-start(f32[16,128]{1,0:T(8,128)S(1)} %max.32), channel_id=1, source_target_pairs={{0,16},{4,20},{8,24},{12,28},{16,0},{20,4},{24,8},{28,12},{1,17},{... | collective-permute-start | bytes 24584 | tf_op jit(solution)/shard_map/ppermute | solution.py:338
  19.9 1.2 %collective-permute-start.7 = (f32[16,128]{1,0:T(8,128)S(1)}, f32[16,128]{1,0:T(8,128)S(1)}, u32[]{:S(2)}, u32[]{:S(2)}) collective-permute-start(f32[16,128]{1,0:T(8,128)S(1)} %max.33), channel_id=1, source_target_pairs={{0,4},{4,0},{8,12},{12,8},{16,20},{20,16},{24,28},{28,24},{1,5},{5... | collective-permute-start | bytes 24584 | tf_op jit(solution)/shard_map/ppermute | solution.py:348
  21.2 6.0 %collective-permute-start.9 = (f32[8,128]{1,0:T(8,128)S(1)}, f32[8,128]{1,0:T(8,128)S(1)}, u32[]{:S(2)}, u32[]{:S(2)}) collective-permute-start(f32[8,128]{1,0:T(8,128)S(1)} %get-tuple-element.57.refs_9_), channel_id=1, source_target_pairs={{0,2},{1,3},{2,0},{3,1},{4,6},{5,7},{6,4},{7,5},{8,10},{9,11},{10,... | collective-permute-start | bytes 12296 | tf_op jit(solution)/shard_map/ppermute | solution.py:344
  23.8 3.6 %collective-permute-start.8 = (f32[8,128]{1,0:T(8,128)S(1)}, f32[8,128]{1,0:T(8,128)S(1)}, u32[]{:S(2)}, u32[]{:S(2)}) collective-permute-start(f32[8,128]{1,0:T(8,128)S(1)} %get-tuple-element.57.refs_9_), channel_id=1, source_target_pairs={{0,1},{1,0},{2,3},{3,2},{4,7},{5,6},{6,5},{7,4},{8,9},{9,8},{10,11... | collective-permute-start | bytes 12296 | tf_op jit(solution)/shard_map/ppermute | solution.py:344
  27.4 1.3 %collective-permute-start.10 = (f32[8,128]{1,0:T(8,128)S(1)}, f32[8,128]{1,0:T(8,128)S(1)}, u32[]{:S(2)}, u32[]{:S(2)}) collective-permute-start(f32[8,128]{1,0:T(8,128)S(1)} %collective-permute-done.8.refs_10_), channel_id=1, source_target_pairs={{0,4},{4,0},{8,12},{12,8},{16,20},{20,16},{24,28},{28,24},{1,5},{5... | collective-permute-start | bytes 12296 | tf_op jit(solution)/shard_map/ppermute | solution.py:348
  30.3 1.3 %collective-permute-start.11 = (f32[4,32,128]{2,1,0:T(8,128)S(1)}, f32[4,32,128]{2,1,0:T(8,128)S(1)}, u32[]{:S(2)}, u32[]{:S(2)}) collective-permute-start(f32[4,32,128]{2,1,0:T(8,128)S(1)} %get-tuple-element.43), channel_id=1, source_target_pairs={{0,4},{4,0},{8,12},{12,8},{16,20},{20,16},{24,28},{28,24},{1,5},{5... | collective-permute-start | bytes 196616 | tf_op jit(solution)/shard_map/ppermute | solution.py:348
  31.7 5.4 %collective-permute-start.14 = (f32[4,32,128]{2,1,0:T(8,128)S(1)}, f32[4,32,128]{2,1,0:T(8,128)S(1)}, u32[]{:S(2)}, u32[]{:S(2)}) collective-permute-start(f32[4,32,128]{2,1,0:T(8,128)S(1)} %add.57), channel_id=1, source_target_pairs={{0,24},{4,28},{8,16},{12,20},{16,8},{20,12},{24,0},{28,4},{1,25},{... | collective-permute-start | bytes 196616 | tf_op jit(solution)/shard_map/ppermute | solution.py:338
  33.6 4.7 %collective-permute-start.13 = (f32[4,32,128]{2,1,0:T(8,128)S(1)}, f32[4,32,128]{2,1,0:T(8,128)S(1)}, u32[]{:S(2)}, u32[]{:S(2)}) collective-permute-start(f32[4,32,128]{2,1,0:T(8,128)S(1)} %add.57), channel_id=1, source_target_pairs={{0,16},{4,20},{8,24},{12,28},{16,0},{20,4},{24,8},{28,12},{1,17},{... | collective-permute-start | bytes 196616 | tf_op jit(solution)/shard_map/ppermute | solution.py:338
  34.5 4.3 %collective-permute-start.12 = (f32[4,32,128]{2,1,0:T(8,128)S(1)}, f32[4,32,128]{2,1,0:T(8,128)S(1)}, u32[]{:S(2)}, u32[]{:S(2)}) collective-permute-start(f32[4,32,128]{2,1,0:T(8,128)S(1)} %add.57), channel_id=1, source_target_pairs={{0,8},{4,12},{8,0},{12,4},{16,24},{20,28},{24,16},{28,20},{1,9},{5... | collective-permute-start | bytes 196616 | tf_op jit(solution)/shard_map/ppermute | solution.py:338
  38.8 1.3 %collective-permute-start.15 = (bf16[4,32,128]{2,1,0:T(8,128)(2,1)S(1)}, bf16[4,32,128]{2,1,0:T(8,128)(2,1)S(1)}, u32[]{:S(2)}, u32[]{:S(2)}) collective-permute-start(bf16[4,32,128]{2,1,0:T(8,128)(2,1)S(1)} %get-tuple-element.53), channel_id=1, source_target_pairs={{0,4},{4,0},{8,12},{12,8},{16,20},{20,16},{24,28},{28,24},{1,5},{5... | collective-permute-start | bytes 98312 | tf_op jit(solution)/shard_map/ppermute | solution.py:348
  40.1 4.6 %collective-permute-start.17 = (f32[8,128]{1,0:T(8,128)S(1)}, f32[8,128]{1,0:T(8,128)S(1)}, u32[]{:S(2)}, u32[]{:S(2)}) collective-permute-start(f32[8,128]{1,0:T(8,128)S(1)} %convert_reduce_fusion.refs_9_), channel_id=1, source_target_pairs={{0,2},{1,3},{2,0},{3,1},{4,6},{5,7},{6,4},{7,5},{8,10},{9,11},{10,... | collective-permute-start | bytes 12296 | tf_op jit(solution)/shard_map/ppermute | solution.py:344
  40.9 3.8 %collective-permute-start.16 = (f32[8,128]{1,0:T(8,128)S(1)}, f32[8,128]{1,0:T(8,128)S(1)}, u32[]{:S(2)}, u32[]{:S(2)}) collective-permute-start(f32[8,128]{1,0:T(8,128)S(1)} %convert_reduce_fusion.refs_9_), channel_id=1, source_target_pairs={{0,1},{1,0},{2,3},{3,2},{4,7},{5,6},{6,5},{7,4},{8,9},{9,8},{10,11... | collective-permute-start | bytes 12296 | tf_op jit(solution)/shard_map/ppermute | solution.py:344
  44.7 1.2 %collective-permute-start.18 = (f32[8,128]{1,0:T(8,128)S(1)}, f32[8,128]{1,0:T(8,128)S(1)}, u32[]{:S(2)}, u32[]{:S(2)}) collective-permute-start(f32[8,128]{1,0:T(8,128)S(1)} %collective-permute-done.16.refs_10_), channel_id=1, source_target_pairs={{0,4},{4,0},{8,12},{12,8},{16,20},{20,16},{24,28},{28,24},{1,5},{5... | collective-permute-start | bytes 12296 | tf_op jit(solution)/shard_map/ppermute | solution.py:348
  47.5 1.3 %collective-permute-start.19 = (f32[4,32,128]{2,1,0:T(8,128)S(1)}, f32[4,32,128]{2,1,0:T(8,128)S(1)}, u32[]{:S(2)}, u32[]{:S(2)}) collective-permute-start(f32[4,32,128]{2,1,0:T(8,128)S(1)} %get-tuple-element.52), channel_id=1, source_target_pairs={{0,4},{4,0},{8,12},{12,8},{16,20},{20,16},{24,28},{28,24},{1,5},{5... | collective-permute-start | bytes 196616 | tf_op jit(solution)/shard_map/ppermute | solution.py:348
  48.8 4.3 %collective-permute-start.20 = (f32[2,32,128]{2,1,0:T(8,128)S(1)}, f32[2,32,128]{2,1,0:T(8,128)S(1)}, u32[]{:S(2)}, u32[]{:S(2)}) collective-permute-start(f32[2,32,128]{2,1,0:T(8,128)S(1)} %slice.53), channel_id=1, source_target_pairs={{0,8},{4,28},{8,0},{12,20},{16,24},{20,12},{24,16},{28,4},{1,9},{5... | collective-permute-start | bytes 98312 | tf_op jit(solution)/shard_map/ppermute | solution.py:338
  49.8 3.9 %collective-permute-start.21 = (f32[32,128]{1,0:T(8,128)S(1)}, f32[32,128]{1,0:T(8,128)S(1)}, u32[]{:S(2)}, u32[]{:S(2)}) collective-permute-start(f32[32,128]{1,0:T(8,128)S(1)} %slice_bitcast_fusion), channel_id=1, source_target_pairs={{0,16},{4,20},{8,24},{12,28},{16,0},{20,4},{24,8},{28,12},{1,17},{... | collective-permute-start | bytes 49160 | tf_op jit(solution)/shard_map/ppermute | solution.py:338
  53.1 1.2 %collective-permute-start.22 = (f32[32,128]{1,0:T(8,128)S(1)}, f32[32,128]{1,0:T(8,128)S(1)}, u32[]{:S(2)}, u32[]{:S(2)}) collective-permute-start(f32[32,128]{1,0:T(8,128)S(1)} %dynamic-slice_bitcast_fusion), channel_id=1, source_target_pairs={{0,4},{4,0},{8,12},{12,8},{16,20},{20,16},{24,28},{28,24},{1,5},{5... | collective-permute-start | bytes 49160 | tf_op jit(solution)/shard_map/ppermute | solution.py:348
